TPU v7x, 128 devices: a whole 4x4x4 slice. The times are simulated.
128 devices in a mesh: dp: 64 (over x, y_hi, z, core), tensor: 2 (over y_lo).
Axes of the slice: x: 4, y: 4 (y_hi: 2, y_lo: 2; y = y_hi * 2 + y_lo), z: 4, core: 2. Of those that a mesh axis runs over, the one named last changes fastest.
Arguments:
- tokens: bfloat16 [16384, 1024], P('dp'), may hold values from -16 to 16
- segments: int32 [64, 256], P('dp'), may hold values from 0 to 3, never falling along the last dimension, each value on 1 to 128 neighbouring positions
- routes: int32 [2, 16384, 2], P(None, 'dp'), may hold values from 0 to 3, all different within a row
- norm_attention: bfloat16 [2, 1024], replicated, may hold values from 0.099609375 to 1.8984375
- query_weight: bfloat16 [2, 1024, 1024], P(None, None, 'tensor'), may hold values from -0.1875 to 0.1875
- key_matrix: bfloat16 [2, 1024, 512], P(None, None, 'tensor'), may hold values from -0.1875 to 0.1875
- value_matrix: bfloat16 [2, 1024, 512], P(None, None, 'tensor'), may hold values from -0.1875 to 0.1875
- output_weight: bfloat16 [2, 1024, 1024], P(None, 'tensor'), may hold values from -0.75 to 0.75
- norm_experts: bfloat16 [2, 1024], replicated, may hold values from 0.099609375 to 1.8984375
- router_weight: bfloat16 [2, 1024, 4], replicated, may hold values from -0.109375 to 0.109375
- gate_weight: bfloat16 [2, 4, 1024, 512], P(None, None, None, 'tensor'), may hold values from -0.1875 to 0.1875
- up_weight: bfloat16 [2, 4, 1024, 512], P(None, None, None, 'tensor'), may hold values from -0.1875 to 0.1875
- down_weight: bfloat16 [2, 4, 512, 1024], P(None, None, 'tensor'), may hold values from -0.375 to 0.375
- cotangent: bfloat16 [16384, 1024], P('dp'), may hold values from -16 to 16
Outputs:
- output: bfloat16 [16384, 1024], P('dp')
- input_gradient: float32 [16384, 1024], P('dp')
- attention_gain_gradient: float32 [2, 1024], P(None, 'dp')
- query_gradient: float32 [2, 1024, 1024], P(None, 'dp', 'tensor')
- key_gradient: float32 [2, 1024, 512], P(None, 'dp', 'tensor')
- value_gradient: float32 [2, 1024, 512], P(None, 'dp', 'tensor')
- projection_gradient: float32 [2, 1024, 1024], P(None, 'tensor', 'dp')
- expert_gain_gradient: float32 [2, 1024], P(None, 'dp')
- router_gradient: float32 [2, 1024, 4], P(None, 'dp')
- gate_gradient: float32 [2, 4, 1024, 512], P(None, None, 'dp', 'tensor')
- up_gradient: float32 [2, 4, 1024, 512], P(None, None, 'dp', 'tensor')
- down_gradient: float32 [2, 4, 512, 1024], P(None, None, 'tensor', 'dp')
Inputs may be any that keep to these rules, and one draw needn't show every extreme that they name: `routes`: in each layer every token names 2 different experts. `segments`: numbers never fall along a sequence; a document has at most half of 256 tokens.
All inputs are finite; a program needn't handle non-finite values.
Results may differ from a plain program's by a relative error of at most 0.022.
The roundings to bfloat16 on the way count: a program that leaves them out, or rounds other values in their place, can miss the bound.
Values sent between devices are 32-bit elements; how exact they have to be, the bound alone decides.
No kernel may reach another device: no remote copies, remote signals or barrier semaphores. Data moves between devices by JAX's collectives and lax.ppermute only.
A program may use at most 256 MiB of HBM per device.

v0:
```python
import functools

import jax
import jax.numpy as jnp
import numpy as np
from jax import lax
from jax.experimental import pallas as pl
from jax.experimental.pallas import tpu as pltpu
from jax.sharding import Mesh
from jax.sharding import PartitionSpec as P

HEAD_SIZE = 64
LANES = 128
STREAMS = 4
SMALL = 128
DP = ("dp_0", "dp_1", "dp_2", "dp_3")
DP_SIZES = (4, 2, 4, 2)
EPSILON = 1e-06
THETA = 10000.0
EXCLUDED = -1e30
F32 = jnp.float32
BF16 = jnp.bfloat16
MIB = 1024 * 1024

EXPERT_ORDERS = (
    (("x", "u"), ("z", "u"), ("z", "v"), ("x", "v")),
    (("z", "v"), ("x", "v"), ("x", "u"), ("z", "u")),
)
ATTENTION_ORDERS = (
    (("z", "v"), ("x", "v"), ("x", "u"), ("z", "u")),
    (("x", "u"), ("z", "u"), ("z", "v"), ("x", "v")),
)


def swapped(order):
    return (order[1], order[0], *order[2:])


def pair_bit(index, kind):
    high = index // 2
    if kind == "v":
        return high
    return high ^ (index % 2)


def ring_place(order, x, z):
    at = 0
    for ring, kind in order:
        at = at * 2 + pair_bit(x if ring == "x" else z, kind)
    return at


def place(order, x, yh, z):
    return ring_place(order, x, z) * 2 + yh


def mm(a, b):
    return lax.dot_general(a, b, (((1,), (0,)), ((), ())), preferred_element_type=F32)


def mm_nt(a, b):
    return lax.dot_general(a, b, (((1,), (1,)), ((), ())), preferred_element_type=F32)


def mm_tn(a, b):
    return lax.dot_general(a, b, (((0,), (0,)), ((), ())), preferred_element_type=F32)


def row_factor(stream):
    return lax.rsqrt(jnp.mean(stream * stream, axis=-1, keepdims=True) + EPSILON)


def norm_back(stream, factor, gain, gradient):
    weighted = gradient * gain
    inner = jnp.sum(weighted * stream, axis=-1, keepdims=True) * (1.0 / stream.shape[-1])
    change = factor * weighted - stream * (factor * factor * factor) * inner
    return change, jnp.sum(gradient * stream * factor, axis=0, keepdims=True)


def lane_of(rows):
    return lax.broadcasted_iota(jnp.int32, (rows, LANES), 1)


def partner(block, lane):
    back = pltpu.roll(block, LANES - HEAD_SIZE // 2, 1)
    ahead = pltpu.roll(block, HEAD_SIZE // 2, 1)
    return jnp.where(lane % HEAD_SIZE < HEAD_SIZE // 2, back, ahead)


def both_heads(block, lane):
    rolled = pltpu.roll(block, HEAD_SIZE, 1)
    low = lane < HEAD_SIZE
    return jnp.where(low, block, rolled), jnp.where(low, rolled, block)


def stacked_pair(block, lane):
    zero = jnp.zeros_like(block)
    low = lane < HEAD_SIZE
    return jnp.concatenate(
        [jnp.where(low, block, zero), jnp.where(low, zero, block)], axis=0
    )


def allowed_pairs(seg_row, seg_column):
    length = seg_column.shape[0]
    rows = lax.broadcasted_iota(jnp.int32, (length, length), 0)
    columns = lax.broadcasted_iota(jnp.int32, (length, length), 1)
    allowed = (columns <= rows) & (seg_column == seg_row)
    bias = jnp.where(allowed, 0.0, 1.0)
    return jnp.concatenate([bias, bias], axis=0) < 0.5


def block_places(orders, places, later=False):
    core = places[4]
    found = []
    for block in range(32):
        x, yh, z = block // 8, (block // 4) % 2, block % 4
        one, two = (
            jnp.where(later, place(swapped(order), x, yh, z), place(order, x, yh, z))
            for order in orders
        )
        own = jnp.where(later, places[2], places[0])
        far = jnp.where(later, places[3], places[1])
        found.append((jnp.where(core == 0, one, two) ^ own, jnp.where(core == 0, two, one) ^ far))
    return core, found


def store_blocks(keep_ref, send_ref, value, column, where_to):
    core, found = where_to
    rows = value.shape[0] // 64
    columns = slice(column, column + value.shape[1])
    for block, (kept, sent) in enumerate(found):
        first = value[2 * block * rows : (2 * block + 1) * rows]
        second = value[(2 * block + 1) * rows : (2 * block + 2) * rows]
        keep_ref[pl.ds(pl.multiple_of(kept * rows, rows), rows), columns] = jnp.where(
            core == 0, first, second
        )
        send_ref[pl.ds(pl.multiple_of(sent * rows, rows), rows), columns] = jnp.where(
            core == 0, second, first
        )


def attend(a, wq, wk, wv, q_out, kk_out, vv_out, mix_out, cosine, sine, allowed):
    length = a.shape[0]
    lane = lane_of(length)
    q = mm(a, wq)
    k = mm(a, wk)
    v = mm(a, wv)
    scale = HEAD_SIZE**-0.5
    for pair in range(k.shape[1] // LANES):
        at = slice(pair * LANES, (pair + 1) * LANES)
        k_block = k[:, at] * cosine + partner(k[:, at], lane) * sine
        k_twice = both_heads(k_block, lane)
        v_twice = both_heads(v[:, at], lane)
        for side in range(2):
            head = 2 * pair + side
            columns = slice(head * LANES, (head + 1) * LANES)
            kk = k_twice[side].astype(BF16)
            vv = v_twice[side].astype(BF16)
            kk_out[head] = kk
            vv_out[head] = vv
            q_block = q[:, columns]
            q_block = (q_block * cosine + partner(q_block, lane) * sine).astype(BF16)
            q_out[:, columns] = q_block
            scores = mm_nt(stacked_pair(q_block, lane), kk) * scale
            scores = jnp.where(allowed, scores, EXCLUDED)
            shifted = jnp.exp(scores - jnp.max(scores, axis=-1, keepdims=True))
            probs = (shifted / jnp.sum(shifted, axis=-1, keepdims=True)).astype(BF16)
            mixed = mm(probs, vv)
            mix_out[:, columns] = jnp.where(
                lane < HEAD_SIZE, mixed[:length], mixed[length:]
            ).astype(BF16)


def halves_of(weights):
    depth = 2 * weights.shape[0] // 3
    quarter = depth // 4
    return (
        weights.at[:depth, : 2 * quarter],
        weights.at[:depth, 2 * quarter : 3 * quarter],
        weights.at[:depth, 3 * quarter :],
        weights.at[depth:, :],
    )


def unpack_gathered(places, gathered, weights):
    core = places[4]
    rows = gathered[0].shape[0] // 8
    width = gathered[0].shape[1]
    top, low = 2 * rows // 3, rows // 3
    for piece in range(32):
        x, z, side = piece // 8, (piece // 2) % 4, piece % 2
        for part in range(2):
            order = EXPERT_ORDERS[side] if part == 0 else swapped(EXPERT_ORDERS[side])
            at = ring_place(order, x, z) ^ places[2 * part + side]
            rows_at = pl.ds(pl.multiple_of((at & 7) * rows, rows), rows)
            columns = slice(part * width, (part + 1) * width)
            first, second, far_first, far_second = (
                gathered[2 * pair + part][rows_at, :] for pair in range(4)
            )
            near, far = jnp.where(at < 8, first, second), jnp.where(at < 8, far_first, far_second)
            value = jnp.where(core == side, near, far).astype(BF16)
            weights[piece * top : (piece + 1) * top, columns] = value[:top]
            start = 32 * top + piece * low
            weights[start : start + low, columns] = value[top:]


def attention_forward_kernel(count, full, *refs):
    parts = refs[:count]
    (gain, wq, wk, wv, wo, cos, sin, seg_row, seg_column) = refs[count : count + 9]
    refs = refs[count + 9 :]
    if full:
        places, gathered = refs[0], refs[1:9]
        refs = refs[9:]
    (x_out, a_out, q_out, kk_out, vv_out, mix_out, part_out) = refs[:7]
    x = parts[0][...].astype(F32)
    if count == 3:
        x = x + (parts[1][...] + parts[2][...])
    x_out[...] = x
    a = (x * row_factor(x) * gain[...].astype(F32)).astype(BF16)
    a_out[...] = a
    common = (cos[...], sin[...], allowed_pairs(seg_row[...], seg_column[...]))
    attend(a, wq[...], wk[...], wv[...], q_out, kk_out, vv_out, mix_out, *common)
    part_out[...] = mm(mix_out[...], wo[...])
    if full:
        q_other, kk_other, vv_other, part_other, weights, mix_other = refs[7:]
        unpack_gathered(places, gathered, weights)
        wq, wk, wv, wo = halves_of(weights)
        attend(a, wq[...], wk[...], wv[...], q_other, kk_other, vv_other, mix_other, *common)
        part_other[...] = mm(mix_other[...], wo[...])


ONCE = pl.Buffered(1)
SMEM = pl.BlockSpec(memory_space=pltpu.SMEM)
ANYWHERE = pl.BlockSpec(memory_space=pl.ANY)


def whole(shape):
    return pl.BlockSpec(shape, lambda i: (0,) * len(shape), pipeline_mode=ONCE)


def of_layer(layer, shape):
    return pl.BlockSpec(
        (None, *shape), lambda i: (layer,) + (0,) * len(shape), pipeline_mode=ONCE
    )


def params(mib):
    return pltpu.CompilerParams(
        vmem_limit_bytes=mib * MIB, dimension_semantics=("arbitrary",)
    )


def cost(flops, nbytes):
    return pl.CostEstimate(flops=flops, bytes_accessed=nbytes, transcendentals=0)


def attention_forward(layer, parts, weights, tables, segment, gathered=()):
    gain, wq, wk, wv, wo = weights
    length, features = parts[0].shape
    q_width, k_width = wq.shape[2], wk.shape[2]
    heads = 2 * k_width // LANES
    ins = [*parts, gain, wq, wk, wv, wo, *tables, *segment]
    in_specs = [whole(part.shape) for part in parts]
    in_specs += [of_layer(layer, w.shape[1:]) for w in (gain, wq, wk, wv, wo)]
    in_specs += [whole(t.shape) for t in (*tables, *segment)]
    outs = [
        ((length, features), F32),
        ((length, features), BF16),
        ((length, q_width), BF16),
        ((heads, length, LANES), BF16),
        ((heads, length, LANES), BF16),
        ((length, q_width), BF16),
        ((length, features), F32),
    ]
    scratch = []
    if gathered:
        ins += gathered
        in_specs += [SMEM, *(whole(array.shape) for array in gathered[1:])]
        outs += [outs[2], outs[3], outs[4], outs[6], ((4 * gathered[1].shape[0], features), BF16)]
        scratch = [pltpu.VMEM((length, q_width), BF16)]
    return pl.pallas_call(
        functools.partial(attention_forward_kernel, len(parts), bool(gathered)),
        grid=(1,),
        scratch_shapes=scratch,
        in_specs=in_specs,
        out_specs=[whole(shape) for shape, _ in outs],
        out_shape=[jax.ShapeDtypeStruct(*out) for out in outs],
        compiler_params=params(60),
        cost_estimate=cost(6 << 30, 8 * MIB),
        name="attention_forward",
    )(*ins)


def column_of(table, lane, index):
    return jnp.sum(jnp.where(lane == index, table, 0.0), axis=1, keepdims=True)


def expert_prologue(x, own, other, gain, router, mask, middle_out, xi_out, share_out):
    middle = x[...] + (own[...] + other[...])
    middle_out[...] = middle
    xi = (middle * row_factor(middle) * gain[...].astype(F32)).astype(BF16)
    xi_out[...] = xi
    logits = mm(xi, router[...])
    chosen = mask[...] > 0.5
    logits = jnp.where(chosen, logits, EXCLUDED)
    shifted = jnp.exp(logits - jnp.max(logits, axis=-1, keepdims=True))
    shifted = jnp.where(chosen, shifted, 0.0)
    share_out[...] = shifted / jnp.sum(shifted, axis=-1, keepdims=True)


def expert_step(gate_in, linear, wd, share):
    squashed = 1.0 / (1.0 + jnp.exp(-gate_in))
    silu = gate_in * squashed
    activation = (silu * linear).astype(BF16)
    return squashed, silu, activation, mm(activation, wd)


def expert_backward_step(places, g, xi, share, gate_in, linear, wg, wu, wd, keep, send):
    where_to = block_places(EXPERT_ORDERS, places, pl.program_id(0) >= STREAMS // 2)
    squashed, silu, activation, expert_out = expert_step(gate_in, linear, wd, share)
    gate_grad = jnp.sum(g * expert_out, axis=1, keepdims=True)
    expert_grad = (share * g).astype(BF16)
    activation_grad = mm_nt(expert_grad, wd)
    gate_in_grad = (
        activation_grad * linear * squashed * (1.0 + gate_in * (1.0 - squashed))
    ).astype(BF16)
    linear_grad = (activation_grad * silu).astype(BF16)
    width = activation.shape[1]
    store_blocks(keep, send, mm_tn(xi, gate_in_grad), 0, where_to)
    store_blocks(keep, send, mm_tn(xi, linear_grad), width, where_to)
    store_blocks(keep, send, mm_tn(expert_grad, activation), 2 * width, where_to)
    return gate_grad, mm_nt(gate_in_grad, wg) + mm_nt(linear_grad, wu), expert_out


def expert_forward_kernel(
    x, own, other, gain, router, mask, wg, wu, wd,
    middle_out, xi_out, share_out, gate_out, linear_out, part_out,
):
    expert = pl.program_id(0)

    @pl.when(expert == 0)
    def _():
        expert_prologue(x, own, other, gain, router, mask, middle_out, xi_out, share_out)
        part_out[...] = jnp.zeros_like(part_out)

    share = column_of(share_out[...], lane_of(share_out.shape[0]), expert)
    xi = xi_out[...]
    gate_in = mm(xi, wg[...])
    linear = mm(xi, wu[...])
    gate_out[...] = gate_in
    linear_out[...] = linear
    part_out[...] += share * expert_step(gate_in, linear, wd[...], share)[3]


def expert_both_kernel(
    places, x, own, other, gain, router, mask, wg, wu, wd, cotangent,
    middle_out, xi_out, share_out, part_out, back_out, gate_grad_out, keep, send,
):
    expert = pl.program_id(0)
    lane = lane_of(share_out.shape[0])

    @pl.when(expert == 0)
    def _():
        expert_prologue(x, own, other, gain, router, mask, middle_out, xi_out, share_out)
        part_out[...] = jnp.zeros_like(part_out)
        back_out[...] = jnp.zeros_like(back_out)
        gate_grad_out[...] = jnp.zeros_like(gate_grad_out)

    share = column_of(share_out[...], lane, expert)
    xi = xi_out[...]
    gate_in = mm(xi, wg[...])
    linear = mm(xi, wu[...])
    gate_grad, back, expert_out = expert_backward_step(
        places, cotangent[...].astype(F32), xi, share, gate_in, linear, wg[...], wu[...],
        wd[...], keep, send,
    )
    part_out[...] += share * expert_out
    back_out[...] += back
    gate_grad_out[...] += jnp.where(lane == expert, gate_grad, 0.0)


def expert_backward_kernel(
    places, g_in, x, gain, own, other, xi_ref, share_ref, gate_ref, linear_ref, wg, wu, wd,
    *rest,
):
    g_out, gain_out, back_out, gate_grad_out, keep, send = rest[-6:]
    expert = pl.program_id(0)
    lane = lane_of(share_ref.shape[0])

    @pl.when(expert == 0)
    def _():
        stream = x[...]
        change, gain_row = norm_back(
            stream, row_factor(stream), gain[...].astype(F32), own[...] + other[...]
        )
        g_out[...] = g_in[...] + change
        gain_out[...] = jnp.broadcast_to(gain_row, gain_out.shape)
        back_out[...] = jnp.zeros_like(back_out)
        gate_grad_out[...] = jnp.zeros_like(gate_grad_out)

    share = column_of(share_ref[...], lane, expert)
    gate_grad, back, _ = expert_backward_step(
        places, g_out[...], xi_ref[...], share, gate_ref[...], linear_ref[...], wg[...],
        wu[...], wd[...], keep, send,
    )
    back_out[...] += back
    gate_grad_out[...] += jnp.where(lane == expert, gate_grad, 0.0)


def of_expert(layer, shape):
    return pl.BlockSpec((None, None, *shape), lambda e: (layer, e, 0, 0))


def each_expert(shape):
    return pl.BlockSpec((None, *shape), lambda e: (e, 0, 0))


def gradient_outs(rows, width):
    spec = pl.BlockSpec((rows, 3 * width), lambda e: (0, e))
    shape = ((rows, 3 * width * STREAMS), F32)
    return [(spec, shape)] * 2


def run_experts(kernel, name, ins, in_specs, outs, flops, nbytes, mib):
    return pl.pallas_call(
        kernel,
        grid=(STREAMS,),
        in_specs=in_specs,
        out_specs=[spec for spec, _ in outs],
        out_shape=[jax.ShapeDtypeStruct(*out) for _, out in outs],
        compiler_params=params(mib),
        cost_estimate=cost(flops, nbytes),
        name=name,
    )(*ins)


def expert_forward(layer, x, own, other, gain, router, mask, wg, wu, wd):
    length, features = x.shape
    width = wg.shape[3]
    big, low = ((length, features), F32), ((length, features), BF16)
    hidden = (each_expert((length, width)), ((STREAMS, length, width), F32))
    ins = [x, own, other, gain, router, mask, wg, wu, wd]
    in_specs = [whole(x.shape)] * 3 + [
        of_layer(layer, gain.shape[1:]),
        of_layer(layer, router.shape[1:]),
        of_layer(layer, mask.shape[1:]),
        *(of_expert(layer, w.shape[2:]) for w in (wg, wu, wd)),
    ]
    outs = [
        (whole(big[0]), big),
        (whole(low[0]), low),
        (whole((length, LANES)), ((length, LANES), F32)),
        hidden,
        hidden,
        (whole(big[0]), big),
    ]
    return run_experts(
        expert_forward_kernel, "experts_forward", ins, in_specs, outs, 8 << 30, 12 * MIB, 60
    )


def expert_both(layer, places, x, own, other, gain, router, mask, wg, wu, wd, cotangent):
    length, features = x.shape
    width = wg.shape[3]
    big, low = ((length, features), F32), ((length, features), BF16)
    table = (whole((length, LANES)), ((length, LANES), F32))
    ins = [places, x, own, other, gain, router, mask, wg, wu, wd, cotangent]
    in_specs = [SMEM] + [whole(x.shape)] * 3 + [
        of_layer(layer, gain.shape[1:]),
        of_layer(layer, router.shape[1:]),
        of_layer(layer, mask.shape[1:]),
        *(of_expert(layer, w.shape[2:]) for w in (wg, wu, wd)),
        whole(cotangent.shape),
    ]
    outs = [
        (whole(big[0]), big),
        (whole(low[0]), low),
        table,
        (whole(big[0]), big),
        (whole(big[0]), big),
        table,
        *gradient_outs(features // 2, width),
    ]
    return run_experts(
        expert_both_kernel, "experts_both", ins, in_specs, outs, 16 << 30, 30 * MIB, 60
    )


def expert_backward(
    layer, places, g, x, gain, own, other, xi, share, gate_in, linear, wg, wu, wd, after
):
    length, features = x.shape
    width = wg.shape[3]
    big = ((length, features), F32)
    table = (whole((length, LANES)), ((length, LANES), F32))
    hidden = each_expert((length, width))
    ins = [places, g, x, gain, own, other, xi, share, gate_in, linear, wg, wu, wd, *after]
    in_specs = [SMEM, whole(x.shape), whole(x.shape)] + [
        of_layer(layer + 1, gain.shape[1:]),
        whole(x.shape),
        whole(x.shape),
        whole(x.shape),
        whole(share.shape),
        hidden,
        hidden,
        *(of_expert(layer, w.shape[2:]) for w in (wg, wu, wd)),
        *([ANYWHERE] * len(after)),
    ]
    outs = [
        (whole(big[0]), big),
        (whole((8, features)), ((8, features), F32)),
        (whole(big[0]), big),
        table,
        *gradient_outs(features // 2, width),
    ]
    return run_experts(
        expert_backward_kernel, "experts_backward", ins, in_specs, outs, 4 << 30, 30 * MIB, 60
    )


def attend_backward(mixture_grad, q, kk, vv, cosine, sine, allowed):
    length = mixture_grad.shape[0]
    lane = lane_of(length)
    low = lane < HEAD_SIZE
    scale = HEAD_SIZE**-0.5
    query_grads, key_grads, value_grads = [], [], []
    for pair in range(q.shape[1] // LANES // 2):
        key_sides, value_sides = [], []
        for side in range(2):
            head = 2 * pair + side
            columns = slice(head * LANES, (head + 1) * LANES)
            stacked = stacked_pair(q[:, columns], lane)
            scores = jnp.where(allowed, mm_nt(stacked, kk[head]) * scale, EXCLUDED)
            shifted = jnp.exp(scores - jnp.max(scores, axis=-1, keepdims=True))
            probs = shifted / jnp.sum(shifted, axis=-1, keepdims=True)
            mix_grad = stacked_pair(mixture_grad[:, columns], lane)
            prob_grad = mm_nt(mix_grad, vv[head])
            inner = jnp.sum(probs * prob_grad, axis=-1, keepdims=True)
            score_grad = (probs * (prob_grad - inner)).astype(BF16)
            query = mm(score_grad, kk[head])
            query = jnp.where(low, query[:length], query[length:]) * scale
            query = query * cosine - partner(query, lane) * sine
            query_grads.append(query.astype(BF16))
            key = mm_tn(score_grad, stacked) * scale
            key_sides.append(key + pltpu.roll(key, HEAD_SIZE, 1))
            value = mm_tn(probs.astype(BF16), mix_grad)
            value_sides.append(value + pltpu.roll(value, HEAD_SIZE, 1))
        key = jnp.where(low, key_sides[0], key_sides[1])
        key_grads.append((key * cosine - partner(key, lane) * sine).astype(BF16))
        value_grads.append(jnp.where(low, value_sides[0], value_sides[1]).astype(BF16))
    return tuple(
        jnp.concatenate(grads, axis=1) for grads in (query_grads, key_grads, value_grads)
    )


def attention_backward_kernel(
    count, full, orders, places, g, own, other, gate_own, gate_other, middle, xi, share, gain, router_rows,
    wo, mix, q, kk, vv, a, wq, wk, wv, cos, sin, seg_row, seg_column, x, late_gain, *rest,
):
    if full:
        q_other, kk_other, vv_other, weights = rest[:4]
        part_other = rest[-2]
        rest = rest[4:]
    g_out, part_out, keep, send = rest[count : count + 4]
    rows_scratch = rest[-1]
    where_to = block_places(orders, places)
    length = middle.shape[0]
    lane = lane_of(length)
    shares = share[...]
    gate_grad = gate_own[...] + gate_other[...]
    pick = shares * (gate_grad - jnp.sum(shares * gate_grad, axis=1, keepdims=True))
    input_grad = own[...] + other[...]
    xi_full = xi[...].astype(F32)
    rows_scratch[...] = jnp.zeros_like(rows_scratch)
    for expert in range(STREAMS):
        logit_grad = column_of(pick, lane, expert)
        input_grad = input_grad + logit_grad * router_rows[expert : expert + 1, :]
        rows_scratch[expert : expert + 1, :] = jnp.sum(
            xi_full * logit_grad, axis=0, keepdims=True
        )
    mid = middle[...]
    change, gain_row = norm_back(mid, row_factor(mid), gain[...].astype(F32), input_grad)
    rows_scratch[4:5, :] = gain_row
    rows_scratch[6:7, :] = late_gain[0:1, :]
    gradient = g[...].astype(F32) + change
    g_out[...] = gradient
    output_grad = gradient.astype(BF16)
    common = (cos[...], sin[...], allowed_pairs(seg_row[...], seg_column[...]))

    def half(output_weight, weights, *saved):
        mixture_grad = mm_nt(output_grad, output_weight[...]).astype(BF16)
        grads = attend_backward(mixture_grad, *saved, *common)
        part = sum(mm_nt(grad, weight[...]) for grad, weight in zip(grads, weights))
        return grads, part

    if full:
        wq_other, wk_other, wv_other, wo_other = halves_of(weights)
        part_other[...] = half(
            wo_other, (wq_other, wk_other, wv_other), q_other, kk_other, vv_other
        )[1]
    grads, attention_part = half(wo, (wq, wk, wv), q, kk, vv)
    part_out[...] = attention_part
    stream = x[...]
    rows_scratch[5:6, :] = jnp.sum(
        attention_part * stream * row_factor(stream), axis=0, keepdims=True
    )
    a_full = a[...]
    column = 0
    for total in (
        jnp.transpose(rows_scratch[...]),
        *(mm_tn(a_full, grad) for grad in grads),
        mm_tn(output_grad, mix[...]),
    ):
        store_blocks(keep, send, total, column, where_to)
        column += total.shape[1]


def attention_backward(
    layer, orders, places, g, own, other, gate_own, gate_other, saved_experts, weights, saved,
    tables, segment, late_gain, after, others=(),
):
    middle, xi, share = saved_experts
    gain, router_rows, wo, wq, wk, wv = weights
    x, a, q, kk, vv, mix = saved
    length, features = middle.shape
    columns = SMALL + wq.shape[2] + wk.shape[2] + wv.shape[2] + wo.shape[1]
    ins = [
        places, g, own, other, gate_own, gate_other, middle, xi, share, gain, router_rows,
        wo, mix, q, kk, vv, a, wq, wk, wv, *tables, *segment, x, late_gain,
    ]
    layered = {9, 10, 11, 17, 18, 19}
    in_specs = [SMEM]
    for at, array in enumerate(ins[1:], 1):
        in_specs.append(of_layer(layer, array.shape[1:]) if at in layered else whole(array.shape))
    ins += [*others, *after]
    in_specs += [whole(array.shape) for array in others]
    in_specs += [ANYWHERE] * len(after)
    outs = [
        ((length, features), F32),
        ((length, features), F32),
        ((features // 2, columns), F32),
        ((features // 2, columns), F32),
    ]
    if others:
        outs.append(((length, features), F32))
    return pl.pallas_call(
        functools.partial(
            attention_backward_kernel, len(after), bool(others), orders
        ),
        grid=(1,),
        in_specs=in_specs,
        out_specs=[whole(shape) for shape, _ in outs],
        out_shape=[jax.ShapeDtypeStruct(*out) for out in outs],
        scratch_shapes=[pltpu.VMEM((LANES, features), F32)],
        compiler_params=params(60),
        cost_estimate=cost(16 << 30, 18 * MIB),
        name="attention_backward",
    )(*ins)


SWAP = ((0, 1), (1, 0))
RING = {"u": tuple((i, i ^ 1) for i in range(4)), "v": tuple((i, 3 - i) for i in range(4))}


def exchange(array):
    return lax.ppermute(array, "tensor", SWAP)


RING_AXES = ("dp_0", "dp_2", "dp_3")


def ring_pairs(orders, step):
    pairs = []
    for x in range(4):
        for z in range(4):
            for core in range(2):
                ring, kind = orders[core][step]
                at = x if ring == "x" else z
                to = at ^ 1 if kind == "u" else 3 - at
                there = (to, z) if ring == "x" else (x, to)
                pairs.append(((x * 4 + z) * 2 + core, (there[0] * 4 + there[1]) * 2 + core))
    return pairs


class Scatter:
    def __init__(self, keep, send, *orders):
        received = lax.ppermute(send, "dp_3", SWAP)
        width = keep.shape[1] // len(orders)
        self.orders = orders
        self.parts = [
            [array[:, at * width : (at + 1) * width] for array in (keep, received)]
            for at in range(len(orders))
        ]
        self.step = 0

    def halve(self):
        half = self.parts[0][0].shape[0] // 2
        self.kept = [first[:half] + second[:half] for first, second in self.parts]
        return [first[half:] + second[half:] for first, second in self.parts]

    def move(self, sends):
        moved = [
            lax.ppermute(send, RING_AXES, ring_pairs(orders, self.step))
            for send, orders in zip(sends, self.orders)
        ]
        self.parts = [list(pair) for pair in zip(self.kept, moved)]
        self.step += 1

    def received(self):
        return [second for _, second in self.parts]

    def advance(self, count=1):
        for _ in range(count):
            self.move(self.halve())

    def join(self, other):
        self.parts = [
            [jnp.concatenate(pair, axis=1) for pair in zip(*both)]
            for both in zip(self.parts, other.parts)
        ]

    def finish(self):
        sends = jnp.concatenate(self.halve(), axis=-1)
        return jnp.concatenate(self.kept, axis=-1) + lax.ppermute(sends, "dp_1", SWAP)


class Gather:
    def __init__(self, weights, layer):
        x, z, core = (lax.axis_index(name) for name in RING_AXES)
        piece = (x * 4 + z) * 2 + core

        def rows_of(weight):
            rows = weight.shape[1] // 32
            return lax.dynamic_slice_in_dim(weight[layer], piece * rows, rows, 0).astype(F32)

        *inputs, output = (rows_of(weight) for weight in weights)
        self.piece = jnp.concatenate([jnp.concatenate(inputs, axis=1), output], axis=0)
        orders = [*EXPERT_ORDERS, *(swapped(order) for order in EXPERT_ORDERS)]
        places = [ring_place(order, x, z) for order in orders]
        self.places = jnp.stack([*places, core]).astype(jnp.int32)

        self.crossed = exchange(self.piece)

    def begin(self, after, received):
        held, *_ = behind([self.crossed], after)
        for step in (3, 2):
            moved = lax.ppermute(held, RING_AXES, ring_pairs(EXPERT_ORDERS, step))
            held = jnp.concatenate([held, moved], axis=0)
        half = held.shape[1] // 2
        self.held = behind([held[:, :half], held[:, half:]], received)
        self.moved = self.moves(self.held, 1)

    def moves(self, held, step):
        return [
            lax.ppermute(half, RING_AXES, ring_pairs(EXPERT_ORDERS, at))
            for half, at in zip(held, (step, 1 - step))
        ]

    def finish(self, after):
        held = behind(self.held, after)
        held = [jnp.concatenate(pair, axis=0) for pair in zip(held, self.moved)]
        near = [*held, *self.moves(held, 0)]
        return [self.places, *near, *(lax.ppermute(half, "dp_3", SWAP) for half in near)]


def behind(arrays, *after):
    return pl.pallas_call(
        lambda *refs: None,
        in_specs=[ANYWHERE] * (len(arrays) + len(after)),
        out_specs=[ANYWHERE] * len(arrays),
        out_shape=[jax.ShapeDtypeStruct(array.shape, array.dtype) for array in arrays],
        input_output_aliases={at: at for at in range(len(arrays))},
        name="behind",
    )(*arrays, *after)


def rope_tables(length):
    half = HEAD_SIZE // 2
    frequency = np.float32(THETA) ** (-2.0 * np.arange(half, dtype=np.float32) / HEAD_SIZE)
    angles = np.arange(length, dtype=np.float32)[:, None] * frequency[None].astype(np.float32)
    angles = angles.astype(np.float32)
    cosine = np.tile(np.cos(angles), (1, LANES // half)).astype(np.float32)
    sine = np.sin(angles)
    sine = np.tile(np.concatenate([-sine, sine], axis=1), (1, LANES // HEAD_SIZE))
    return jnp.asarray(cosine), jnp.asarray(sine.astype(np.float32))


def shards(
    tokens, segments, routes, norm_attention, query_weight, key_matrix, value_matrix,
    output_weight, norm_experts, router_weight, gate_weight, up_weight, down_weight, cotangent,
):
    length, features = tokens.shape
    experts = gate_weight.shape[1]
    hidden = gate_weight.shape[3]
    tables = rope_tables(length)
    segment = (segments.reshape(1, length), segments.reshape(length, 1))
    gain_attention = norm_attention[:, None, :]
    gain_experts = norm_experts[:, None, :]
    router = jnp.pad(router_weight, ((0, 0), (0, 0), (0, LANES - experts)))
    router_rows = jnp.pad(
        jnp.swapaxes(router_weight, 1, 2).astype(F32), ((0, 0), (0, 8 - experts), (0, 0))
    )
    mask = jnp.any(
        routes[..., None] == jnp.arange(LANES, dtype=jnp.int32), axis=2
    ).astype(F32)
    x_at, y_at, z_at = (lax.axis_index(name) for name in DP[:3])
    core = lax.axis_index("dp_3")

    def places_in(orders):
        found = []
        for which in (orders, [swapped(order) for order in orders]):
            one, two = (place(order, x_at, y_at, z_at) for order in which)
            found += [jnp.where(core == 0, one, two), jnp.where(core == 0, two, one)]
        return jnp.stack([*found, core]).astype(jnp.int32)

    expert_places = places_in(EXPERT_ORDERS)
    late_orders = tuple(swapped(order) for order in ATTENTION_ORDERS)

    attention_weights = (gain_attention, query_weight, key_matrix, value_matrix, output_weight)
    expert_weights = (gate_weight, up_weight, down_weight)
    back_weights = (
        gain_experts, router_rows, output_weight, query_weight, key_matrix, value_matrix,
    )

    others = Gather(attention_weights[1:], 1)
    x1, *saved1, part = attention_forward(0, [tokens], attention_weights, tables, segment)
    other = exchange(part)
    others.begin(part, other)
    middle1, xi1, share1, gate1, linear1, part = expert_forward(
        0, x1, part, other, gain_experts, router, mask, *expert_weights
    )
    x2, *saved2, part, q_other, kk_other, vv_other, part_other, weights_other = attention_forward(
        1, [middle1, part, exchange(part)], attention_weights, tables, segment,
        others.finish(part),
    )
    middle2, xi2, share2, last, back, gate_grad, keep, send = expert_both(
        1, expert_places, x2, part, part_other, gain_experts, router, mask, *expert_weights,
        cotangent,
    )
    both_orders = (EXPERT_ORDERS, tuple(swapped(order) for order in EXPERT_ORDERS))
    sum_e2 = Scatter(keep, send, *both_orders)
    other, gate_other = exchange(back), exchange(gate_grad)
    *sends, last = behind([*sum_e2.halve(), last], other)
    sum_e2.move(sends)
    last_other = exchange(last)
    no_gain = jnp.zeros((8, features), F32)
    g2, part, keep, send, part_other = attention_backward(
        1, late_orders, places_in(late_orders), cotangent, back, other, gate_grad, gate_other,
        (middle2, xi2, share2), back_weights, (x2, *saved2), tables, segment, no_gain, sends,
        (q_other, kk_other, vv_other, weights_other),
    )
    sum_a2 = Scatter(keep, send, late_orders)
    sends = sum_e2.halve()
    g1, late_gain, back, gate_grad, keep, send = expert_backward(
        0, expert_places, g2, x2, gain_attention, part, part_other, xi1, share1, gate1,
        linear1, *expert_weights, [*sends, last_other],
    )
    sum_e2.move(sends)
    sum_e1 = Scatter(keep, send, *both_orders)
    other, gate_other = exchange(back), exchange(gate_grad)
    sends_a, sends_e = sum_a2.halve(), sum_e1.halve()
    sum_a2.move(sends_a)
    sum_e1.move(sends_e)
    sends = sends_a + sends_e + sum_e2.received()
    g0, part, keep, send = attention_backward(
        0, ATTENTION_ORDERS, places_in(ATTENTION_ORDERS), g1, back, other, gate_grad, gate_other,
        (middle1, xi1, share1), back_weights, (x1, *saved1), tables, segment, late_gain,
        sends,
    )
    (send,) = behind([send], *sum_a2.received(), *sum_e1.received())
    sum_a1 = Scatter(keep, send, ATTENTION_ORDERS)
    sum_a1.advance()
    (other,) = behind([exchange(part)], *sum_a1.received())
    sum_a1.advance()
    sum_e1.advance()
    sum_a2.advance()
    sums = ((sum_a1, sum_a2), (sum_e1, sum_e2))
    for one, two in sums:
        one.join(two)
        one.advance(2)
    gain = norm_attention[0].astype(F32)
    change, _ = norm_back(x1, row_factor(x1), gain, part + other)
    gradient = g0 + change
    output = (middle2 + (last + last_other)).astype(BF16)
    blocks = [one.finish() for one, _ in sums]

    attention_sums, expert_sums = blocks
    rows = attention_sums.shape[0]
    layers = query_weight.shape[0]
    attention_sums = jnp.swapaxes(attention_sums.reshape(rows, layers, -1), 0, 1)
    bounds = np.cumsum(
        [0, SMALL, query_weight.shape[2], key_matrix.shape[2], value_matrix.shape[2],
         output_weight.shape[1]]
    )
    attention_sums = [attention_sums[..., a:b] for a, b in zip(bounds[:-1], bounds[1:])]
    expert_sums = expert_sums.reshape(rows, 2, layers, experts // 2, 3, hidden)
    expert_sums = [
        expert_sums[..., kind, :].transpose(2, 1, 3, 0, 4).reshape(layers, experts, rows, hidden)
        for kind in range(3)
    ]
    small = attention_sums[0]
    attention_gain = small[:, :, 5]
    attention_gain = attention_gain + exchange(attention_gain)
    return (
        output,
        gradient,
        attention_gain,
        *attention_sums[1:4],
        jnp.swapaxes(attention_sums[4], 1, 2),
        small[:, :, 4],
        small[:, :, :experts],
        expert_sums[0],
        expert_sums[1],
        jnp.swapaxes(expert_sums[2], 2, 3),
    )


def solution(mesh):
    torus = Mesh(
        mesh.devices.reshape(*DP_SIZES, mesh.shape["tensor"]), (*DP, "tensor")
    )
    rows, copied, last = P(DP, None), P(), P(None, None, "tensor")
    in_specs = (
        rows, rows, P(None, DP, None), copied, last, last, last, P(None, "tensor", None),
        copied, copied, P(None, None, None, "tensor"), P(None, None, None, "tensor"),
        P(None, None, "tensor", None), rows,
    )
    out_specs = (
        rows, rows, P(None, DP), P(None, DP, "tensor"), P(None, DP, "tensor"),
        P(None, DP, "tensor"), P(None, "tensor", DP), P(None, DP), P(None, DP, None),
        P(None, None, DP, "tensor"), P(None, None, DP, "tensor"), P(None, None, "tensor", DP),
    )
    return jax.shard_map(
        shards, mesh=torus, in_specs=in_specs, out_specs=out_specs, check_vma=False
    )
```

profile of v0, /device:TPU:0, one launch (start us, length us, event | category | flops | bytes accessed | tf_op | source)
XLA Modules:
  0.0 359.6 jit_solution(17742354645089320498)
XLA Ops:
  0.7 1.2 slice-done.2
  2.5 1.7 collective-permute-start.2
  5.7 6.6 %attention_forward.2 = (f32[256,1024]{1,0:T(8,128)}, bf16[256,1024]{1,0:T(8,128)(2,1)}, bf16[256,512]{1,0:T(8,128)(2,1)}, bf16[4,256,128]{2,1,0:T(8,128)(2,1)}, ...) custom-call(bf16[256,1024]{1,0:T(8,128)(2,1)} %refs_0_.1, ...), custom_call_target="tpu_custom_call" | custom-call | flops 6442450944 | bytes 8388608 | tf_op jit(solution)/shard_map/attention_forward/pallas_call | solution.py:282
  13.0 2.8 collective-permute-start.3
  16.2 3.9 %collective-permute-done.3 = f32[48,1024]{1,0:T(8,128)S(1)} collective-permute-done((f32[48,1024]{1,0:T(8,128)}, f32[48,1024]{1,0:T(8,128)S(1)}, u32[]{:S(2)}, u32[]{:S(2)}) %collective-permute-start.3) | collective-permute-done | bytes 196640 | tf_op jit(solution)/shard_map/ppermute | solution.py:748
  21.0 4.1 %collective-permute-start.4 = (f32[96,1024]{1,0:T(8,128)S(1)}, f32[96,1024]{1,0:T(8,128)S(1)}, u32[]{:S(2)}, u32[]{:S(2)}) collective-permute-start(f32[96,1024]{1,0:T(8,128)S(1)} %pad_maximum_fusion.4), channel_id=1, source_target_pairs={{0,12},{2,34},{4,8},{6,38},{8,4},{10,42},{12,0},{14,46},{32,44},{3... | collective-permute-start | bytes 1179656 | tf_op jit(solution)/shard_map/ppermute | solution.py:748
  27.9 3.0 collective-permute-done.4
  31.9 7.5 %collective-permute-done.other.refs_2_ = f32[256,1024]{1,0:T(8,128)S(1)} collective-permute-done((f32[256,1024]{1,0:T(8,128)}, f32[256,1024]{1,0:T(8,128)S(1)}, u32[]{:S(2)}, u32[]{:S(2)}) %collective-permute-start) | collective-permute-done | bytes 1048608 | tf_op jit(solution)/shard_map/ppermute | solution.py:667
  40.7 1.5 collective-permute-start.6
  42.2 7.9 %experts_forward.1 = (f32[256,1024]{1,0:T(8,128)}, bf16[256,1024]{1,0:T(8,128)(2,1)}, f32[256,128]{1,0:T(8,128)}, f32[4,256,256]{2,1,0:T(8,128)}, f32[4,256,256]{2,1,0:T(8,128)}, /*index=5*/f32[256,1024]{1,0:T(8,128)}) custom-call(f32[256,1024]{1,0:T(8,128)} %get-tuple-element.67.x, f32[256,1024]{1,0:T(8,128)} %get-tuple-element.68.own.refs_1_, ...), custom_call_target="tpu_custom_call" | custom-call | flops 8589934592 | bytes 12582912 | tf_op jit(solution)/shard_map/experts_forward/pallas_call | solution.py:426
  50.2 1.1 constant_dynamic-update-slice_fusion.1
  53.0 1.8 collective-permute-start.8
  56.1 8.4 %collective-permute-done.7.refs_15_ = f32[384,512]{1,0:T(8,128)} collective-permute-done((f32[384,512]{1,0:T(8,128)S(1)}, f32[384,512]{1,0:T(8,128)}, u32[]{:S(2)}, u32[]{:S(2)}) %collective-permute-start.7) | collective-permute-done | bytes 786464 | tf_op jit(solution)/shard_map/ppermute | solution.py:756
  64.5 1.3 collective-permute-start.11
  65.8 2.2 collective-permute-start.12
  69.3 11.6 %collective-permute-done.1.refs_2_ = f32[256,1024]{1,0:T(8,128)} collective-permute-done((f32[256,1024]{1,0:T(8,128)S(1)}, f32[256,1024]{1,0:T(8,128)}, u32[]{:S(2)}, u32[]{:S(2)}) %collective-permute-start.1) | collective-permute-done | bytes 1048608 | tf_op jit(solution)/shard_map/ppermute | solution.py:667
  80.9 16.1 %attention_forward.3 = (f32[256,1024]{1,0:T(8,128)}, bf16[256,1024]{1,0:T(8,128)(2,1)}, bf16[256,512]{1,0:T(8,128)(2,1)}, bf16[4,256,128]{2,1,0:T(8,128)(2,1)}, ...) custom-call(f32[256,1024]{1,0:T(8,128)} %get-tuple-element.69.refs_0, ...), custom_call_target="tpu_custom_call" | custom-call | flops 6442450944 | bytes 8388608 | tf_op jit(solution)/shard_map/attention_forward/pallas_call | solution.py:282
  97.0 14.7 %experts_both.1 = (f32[256,1024]{1,0:T(8,128)}, bf16[256,1024]{1,0:T(8,128)(2,1)}, f32[256,128]{1,0:T(8,128)}, f32[256,1024]{1,0:T(8,128)}, f32[256,1024]{1,0:T(...) custom-call(s32[5]{0:T(128)} %stack.55.places, f32[256,1024]{1,0:T(8,128)} %get-tuple-element.75.x, ...), custom_call_target="tpu_custom_call" | custom-call | flops 17179869184 | bytes 31457280 | tf_op jit(solution)/shard_map/experts_both/pallas_call | solution.py:426
  113.6 1.6 collective-permute-start.16
  115.2 7.1 %collective-permute-done.13 = f32[512,3072]{1,0:T(8,128)} collective-permute-done((f32[512,3072]{1,0:T(8,128)}, f32[512,3072]{1,0:T(8,128)}, u32[]{:S(2)}, u32[]{:S(2)}) %collective-permute-start.13) | collective-permute-done | bytes 6291488 | tf_op jit(solution)/shard_map/ppermute | solution.py:688
  122.3 7.8 %slice_add_fusion.8 = (f32[256,1536]{1,0:T(8,128)S(1)}, f32[256,1536]{1,0:T(8,128)S(1)}, f32[256,1536]{1,0:T(8,128)}, f32[256,1536]{1,0:T(8,128)}) fusion(f32[512,3072]{1,0:T(8,128)} %collective-permute-done.13, f32[512,3072]{1,0:T(8,128)} %get-tuple-element.79), kind=kLoop, calls=%fused_computation.10 | loop fusion | flops 1572864 | bytes 18874368 | tf_op jit(solution)/shard_map/add | solution.py:699
  130.1 8.1 %collective-permute-done.14.refs_3_.other = f32[256,1024]{1,0:T(8,128)} collective-permute-done((f32[256,1024]{1,0:T(8,128)}, f32[256,1024]{1,0:T(8,128)}, u32[]{:S(2)}, u32[]{:S(2)}) %collective-permute-start.14) | collective-permute-done | bytes 1048608 | tf_op jit(solution)/shard_map/ppermute | solution.py:667
  141.3 21.5 %attention_backward.2 = (f32[256,1024]{1,0:T(8,128)}, f32[256,1024]{1,0:T(8,128)}, f32[512,1664]{1,0:T(8,128)}, f32[512,1664]{1,0:T(8,128)}, f32[256,1024]{1,0:T(8,128)}) custom-call(s32[5]{0:T(128)} %stack.62.places, bf16[256,1024]{1,0:T(8,128)(2,1)} %g.1, f32[256,1024]{1,0:T(8,128)} %get-tuple-element.82.own, ...), custom_call_target="tpu_custom_call" | custom-call | flops 17179869184 | bytes 18874368 | tf_op jit(solution)/shard_map/attention_backward/pallas_call | solution.py:647
  162.9 2.7 slice_add_fusion.23
  165.6 2.7 slice_add_fusion.19
  168.3 13.7 %experts_backward.1 = (f32[256,1024]{1,0:T(8,128)}, f32[8,1024]{1,0:T(8,128)}, f32[256,1024]{1,0:T(8,128)}, f32[256,128]{1,0:T(8,128)}, f32[512,3072]{1,0:T(8,128)}, /*index=5*/f32[512,3072]{1,0:T(8,128)}) custom-call(s32[5]{0:T(128)} %stack.55.places, f32[256,1024]{1,0:T(8,128)} %get-tuple-element.98.g_in, f32[256,1024]{1,0:T(8,128)} %get-tuple-element.75.x, ...), custom_call_target="tpu_custom_call" | custom-call | flops 4294967296 | bytes 31457280 | tf_op jit(solution)/shard_map/experts_backward/pallas_call | solution.py:426
  183.5 2.4 add_convert_fusion
  185.9 1.2 collective-permute-start.23
  188.1 1.6 collective-permute-start.19
  189.7 8.1 %collective-permute-done.21 = f32[512,1664]{1,0:T(8,128)} collective-permute-done((f32[512,1664]{1,0:T(8,128)}, f32[512,1664]{1,0:T(8,128)}, u32[]{:S(2)}, u32[]{:S(2)}) %collective-permute-start.21) | collective-permute-done | bytes 3407904 | tf_op jit(solution)/shard_map/ppermute | solution.py:688
  197.8 1.6 collective-permute-start.20
  199.4 3.8 %slice_add_fusion = (f32[256,1664]{1,0:T(8,128)S(1)}, f32[256,1664]{1,0:T(8,128)}) fusion(f32[512,1664]{1,0:T(8,128)} %collective-permute-done.21, f32[512,1664]{1,0:T(8,128)S(1)} %copy-done.11), kind=kLoop, calls=%fused_computation | loop fusion | flops 851968 | bytes 10223616 | tf_op jit(solution)/shard_map/add | solution.py:699
  204.2 6.2 %slice_add_fusion.5 = (f32[256,1536]{1,0:T(8,128)}, f32[256,1536]{1,0:T(8,128)}, f32[256,1536]{1,0:T(8,128)}, f32[256,1536]{1,0:T(8,128)}) fusion(f32[512,3072]{1,0:T(8,128)} %collective-permute-done.22, f32[512,3072]{1,0:T(8,128)S(1)} %bitcast.54), kind=kLoop, calls=%fused_computation.7 | loop fusion | flops 1572864 | bytes 18874368 | tf_op jit(solution)/shard_map/add | solution.py:699
  210.4 6.4 %collective-permute-done.20.gate_other = f32[256,128]{1,0:T(8,128)S(1)} collective-permute-done((f32[256,128]{1,0:T(8,128)}, f32[256,128]{1,0:T(8,128)S(1)}, u32[]{:S(2)}, u32[]{:S(2)}) %collective-permute-start.20) | collective-permute-done | bytes 131104 | tf_op jit(solution)/shard_map/ppermute | solution.py:667
  218.5 15.1 %attention_backward.3 = (f32[256,1024]{1,0:T(8,128)}, f32[256,1024]{1,0:T(8,128)}, f32[512,1664]{1,0:T(8,128)}, f32[512,1664]{1,0:T(8,128)}) custom-call(s32[5]{0:T(128)} %stack.61.places, f32[256,1024]{1,0:T(8,128)} %get-tuple-element.105.g, f32[256,1024]{1,0:T(8,128)} %get-tuple-element.106.own, f32[256,1024]{1,0:T(8,128)} %collective-permute-done.19.other, ...), custom_call_target="tpu_custom_call" | custom-call | flops 17179869184 | bytes 18874368 | tf_op jit(solution)/shard_map/attention_backward/pallas_call | solution.py:647
  233.6 3.9 %collective-permute-done.27.refs_2_ = f32[256,1536]{1,0:T(8,128)} collective-permute-done((f32[256,1536]{1,0:T(8,128)}, f32[256,1536]{1,0:T(8,128)}, u32[]{:S(2)}, u32[]{:S(2)}) %collective-permute-start.27) | collective-permute-done | bytes 1572896 | tf_op jit(solution)/shard_map/ppermute | solution.py:704
  237.5 3.8 %collective-permute-done.28.refs_3_ = f32[256,1536]{1,0:T(8,128)} collective-permute-done((f32[256,1536]{1,0:T(8,128)}, f32[256,1536]{1,0:T(8,128)}, u32[]{:S(2)}, u32[]{:S(2)}) %collective-permute-start.28) | collective-permute-done | bytes 1572896 | tf_op jit(solution)/shard_map/ppermute | solution.py:704
  241.3 1.9 collective-permute-start.29
  243.2 2.2 slice_add_fusion.20
  245.8 2.0 collective-permute-start.32
  248.3 1.6 slice_add_fusion.24
  250.3 14.6 %collective-permute-done.40 = f32[128,1536]{1,0:T(8,128)S(1)} collective-permute-done((f32[128,1536]{1,0:T(8,128)S(1)}, f32[128,1536]{1,0:T(8,128)S(1)}, u32[]{:S(2)}, u32[]{:S(2)}) %collective-permute-start.40) | collective-permute-done | bytes 786464 | tf_op jit(solution)/shard_map/ppermute | solution.py:704
  264.9 1.2 constant_dynamic-update-slice_fusion.8
  266.4 2.8 collective-permute-start.41
  269.2 1.2 constant_dynamic-update-slice_fusion.6
  271.2 1.1 copy-done.10
  272.7 1.6 collective-permute-start.30
  274.3 5.3 %collective-permute-done.41 = f32[64,3072]{1,0:T(8,128)S(1)} collective-permute-done((f32[64,3072]{1,0:T(8,128)S(1)}, f32[64,3072]{1,0:T(8,128)S(1)}, u32[]{:S(2)}, u32[]{:S(2)}) %collective-permute-start.41) | collective-permute-done | bytes 786464 | tf_op jit(solution)/shard_map/ppermute | solution.py:704
  279.7 1.7 collective-permute-start.42
  281.5 6.6 %collective-permute-done.38 = f32[64,3072]{1,0:T(8,128)S(1)} collective-permute-done((f32[64,3072]{1,0:T(8,128)S(1)}, f32[64,3072]{1,0:T(8,128)S(1)}, u32[]{:S(2)}, u32[]{:S(2)}) %collective-permute-start.38) | collective-permute-done | bytes 786464 | tf_op jit(solution)/shard_map/ppermute | solution.py:704
  288.2 1.7 collective-permute-start.39
  289.9 16.4 %collective-permute-done.30.refs_1_ = f32[256,1664]{1,0:T(8,128)S(1)} collective-permute-done((f32[256,1664]{1,0:T(8,128)S(1)}, f32[256,1664]{1,0:T(8,128)S(1)}, u32[]{:S(2)}, u32[]{:S(2)}) %collective-permute-start.30) | collective-permute-done | bytes 1703968 | tf_op jit(solution)/shard_map/ppermute | solution.py:704
  307.5 1.8 collective-permute-start.31
  309.5 3.0 collective-permute-start.43
  312.5 9.1 %collective-permute-done.31 = f32[128,1664]{1,0:T(8,128)S(1)} collective-permute-done((f32[128,1664]{1,0:T(8,128)S(1)}, f32[128,1664]{1,0:T(8,128)S(1)}, u32[]{:S(2)}, u32[]{:S(2)}) %collective-permute-start.31) | collective-permute-done | bytes 852000 | tf_op jit(solution)/shard_map/ppermute | solution.py:704
  321.8 1.4 fusion.1
  327.7 1.6 multiply_reduce_fusion.1
  329.3 6.9 %collective-permute-done.33 = f32[64,3328]{1,0:T(8,128)} collective-permute-done((f32[64,3328]{1,0:T(8,128)}, f32[64,3328]{1,0:T(8,128)}, u32[]{:S(2)}, u32[]{:S(2)}) %collective-permute-start.33) | collective-permute-done | bytes 852000 | tf_op jit(solution)/shard_map/ppermute | solution.py:704
  336.2 1.4 slice_add_fusion.28
  337.6 1.0 collective-permute-start.34
  338.7 7.2 %collective-permute-done.34 = f32[32,3328]{1,0:T(8,128)S(1)} collective-permute-done((f32[32,3328]{1,0:T(8,128)S(1)}, f32[32,3328]{1,0:T(8,128)S(1)}, u32[]{:S(2)}, u32[]{:S(2)}) %collective-permute-start.34) | collective-permute-done | bytes 426016 | tf_op jit(solution)/shard_map/ppermute | solution.py:704
  345.9 3.2 collective-permute-start.35
  349.0 1.3 subtract_add_fusion
  350.4 2.9 collective-permute-done.35
  (186 shorter events, 38.6 us)
Async XLA Ops:
  0.7 4.1 %copy-start.26 = (s32[1,256]{1,0:T(1,128)S(1)}, s32[1,256]{1,0:T(1,128)}, u32[]{:S(2)}) copy-start(s32[1,256]{1,0:T(1,128)} %seg_row.3) | copy-start | bytes 3076
  2.5 9.8 %collective-permute-start.2 = (f32[48,1024]{1,0:T(8,128)S(1)}, f32[48,1024]{1,0:T(8,128)S(1)}, u32[]{:S(2)}, u32[]{:S(2)}) collective-permute-start(f32[48,1024]{1,0:T(8,128)S(1)} %maximum_convert_fusion), channel_id=1, source_target_pairs={{0,1},{1,0},{2,3},{3,2},{4,5},{5,4},{6,7},{7,6},{8,9},{9,8},{10,11... | collective-permute-start | bytes 589832 | tf_op jit(solution)/shard_map/ppermute | solution.py:667
  12.2 12.9 %copy-start.24 = (bf16[2,1024]{1,0:T(2,128)(2,1)S(1)}, bf16[2,1024]{1,0:T(2,128)(2,1)}, u32[]{:S(2)}) copy-start(bf16[2,1024]{1,0:T(2,128)(2,1)} %param.24) | copy-start | bytes 12292
  12.3 13.5 %copy-start.22 = (bf16[2,1024,4]{1,2,0:T(4,128)(2,1)S(1)}, bf16[2,1024,4]{1,2,0:T(4,128)(2,1)}, u32[]{:S(2)}) copy-start(bf16[2,1024,4]{1,2,0:T(4,128)(2,1)} %param.25) | copy-start | bytes 49156
  12.3 13.8 %copy-start.25 = (s32[2,256,2]{1,2,0:T(2,128)S(1)}, s32[2,256,2]{1,2,0:T(2,128)}, u32[]{:S(2)}) copy-start(s32[2,256,2]{1,2,0:T(2,128)} %param.18) | copy-start | bytes 12292
  13.0 17.9 %copy-start.15 = (f32[48,1024]{1,0:T(8,128)S(1)}, f32[48,1024]{1,0:T(8,128)}, u32[]{:S(2)}) copy-start(f32[48,1024]{1,0:T(8,128)} %behind.6) | copy-start | bytes 589828
  13.0 7.1 %collective-permute-start.3 = (f32[48,1024]{1,0:T(8,128)}, f32[48,1024]{1,0:T(8,128)S(1)}, u32[]{:S(2)}, u32[]{:S(2)}) collective-permute-start(f32[48,1024]{1,0:T(8,128)} %behind.6), channel_id=1, source_target_pairs={{0,96},{2,6},{4,100},{6,2},{8,104},{10,14},{12,108},{14,10},{32,64... | collective-permute-start | bytes 589832 | tf_op jit(solution)/shard_map/ppermute | solution.py:748
  15.7 23.7 %collective-permute-start = (f32[256,1024]{1,0:T(8,128)}, f32[256,1024]{1,0:T(8,128)S(1)}, u32[]{:S(2)}, u32[]{:S(2)}) collective-permute-start(f32[256,1024]{1,0:T(8,128)} %get-tuple-element.68.own.refs_1_), channel_id=1, source_target_pairs={{0,1},{1,0},{2,3},{3,2},{4,5},{5,4},{6,7},{7,6},{8,9},{9,8},{10,11... | collective-permute-start | bytes 3145736 | tf_op jit(solution)/shard_map/ppermute | solution.py:667
  21.0 9.9 %collective-permute-start.4 = (f32[96,1024]{1,0:T(8,128)S(1)}, f32[96,1024]{1,0:T(8,128)S(1)}, u32[]{:S(2)}, u32[]{:S(2)}) collective-permute-start(f32[96,1024]{1,0:T(8,128)S(1)} %pad_maximum_fusion.4), channel_id=1, source_target_pairs={{0,12},{2,34},{4,8},{6,38},{8,4},{10,42},{12,0},{14,46},{32,44},{3... | collective-permute-start | bytes 1179656 | tf_op jit(solution)/shard_map/ppermute | solution.py:748
  40.4 9.7 %collective-permute-start.5 = (f32[192,512]{1,0:T(8,128)}, f32[192,512]{1,0:T(8,128)S(1)}, u32[]{:S(2)}, u32[]{:S(2)}) collective-permute-start(f32[192,512]{1,0:T(8,128)} %get-tuple-element.71.refs_0_), channel_id=1, source_target_pairs={{0,4},{2,98},{4,0},{6,102},{8,12},{10,106},{12,8},{14,110},{32,36}... | collective-permute-start | bytes 1179656 | tf_op jit(solution)/shard_map/ppermute | solution.py:756
  40.7 9.4 %collective-permute-start.6 = (f32[192,512]{1,0:T(8,128)}, f32[192,512]{1,0:T(8,128)S(1)}, u32[]{:S(2)}, u32[]{:S(2)}) collective-permute-start(f32[192,512]{1,0:T(8,128)} %get-tuple-element.72.refs_1_), channel_id=1, source_target_pairs={{0,32},{2,14},{4,36},{6,10},{8,40},{10,6},{12,44},{14,2},{32,0},{3... | collective-permute-start | bytes 1179656 | tf_op jit(solution)/shard_map/ppermute | solution.py:756
  50.2 4.7 %copy-start.17 = (f32[256,1024]{1,0:T(8,128)S(1)}, f32[256,1024]{1,0:T(8,128)}, u32[]{:S(2)}) copy-start(f32[256,1024]{1,0:T(8,128)} %get-tuple-element.70.refs_2_.refs_1_) | copy-start | bytes 3145732
  52.3 28.6 %copy-start.21 = (f32[384,512]{1,0:T(8,128)}, f32[384,512]{1,0:T(8,128)S(1)}, u32[]{:S(2)}) copy-start(f32[384,512]{1,0:T(8,128)S(1)} %constant_dynamic-update-slice_fusion.refs_13_) | copy-start | bytes 2359300
  52.3 12.2 %collective-permute-start.7 = (f32[384,512]{1,0:T(8,128)S(1)}, f32[384,512]{1,0:T(8,128)}, u32[]{:S(2)}, u32[]{:S(2)}) collective-permute-start(f32[384,512]{1,0:T(8,128)S(1)} %constant_dynamic-update-slice_fusion.refs_13_), channel_id=1, source_target_pairs={{0,32},{2,14},{4,36},{6,10},{8,40},{10,6},{12,44},{14,2},{32,0},{3... | collective-permute-start | bytes 2359304 | tf_op jit(solution)/shard_map/ppermute | solution.py:756
  53.0 27.9 %copy-start.20 = (f32[384,512]{1,0:T(8,128)}, f32[384,512]{1,0:T(8,128)S(1)}, u32[]{:S(2)}) copy-start(f32[384,512]{1,0:T(8,128)S(1)} %constant_dynamic-update-slice_fusion.2.refs_14_) | copy-start | bytes 2359300
  53.0 12.8 %collective-permute-start.8 = (f32[384,512]{1,0:T(8,128)S(1)}, f32[384,512]{1,0:T(8,128)S(1)}, u32[]{:S(2)}, u32[]{:S(2)}) collective-permute-start(f32[384,512]{1,0:T(8,128)S(1)} %constant_dynamic-update-slice_fusion.2.refs_14_), channel_id=1, source_target_pairs={{0,4},{2,98},{4,0},{6,102},{8,12},{10,106},{12,8},{14,110},{32,36}... | collective-permute-start | bytes 2359304 | tf_op jit(solution)/shard_map/ppermute | solution.py:756
  54.8 26.0 %collective-permute-start.1 = (f32[256,1024]{1,0:T(8,128)S(1)}, f32[256,1024]{1,0:T(8,128)}, u32[]{:S(2)}, u32[]{:S(2)}) collective-permute-start(f32[256,1024]{1,0:T(8,128)S(1)} %copy-done.17), channel_id=1, source_target_pairs={{0,1},{1,0},{2,3},{3,2},{4,5},{5,4},{6,7},{7,6},{8,9},{9,8},{10,11... | collective-permute-start | bytes 3145736 | tf_op jit(solution)/shard_map/ppermute | solution.py:667
  55.3 25.6 %collective-permute-start.9 = (f32[384,512]{1,0:T(8,128)S(1)}, f32[384,512]{1,0:T(8,128)}, u32[]{:S(2)}, u32[]{:S(2)}) collective-permute-start(f32[384,512]{1,0:T(8,128)S(1)} %constant_dynamic-update-slice_fusion.refs_13_), channel_id=1, source_target_pairs={{0,2},{2,0},{1,3},{3,1},{4,6},{6,4},{5,7},{7,5},{8,10},{10,8},{9,1... | collective-permute-start | bytes 2359304 | tf_op jit(solution)/shard_map/ppermute | solution.py:764
  56.1 24.7 %collective-permute-start.10 = (f32[384,512]{1,0:T(8,128)S(1)}, f32[384,512]{1,0:T(8,128)}, u32[]{:S(2)}, u32[]{:S(2)}) collective-permute-start(f32[384,512]{1,0:T(8,128)S(1)} %constant_dynamic-update-slice_fusion.2.refs_14_), channel_id=1, source_target_pairs={{0,2},{2,0},{1,3},{3,1},{4,6},{6,4},{5,7},{7,5},{8,10},{10,8},{9,1... | collective-permute-start | bytes 2359304 | tf_op jit(solution)/shard_map/ppermute | solution.py:764
  64.5 16.4 %collective-permute-start.11 = (f32[384,512]{1,0:T(8,128)}, f32[384,512]{1,0:T(8,128)}, u32[]{:S(2)}, u32[]{:S(2)}) collective-permute-start(f32[384,512]{1,0:T(8,128)} %collective-permute-done.7.refs_15_), channel_id=1, source_target_pairs={{0,2},{2,0},{1,3},{3,1},{4,6},{6,4},{5,7},{7,5},{8,10},{10,8},{9,1... | collective-permute-start | bytes 2359304 | tf_op jit(solution)/shard_map/ppermute | solution.py:764
  65.8 15.1 %copy-start.27 = (f32[384,512]{1,0:T(8,128)}, f32[384,512]{1,0:T(8,128)S(1)}, u32[]{:S(2)}) copy-start(f32[384,512]{1,0:T(8,128)S(1)} %collective-permute-done.8.refs_16_) | copy-start | bytes 2359300
  65.8 15.1 %collective-permute-start.12 = (f32[384,512]{1,0:T(8,128)S(1)}, f32[384,512]{1,0:T(8,128)}, u32[]{:S(2)}, u32[]{:S(2)}) collective-permute-start(f32[384,512]{1,0:T(8,128)S(1)} %collective-permute-done.8.refs_16_), channel_id=1, source_target_pairs={{0,2},{2,0},{1,3},{3,1},{4,6},{6,4},{5,7},{7,5},{8,10},{10,8},{9,1... | collective-permute-start | bytes 2359304 | tf_op jit(solution)/shard_map/ppermute | solution.py:764
  111.8 10.6 %collective-permute-start.13 = (f32[512,3072]{1,0:T(8,128)}, f32[512,3072]{1,0:T(8,128)}, u32[]{:S(2)}, u32[]{:S(2)}) collective-permute-start(f32[512,3072]{1,0:T(8,128)} %get-tuple-element.80), channel_id=1, source_target_pairs={{0,2},{2,0},{1,3},{3,1},{4,6},{6,4},{5,7},{7,5},{8,10},{10,8},{9,1... | collective-permute-start | bytes 18874376 | tf_op jit(solution)/shard_map/ppermute | solution.py:688
  112.0 26.3 %collective-permute-start.14 = (f32[256,1024]{1,0:T(8,128)}, f32[256,1024]{1,0:T(8,128)}, u32[]{:S(2)}, u32[]{:S(2)}) collective-permute-start(f32[256,1024]{1,0:T(8,128)} %get-tuple-element.82.own), channel_id=1, source_target_pairs={{0,1},{1,0},{2,3},{3,2},{4,5},{5,4},{6,7},{7,6},{8,9},{9,8},{10,11... | collective-permute-start | bytes 3145736 | tf_op jit(solution)/shard_map/ppermute | solution.py:667
  113.6 27.1 %collective-permute-start.16 = (f32[256,128]{1,0:T(8,128)}, f32[256,128]{1,0:T(8,128)S(1)}, u32[]{:S(2)}, u32[]{:S(2)}) collective-permute-start(f32[256,128]{1,0:T(8,128)} %get-tuple-element.84.gate_own), channel_id=1, source_target_pairs={{0,1},{1,0},{2,3},{3,2},{4,5},{5,4},{6,7},{7,6},{8,9},{9,8},{10,11... | collective-permute-start | bytes 393224 | tf_op jit(solution)/shard_map/ppermute | solution.py:667
  138.2 30.1 %collective-permute-start.15 = (f32[256,1024]{1,0:T(8,128)}, f32[256,1024]{1,0:T(8,128)}, u32[]{:S(2)}, u32[]{:S(2)}) collective-permute-start(f32[256,1024]{1,0:T(8,128)} %get-tuple-element.83), channel_id=1, source_target_pairs={{0,1},{1,0},{2,3},{3,2},{4,5},{5,4},{6,7},{7,6},{8,9},{9,8},{10,11... | collective-permute-start | bytes 3145736 | tf_op jit(solution)/shard_map/ppermute | solution.py:667
  138.6 24.2 %collective-permute-start.17 = (f32[256,1536]{1,0:T(8,128)}, f32[256,1536]{1,0:T(8,128)}, u32[]{:S(2)}, u32[]{:S(2)}) collective-permute-start(f32[256,1536]{1,0:T(8,128)} %get-tuple-element.96.rest_4_), channel_id=1, source_target_pairs={{0,32},{2,14},{4,36},{6,10},{8,40},{10,6},{12,44},{14,2},{32,0},{3... | collective-permute-start | bytes 4718600 | tf_op jit(solution)/shard_map/ppermute | solution.py:704
  139.5 26.1 %collective-permute-start.18 = (f32[256,1536]{1,0:T(8,128)}, f32[256,1536]{1,0:T(8,128)}, u32[]{:S(2)}, u32[]{:S(2)}) collective-permute-start(f32[256,1536]{1,0:T(8,128)} %get-tuple-element.97.rest_5_), channel_id=1, source_target_pairs={{0,4},{2,98},{4,0},{6,102},{8,12},{10,106},{12,8},{14,110},{32,36}... | collective-permute-start | bytes 4718600 | tf_op jit(solution)/shard_map/ppermute | solution.py:704
  168.3 15.2 %copy-start.6 = (f32[256,1024]{1,0:T(8,128)S(1)}, f32[256,1024]{1,0:T(8,128)}, u32[]{:S(2)}) copy-start(f32[256,1024]{1,0:T(8,128)} %get-tuple-element.83) | copy-start | bytes 3145732
  168.3 15.2 %copy-start.16 = (f32[256,1024]{1,0:T(8,128)S(1)}, f32[256,1024]{1,0:T(8,128)}, u32[]{:S(2)}) copy-start(f32[256,1024]{1,0:T(8,128)} %get-tuple-element.78.middle) | copy-start | bytes 3145732
  182.0 21.2 %collective-permute-start.22 = (f32[512,3072]{1,0:T(8,128)}, f32[512,3072]{1,0:T(8,128)}, u32[]{:S(2)}, u32[]{:S(2)}) collective-permute-start(f32[512,3072]{1,0:T(8,128)} %get-tuple-element.117), channel_id=1, source_target_pairs={{0,2},{2,0},{1,3},{3,1},{4,6},{6,4},{5,7},{7,5},{8,10},{10,8},{9,1... | collective-permute-start | bytes 18874376 | tf_op jit(solution)/shard_map/ppermute | solution.py:688
  182.8 15.0 %collective-permute-start.21 = (f32[512,1664]{1,0:T(8,128)}, f32[512,1664]{1,0:T(8,128)}, u32[]{:S(2)}, u32[]{:S(2)}) collective-permute-start(f32[512,1664]{1,0:T(8,128)} %get-tuple-element.115), channel_id=1, source_target_pairs={{0,2},{2,0},{1,3},{3,1},{4,6},{6,4},{5,7},{7,5},{8,10},{10,8},{9,1... | collective-permute-start | bytes 10223624 | tf_op jit(solution)/shard_map/ppermute | solution.py:688
  183.5 15.9 %copy-start.11 = (f32[512,1664]{1,0:T(8,128)S(1)}, f32[512,1664]{1,0:T(8,128)}, u32[]{:S(2)}) copy-start(f32[512,1664]{1,0:T(8,128)} %get-tuple-element.114) | copy-start | bytes 10223620
  183.5 20.7 %slice-start = ((s8[6291456]{0:T(1024)(128)(4,1)}), s8[4194304]{0:T(1024)(128)(4,1)S(1)}, s32[]{:S(2)}) async-start(s8[6291456]{0:T(1024)(128)(4,1)} %bitcast.53), calls=%async_computation | async-start | bytes 8388608
  185.9 31.7 %collective-permute-start.23 = (f32[128,1536]{1,0:T(8,128)}, f32[128,1536]{1,0:T(8,128)}, u32[]{:S(2)}, u32[]{:S(2)}) collective-permute-start(f32[128,1536]{1,0:T(8,128)} %get-tuple-element.195.rest_0_), channel_id=1, source_target_pairs={{0,4},{2,98},{4,0},{6,102},{8,12},{10,106},{12,8},{14,110},{32,36}... | collective-permute-start | bytes 2359304 | tf_op jit(solution)/shard_map/ppermute | solution.py:704
  187.2 31.4 %collective-permute-start.24 = (f32[128,1536]{1,0:T(8,128)}, f32[128,1536]{1,0:T(8,128)}, u32[]{:S(2)}, u32[]{:S(2)}) collective-permute-start(f32[128,1536]{1,0:T(8,128)} %get-tuple-element.201.rest_1_), channel_id=1, source_target_pairs={{0,32},{2,14},{4,36},{6,10},{8,40},{10,6},{12,44},{14,2},{32,0},{3... | collective-permute-start | bytes 2359304 | tf_op jit(solution)/shard_map/ppermute | solution.py:704
  188.1 30.5 %collective-permute-start.19 = (f32[256,1024]{1,0:T(8,128)}, f32[256,1024]{1,0:T(8,128)}, u32[]{:S(2)}, u32[]{:S(2)}) collective-permute-start(f32[256,1024]{1,0:T(8,128)} %get-tuple-element.106.own), channel_id=1, source_target_pairs={{0,1},{1,0},{2,3},{3,2},{4,5},{5,4},{6,7},{7,6},{8,9},{9,8},{10,11... | collective-permute-start | bytes 3145736 | tf_op jit(solution)/shard_map/ppermute | solution.py:667
  197.8 19.0 %collective-permute-start.20 = (f32[256,128]{1,0:T(8,128)}, f32[256,128]{1,0:T(8,128)S(1)}, u32[]{:S(2)}, u32[]{:S(2)}) collective-permute-start(f32[256,128]{1,0:T(8,128)} %get-tuple-element.107.gate_own), channel_id=1, source_target_pairs={{0,1},{1,0},{2,3},{3,2},{4,5},{5,4},{6,7},{7,6},{8,9},{9,8},{10,11... | collective-permute-start | bytes 393224 | tf_op jit(solution)/shard_map/ppermute | solution.py:667
  199.4 4.8 %slice-start.1 = ((s8[6291456]{0:T(1024)(128)(4,1)}), s8[2097152]{0:T(1024)(128)(4,1)S(1)}, s32[]{:S(2)}) async-start(s8[6291456]{0:T(1024)(128)(4,1)} %bitcast.53), calls=%async_computation.1 | async-start | bytes 4194304
  203.2 30.4 %collective-permute-start.26 = (f32[256,1664]{1,0:T(8,128)}, f32[256,1664]{1,0:T(8,128)S(1)}, u32[]{:S(2)}, u32[]{:S(2)}) collective-permute-start(f32[256,1664]{1,0:T(8,128)} %get-tuple-element.181.rest_0_), channel_id=1, source_target_pairs={{0,96},{2,6},{4,100},{6,2},{8,104},{10,14},{12,108},{14,10},{32,64... | collective-permute-start | bytes 5111816 | tf_op jit(solution)/shard_map/ppermute | solution.py:704
  216.8 20.7 %collective-permute-start.27 = (f32[256,1536]{1,0:T(8,128)}, f32[256,1536]{1,0:T(8,128)}, u32[]{:S(2)}, u32[]{:S(2)}) collective-permute-start(f32[256,1536]{1,0:T(8,128)} %get-tuple-element.175.rest_1_), channel_id=1, source_target_pairs={{0,32},{2,14},{4,36},{6,10},{8,40},{10,6},{12,44},{14,2},{32,0},{3... | collective-permute-start | bytes 4718600 | tf_op jit(solution)/shard_map/ppermute | solution.py:704
  217.6 23.6 %collective-permute-start.28 = (f32[256,1536]{1,0:T(8,128)}, f32[256,1536]{1,0:T(8,128)}, u32[]{:S(2)}, u32[]{:S(2)}) collective-permute-start(f32[256,1536]{1,0:T(8,128)} %get-tuple-element.174.rest_2_), channel_id=1, source_target_pairs={{0,4},{2,98},{4,0},{6,102},{8,12},{10,106},{12,8},{14,110},{32,36}... | collective-permute-start | bytes 4718600 | tf_op jit(solution)/shard_map/ppermute | solution.py:704
  233.6 7.7 %copy-start.3 = (f32[256,1664]{1,0:T(8,128)}, f32[256,1664]{1,0:T(8,128)S(1)}, u32[]{:S(2)}) copy-start(f32[256,1664]{1,0:T(8,128)S(1)} %collective-permute-done.26.refs_1_) | copy-start | bytes 5111812
  241.3 29.9 %collective-permute-start.29 = (f32[512,1664]{1,0:T(8,128)}, f32[512,1664]{1,0:T(8,128)S(1)}, u32[]{:S(2)}, u32[]{:S(2)}) collective-permute-start(f32[512,1664]{1,0:T(8,128)} %behind.10), channel_id=1, source_target_pairs={{0,2},{2,0},{1,3},{3,1},{4,6},{6,4},{5,7},{7,5},{8,10},{10,8},{9,1... | collective-permute-start | bytes 10223624 | tf_op jit(solution)/shard_map/ppermute | solution.py:688
  245.4 19.5 %collective-permute-start.40 = (f32[128,1536]{1,0:T(8,128)S(1)}, f32[128,1536]{1,0:T(8,128)S(1)}, u32[]{:S(2)}, u32[]{:S(2)}) collective-permute-start(f32[128,1536]{1,0:T(8,128)S(1)} %get-tuple-element.199), channel_id=1, source_target_pairs={{0,32},{2,14},{4,36},{6,10},{8,40},{10,6},{12,44},{14,2},{32,0},{3... | collective-permute-start | bytes 2359304 | tf_op jit(solution)/shard_map/ppermute | solution.py:704
  245.8 75.8 %collective-permute-start.32 = (f32[128,1664]{1,0:T(8,128)S(1)}, f32[128,1664]{1,0:T(8,128)S(1)}, u32[]{:S(2)}, u32[]{:S(2)}) collective-permute-start(f32[128,1664]{1,0:T(8,128)S(1)} %get-tuple-element.189), channel_id=1, source_target_pairs={{0,12},{2,34},{4,8},{6,38},{8,4},{10,42},{12,0},{14,46},{32,44},{3... | collective-permute-start | bytes 2555912 | tf_op jit(solution)/shard_map/ppermute | solution.py:704
  247.9 78.3 %collective-permute-start.25 = (f32[256,1024]{1,0:T(8,128)S(1)}, f32[256,1024]{1,0:T(8,128)S(1)}, u32[]{:S(2)}, u32[]{:S(2)}) collective-permute-start(f32[256,1024]{1,0:T(8,128)S(1)} %copy-done.8), channel_id=1, source_target_pairs={{0,1},{1,0},{2,3},{3,2},{4,5},{5,4},{6,7},{7,6},{8,9},{9,8},{10,11... | collective-permute-start | bytes 3145736 | tf_op jit(solution)/shard_map/ppermute | solution.py:667
  249.9 16.3 %copy-start.13 = (f32[128,1536]{1,0:T(8,128)S(1)}, f32[128,1536]{1,0:T(8,128)}, u32[]{:S(2)}) copy-start(f32[128,1536]{1,0:T(8,128)} %get-tuple-element.200) | copy-start | bytes 2359300
  249.9 19.2 %collective-permute-start.37 = (f32[128,1536]{1,0:T(8,128)S(1)}, f32[128,1536]{1,0:T(8,128)S(1)}, u32[]{:S(2)}, u32[]{:S(2)}) collective-permute-start(f32[128,1536]{1,0:T(8,128)S(1)} %get-tuple-element.193), channel_id=1, source_target_pairs={{0,4},{2,98},{4,0},{6,102},{8,12},{10,106},{12,8},{14,110},{32,36}... | collective-permute-start | bytes 2359304 | tf_op jit(solution)/shard_map/ppermute | solution.py:704
  266.4 4.0 %copy-start.12 = (f32[128,1536]{1,0:T(8,128)S(1)}, f32[128,1536]{1,0:T(8,128)}, u32[]{:S(2)}) copy-start(f32[128,1536]{1,0:T(8,128)} %get-tuple-element.194) | copy-start | bytes 2359300
  266.4 13.3 %collective-permute-start.41 = (f32[64,3072]{1,0:T(8,128)S(1)}, f32[64,3072]{1,0:T(8,128)S(1)}, u32[]{:S(2)}, u32[]{:S(2)}) collective-permute-start(f32[64,3072]{1,0:T(8,128)S(1)} %get-tuple-element.197), channel_id=1, source_target_pairs={{0,12},{2,34},{4,8},{6,38},{8,4},{10,42},{12,0},{14,46},{32,44},{3... | collective-permute-start | bytes 2359304 | tf_op jit(solution)/shard_map/ppermute | solution.py:704
  270.6 17.5 %collective-permute-start.38 = (f32[64,3072]{1,0:T(8,128)S(1)}, f32[64,3072]{1,0:T(8,128)S(1)}, u32[]{:S(2)}, u32[]{:S(2)}) collective-permute-start(f32[64,3072]{1,0:T(8,128)S(1)} %get-tuple-element.191), channel_id=1, source_target_pairs={{0,12},{2,34},{4,8},{6,38},{8,4},{10,42},{12,0},{14,46},{32,44},{3... | collective-permute-start | bytes 2359304 | tf_op jit(solution)/shard_map/ppermute | solution.py:704
  272.7 33.6 %collective-permute-start.30 = (f32[256,1664]{1,0:T(8,128)S(1)}, f32[256,1664]{1,0:T(8,128)S(1)}, u32[]{:S(2)}, u32[]{:S(2)}) collective-permute-start(f32[256,1664]{1,0:T(8,128)S(1)} %get-tuple-element.183), channel_id=1, source_target_pairs={{0,12},{2,34},{4,8},{6,38},{8,4},{10,42},{12,0},{14,46},{32,44},{3... | collective-permute-start | bytes 5111816 | tf_op jit(solution)/shard_map/ppermute | solution.py:704
  279.7 10.1 %collective-permute-start.42 = (f32[32,3072]{1,0:T(8,128)S(1)}, f32[32,3072]{1,0:T(8,128)S(1)}, u32[]{:S(2)}, u32[]{:S(2)}) collective-permute-start(f32[32,3072]{1,0:T(8,128)S(1)} %get-tuple-element.213), channel_id=1, source_target_pairs={{0,96},{2,6},{4,100},{6,2},{8,104},{10,14},{12,108},{14,10},{32,64... | collective-permute-start | bytes 1179656 | tf_op jit(solution)/shard_map/ppermute | solution.py:704
  288.2 21.2 %collective-permute-start.39 = (f32[32,3072]{1,0:T(8,128)S(1)}, f32[32,3072]{1,0:T(8,128)S(1)}, u32[]{:S(2)}, u32[]{:S(2)}) collective-permute-start(f32[32,3072]{1,0:T(8,128)S(1)} %get-tuple-element.211), channel_id=1, source_target_pairs={{0,96},{2,6},{4,100},{6,2},{8,104},{10,14},{12,108},{14,10},{32,64... | collective-permute-start | bytes 1179656 | tf_op jit(solution)/shard_map/ppermute | solution.py:704
  307.5 14.1 %collective-permute-start.31 = (f32[128,1664]{1,0:T(8,128)S(1)}, f32[128,1664]{1,0:T(8,128)S(1)}, u32[]{:S(2)}, u32[]{:S(2)}) collective-permute-start(f32[128,1664]{1,0:T(8,128)S(1)} %get-tuple-element.187), channel_id=1, source_target_pairs={{0,96},{2,6},{4,100},{6,2},{8,104},{10,14},{12,108},{14,10},{32,64... | collective-permute-start | bytes 2555912 | tf_op jit(solution)/shard_map/ppermute | solution.py:704
  309.5 13.8 %collective-permute-start.43 = (f32[16,6144]{1,0:T(8,128)S(1)}, f32[16,6144]{1,0:T(8,128)S(1)}, u32[]{:S(2)}, u32[]{:S(2)}) collective-permute-start(f32[16,6144]{1,0:T(8,128)S(1)} %pad_maximum_fusion.5), channel_id=1, source_target_pairs={{0,16},{16,0},{1,17},{17,1},{2,18},{18,2},{3,19},{19,3},{4,20},{20... | collective-permute-start | bytes 1179656 | tf_op jit(solution)/shard_map/ppermute | solution.py:725
  323.2 13.0 %collective-permute-start.33 = (f32[64,3328]{1,0:T(8,128)}, f32[64,3328]{1,0:T(8,128)}, u32[]{:S(2)}, u32[]{:S(2)}) collective-permute-start(f32[64,3328]{1,0:T(8,128)} %get-tuple-element.185), channel_id=1, source_target_pairs={{0,32},{2,14},{4,36},{6,10},{8,40},{10,6},{12,44},{14,2},{32,0},{3... | collective-permute-start | bytes 2555912 | tf_op jit(solution)/shard_map/ppermute | solution.py:704
  327.7 8.5 %copy-start.9 = (f32[64,3328]{1,0:T(8,128)S(1)}, f32[64,3328]{1,0:T(8,128)}, u32[]{:S(2)}) copy-start(f32[64,3328]{1,0:T(8,128)} %get-tuple-element.184) | copy-start | bytes 2555908
  336.2 12.8 %copy-start.1 = (f32[256,1024]{1,0:T(8,128)S(1)}, f32[256,1024]{1,0:T(8,128)}, u32[]{:S(2)}) copy-start(f32[256,1024]{1,0:T(8,128)} %behind.11) | copy-start | bytes 3145732
  336.2 12.8 %copy-start.19 = (f32[256,1024]{1,0:T(8,128)S(1)}, f32[256,1024]{1,0:T(8,128)}, u32[]{:S(2)}) copy-start(f32[256,1024]{1,0:T(8,128)} %get-tuple-element.118) | copy-start | bytes 3145732
  337.6 8.2 %collective-permute-start.34 = (f32[32,3328]{1,0:T(8,128)S(1)}, f32[32,3328]{1,0:T(8,128)S(1)}, u32[]{:S(2)}, u32[]{:S(2)}) collective-permute-start(f32[32,3328]{1,0:T(8,128)S(1)} %get-tuple-element.209), channel_id=1, source_target_pairs={{0,4},{2,98},{4,0},{6,102},{8,12},{10,106},{12,8},{14,110},{32,36}... | collective-permute-start | bytes 1277960 | tf_op jit(solution)/shard_map/ppermute | solution.py:704
  345.9 7.4 %collective-permute-start.35 = (f32[16,3328]{1,0:T(8,128)S(1)}, f32[16,3328]{1,0:T(8,128)S(1)}, u32[]{:S(2)}, u32[]{:S(2)}) collective-permute-start(f32[16,3328]{1,0:T(8,128)S(1)} %slice_add_fusion.33), channel_id=1, source_target_pairs={{0,16},{16,0},{1,17},{17,1},{2,18},{18,2},{3,19},{19,3},{4,20},{20... | collective-permute-start | bytes 638984 | tf_op jit(solution)/shard_map/ppermute | solution.py:725
  355.1 3.7 %collective-permute-start.36 = (f32[2,16]{1,0:T(2,128)S(1)}, f32[2,16]{1,0:T(2,128)S(1)}, u32[]{:S(2)}, u32[]{:S(2)}) collective-permute-start(f32[2,16]{1,0:T(2,128)S(1)} %bitcast.66), channel_id=1, source_target_pairs={{0,1},{1,0},{2,3},{3,2},{4,5},{5,4},{6,7},{7,6},{8,9},{9,8},{10,11... | collective-permute-start | bytes 392 | tf_op jit(solution)/shard_map/ppermute | solution.py:667
  (16 other events, 26.8 us)
where the time goes:
time: 367 us; the launch traced here: 360 us
  waiting for transfers between devices  142 us (39%)
  Pallas kernels  95.6 us (26%)
  starting transfers between devices  53.9 us (15%)
  other arithmetic  39.9 us (11%)
  local copies, waits for them, and re-layouts  27.1 us (7%)
    ppermute x18, waiting for transfers between devices, move(): lax.ppermute(send, RING_AXES, ring_pairs(orders, self.step))  73.8 us
    pallas_call x2, Pallas kernels, attention_backward(): pl.pallas_call(functools.partial(attention_backward_kernel, len(after), b...  36.6 us
    pallas_call x3, Pallas kernels, run_experts(): pl.pallas_call(kernel, grid=(STREAMS,), in_specs=in_specs, out_specs=[spe...  36.3 us
    ppermute x10, waiting for transfers between devices, exchange(): return lax.ppermute(array, 'tensor', SWAP)  34.4 us
    add x18, other arithmetic, halve(): self.kept = [first[:half] + second[:half] for first, second in self.parts]  31.3 us
    pallas_call x2, Pallas kernels, attention_forward(): pl.pallas_call(functools.partial(attention_forward_kernel, len(parts), bo...  22.7 us
    ppermute x18, starting transfers between devices, move(): lax.ppermute(send, RING_AXES, ring_pairs(orders, self.step))  19.9 us
    ppermute x4, waiting for transfers between devices, __init__(): received = lax.ppermute(send, 'dp_3', SWAP)  15.2 us
  transfers between devices with their start and end apart: 44, of which 20 were waited for; matrix products, arithmetic and copies ran while one was open for 15% of the time, Pallas kernels for 14%

commit v1 on v0

--- a/solution.py
+++ b/solution.py
@@ -36,6 +36,10 @@
     return (order[1], order[0], *order[2:])
 
 
+def crossed(orders):
+    return tuple((order[1], order[0], order[3], order[2]) for order in orders)
+
+
 def pair_bit(index, kind):
     high = index // 2
     if kind == "v":
@@ -116,8 +120,8 @@
     for block in range(32):
         x, yh, z = block // 8, (block // 4) % 2, block % 4
         one, two = (
-            jnp.where(later, place(swapped(order), x, yh, z), place(order, x, yh, z))
-            for order in orders
+            jnp.where(later, place(second, x, yh, z), place(first, x, yh, z))
+            for first, second in zip(orders, crossed(orders))
         )
         own = jnp.where(later, places[2], places[0])
         far = jnp.where(later, places[3], places[1])
@@ -355,7 +359,7 @@
 
 def expert_both_kernel(
     places, x, own, other, gain, router, mask, wg, wu, wd, cotangent,
-    middle_out, xi_out, share_out, part_out, back_out, gate_grad_out, keep, send,
+    middle_out, xi_out, share_out, part_out, back_out, keep, send,
 ):
     expert = pl.program_id(0)
     lane = lane_of(share_out.shape[0])
@@ -365,7 +369,6 @@
         expert_prologue(x, own, other, gain, router, mask, middle_out, xi_out, share_out)
         part_out[...] = jnp.zeros_like(part_out)
         back_out[...] = jnp.zeros_like(back_out)
-        gate_grad_out[...] = jnp.zeros_like(gate_grad_out)
 
     share = column_of(share_out[...], lane, expert)
     xi = xi_out[...]
@@ -376,15 +379,15 @@
         wd[...], keep, send,
     )
     part_out[...] += share * expert_out
-    back_out[...] += back
-    gate_grad_out[...] += jnp.where(lane == expert, gate_grad, 0.0)
+    back_out[:, : back.shape[1]] += back
+    back_out[:, back.shape[1] :] += jnp.where(lane == expert, gate_grad, 0.0)
 
 
 def expert_backward_kernel(
     places, g_in, x, gain, own, other, xi_ref, share_ref, gate_ref, linear_ref, wg, wu, wd,
     *rest,
 ):
-    g_out, gain_out, back_out, gate_grad_out, keep, send = rest[-6:]
+    g_out, gain_out, back_out, keep, send = rest[-5:]
     expert = pl.program_id(0)
     lane = lane_of(share_ref.shape[0])
 
@@ -397,15 +400,14 @@
         g_out[...] = g_in[...] + change
         gain_out[...] = jnp.broadcast_to(gain_row, gain_out.shape)
         back_out[...] = jnp.zeros_like(back_out)
-        gate_grad_out[...] = jnp.zeros_like(gate_grad_out)
 
     share = column_of(share_ref[...], lane, expert)
     gate_grad, back, _ = expert_backward_step(
         places, g_out[...], xi_ref[...], share, gate_ref[...], linear_ref[...], wg[...],
         wu[...], wd[...], keep, send,
     )
-    back_out[...] += back
-    gate_grad_out[...] += jnp.where(lane == expert, gate_grad, 0.0)
+    back_out[:, : back.shape[1]] += back
+    back_out[:, back.shape[1] :] += jnp.where(lane == expert, gate_grad, 0.0)
 
 
 def of_expert(layer, shape):
@@ -414,6 +416,11 @@
 
 def each_expert(shape):
     return pl.BlockSpec((None, *shape), lambda e: (e, 0, 0))
+
+
+def with_gates(length, features):
+    shape = (length, features + LANES)
+    return whole(shape), (shape, F32)
 
 
 def gradient_outs(rows, width):
@@ -478,8 +485,7 @@
         (whole(low[0]), low),
         table,
         (whole(big[0]), big),
-        (whole(big[0]), big),
-        table,
+        with_gates(length, features),
         *gradient_outs(features // 2, width),
     ]
     return run_experts(
@@ -493,7 +499,6 @@
     length, features = x.shape
     width = wg.shape[3]
     big = ((length, features), F32)
-    table = (whole((length, LANES)), ((length, LANES), F32))
     hidden = each_expert((length, width))
     ins = [places, g, x, gain, own, other, xi, share, gate_in, linear, wg, wu, wd, *after]
     in_specs = [SMEM, whole(x.shape), whole(x.shape)] + [
@@ -510,8 +515,7 @@
     outs = [
         (whole(big[0]), big),
         (whole((8, features)), ((8, features), F32)),
-        (whole(big[0]), big),
-        table,
+        with_gates(length, features),
         *gradient_outs(features // 2, width),
     ]
     return run_experts(
@@ -555,7 +559,7 @@
 
 
 def attention_backward_kernel(
-    count, full, orders, places, g, own, other, gate_own, gate_other, middle, xi, share, gain, router_rows,
+    count, full, places, g, own, other, middle, xi, share, gain, router_rows,
     wo, mix, q, kk, vv, a, wq, wk, wv, cos, sin, seg_row, seg_column, x, late_gain, *rest,
 ):
     if full:
@@ -564,13 +568,14 @@
         rest = rest[4:]
     g_out, part_out, keep, send = rest[count : count + 4]
     rows_scratch = rest[-1]
-    where_to = block_places(orders, places)
+    first, second = (block_places(ATTENTION_ORDERS, places, later) for later in (False, True))
     length = middle.shape[0]
     lane = lane_of(length)
     shares = share[...]
-    gate_grad = gate_own[...] + gate_other[...]
+    features = middle.shape[1]
+    gate_grad = own[:, features:] + other[:, features:]
     pick = shares * (gate_grad - jnp.sum(shares * gate_grad, axis=1, keepdims=True))
-    input_grad = own[...] + other[...]
+    input_grad = own[:, :features] + other[:, :features]
     xi_full = xi[...].astype(F32)
     rows_scratch[...] = jnp.zeros_like(rows_scratch)
     for expert in range(STREAMS):
@@ -607,18 +612,21 @@
     )
     a_full = a[...]
     column = 0
-    for total in (
-        jnp.transpose(rows_scratch[...]),
-        *(mm_tn(a_full, grad) for grad in grads),
-        mm_tn(output_grad, mix[...]),
+    query_grad, key_grad, value_grad = grads
+    for total, where_to in (
+        (jnp.transpose(rows_scratch[...]), first),
+        (mm_tn(a_full, query_grad), first),
+        (mm_tn(a_full, key_grad), first),
+        (mm_tn(a_full, value_grad), second),
+        (mm_tn(output_grad, mix[...]), second),
     ):
         store_blocks(keep, send, total, column, where_to)
         column += total.shape[1]
 
 
 def attention_backward(
-    layer, orders, places, g, own, other, gate_own, gate_other, saved_experts, weights, saved,
-    tables, segment, late_gain, after, others=(),
+    layer, places, g, own, other, saved_experts, weights, saved, tables, segment, late_gain, after,
+    others=(),
 ):
     middle, xi, share = saved_experts
     gain, router_rows, wo, wq, wk, wv = weights
@@ -626,10 +634,10 @@
     length, features = middle.shape
     columns = SMALL + wq.shape[2] + wk.shape[2] + wv.shape[2] + wo.shape[1]
     ins = [
-        places, g, own, other, gate_own, gate_other, middle, xi, share, gain, router_rows,
-        wo, mix, q, kk, vv, a, wq, wk, wv, *tables, *segment, x, late_gain,
+        places, g, own, other, middle, xi, share, gain, router_rows, wo,
+        mix, q, kk, vv, a, wq, wk, wv, *tables, *segment, x, late_gain,
     ]
-    layered = {9, 10, 11, 17, 18, 19}
+    layered = {7, 8, 9, 15, 16, 17}
     in_specs = [SMEM]
     for at, array in enumerate(ins[1:], 1):
         in_specs.append(of_layer(layer, array.shape[1:]) if at in layered else whole(array.shape))
@@ -646,7 +654,7 @@
         outs.append(((length, features), F32))
     return pl.pallas_call(
         functools.partial(
-            attention_backward_kernel, len(after), bool(others), orders
+            attention_backward_kernel, len(after), bool(others)
         ),
         grid=(1,),
         in_specs=in_specs,
@@ -684,13 +692,12 @@
 
 
 class Scatter:
-    def __init__(self, keep, send, *orders):
+    def __init__(self, keep, send, orders, column):
         received = lax.ppermute(send, "dp_3", SWAP)
-        width = keep.shape[1] // len(orders)
-        self.orders = orders
+        self.orders = (orders, crossed(orders))
         self.parts = [
-            [array[:, at * width : (at + 1) * width] for array in (keep, received)]
-            for at in range(len(orders))
+            [array[:, :column] for array in (keep, received)],
+            [array[:, column:] for array in (keep, received)],
         ]
         self.step = 0
 
@@ -709,6 +716,10 @@
 
     def received(self):
         return [second for _, second in self.parts]
+
+    def hold(self, *after):
+        for pair, second in zip(self.parts, behind(self.received(), *after)):
+            pair[1] = second
 
     def advance(self, count=1):
         for _ in range(count):
@@ -809,13 +820,13 @@
 
     def places_in(orders):
         found = []
-        for which in (orders, [swapped(order) for order in orders]):
+        for which in (orders, crossed(orders)):
             one, two = (place(order, x_at, y_at, z_at) for order in which)
             found += [jnp.where(core == 0, one, two), jnp.where(core == 0, two, one)]
         return jnp.stack([*found, core]).astype(jnp.int32)
 
     expert_places = places_in(EXPERT_ORDERS)
-    late_orders = tuple(swapped(order) for order in ATTENTION_ORDERS)
+    attention_places = places_in(ATTENTION_ORDERS)
 
     attention_weights = (gain_attention, query_weight, key_matrix, value_matrix, output_weight)
     expert_weights = (gate_weight, up_weight, down_weight)
@@ -834,66 +845,70 @@
         1, [middle1, part, exchange(part)], attention_weights, tables, segment,
         others.finish(part),
     )
-    middle2, xi2, share2, last, back, gate_grad, keep, send = expert_both(
+    middle2, xi2, share2, last, back, keep, send = expert_both(
         1, expert_places, x2, part, part_other, gain_experts, router, mask, *expert_weights,
         cotangent,
     )
-    both_orders = (EXPERT_ORDERS, tuple(swapped(order) for order in EXPERT_ORDERS))
-    sum_e2 = Scatter(keep, send, *both_orders)
-    other, gate_other = exchange(back), exchange(gate_grad)
+    half = keep.shape[1] // 2
+    split = SMALL + query_weight.shape[2] + key_matrix.shape[2]
+    sum_e2 = Scatter(keep, send, EXPERT_ORDERS, half)
+    other = exchange(back)
     *sends, last = behind([*sum_e2.halve(), last], other)
     sum_e2.move(sends)
     last_other = exchange(last)
     no_gain = jnp.zeros((8, features), F32)
     g2, part, keep, send, part_other = attention_backward(
-        1, late_orders, places_in(late_orders), cotangent, back, other, gate_grad, gate_other,
-        (middle2, xi2, share2), back_weights, (x2, *saved2), tables, segment, no_gain, sends,
+        1, attention_places, cotangent, back, other, (middle2, xi2, share2), back_weights,
+        (x2, *saved2), tables, segment, no_gain, sends,
         (q_other, kk_other, vv_other, weights_other),
     )
-    sum_a2 = Scatter(keep, send, late_orders)
+    sum_a2 = Scatter(keep, send, ATTENTION_ORDERS, split)
     sends = sum_e2.halve()
-    g1, late_gain, back, gate_grad, keep, send = expert_backward(
+    g1, late_gain, back, keep, send = expert_backward(
         0, expert_places, g2, x2, gain_attention, part, part_other, xi1, share1, gate1,
         linear1, *expert_weights, [*sends, last_other],
     )
     sum_e2.move(sends)
-    sum_e1 = Scatter(keep, send, *both_orders)
-    other, gate_other = exchange(back), exchange(gate_grad)
+    sum_e1 = Scatter(keep, send, EXPERT_ORDERS, half)
+    other = exchange(back)
     sends_a, sends_e = sum_a2.halve(), sum_e1.halve()
     sum_a2.move(sends_a)
     sum_e1.move(sends_e)
-    sends = sends_a + sends_e + sum_e2.received()
     g0, part, keep, send = attention_backward(
-        0, ATTENTION_ORDERS, places_in(ATTENTION_ORDERS), g1, back, other, gate_grad, gate_other,
-        (middle1, xi1, share1), back_weights, (x1, *saved1), tables, segment, late_gain,
-        sends,
+        0, attention_places, g1, back, other, (middle1, xi1, share1), back_weights,
+        (x1, *saved1), tables, segment, late_gain, sends_a + sends_e + sum_e2.received(),
     )
     (send,) = behind([send], *sum_a2.received(), *sum_e1.received())
-    sum_a1 = Scatter(keep, send, ATTENTION_ORDERS)
-    sum_a1.advance()
+    sum_a1 = Scatter(keep, send, ATTENTION_ORDERS, split)
+    sends = sum_a1.halve()
+    sum_a1.move(sends)
     (other,) = behind([exchange(part)], *sum_a1.received())
     sum_a1.advance()
+    sum_a2.advance()
     sum_e1.advance()
-    sum_a2.advance()
-    sums = ((sum_a1, sum_a2), (sum_e1, sum_e2))
-    for one, two in sums:
-        one.join(two)
-        one.advance(2)
+    sum_e1.hold(*sends)
+    sum_e1.join(sum_e2)
+    sum_e1.advance(2)
+    sum_a1.join(sum_a2)
+    sum_a1.advance(2)
+    sums = (sum_a1, sum_e1)
     gain = norm_attention[0].astype(F32)
     change, _ = norm_back(x1, row_factor(x1), gain, part + other)
     gradient = g0 + change
     output = (middle2 + (last + last_other)).astype(BF16)
-    blocks = [one.finish() for one, _ in sums]
+    blocks = [one.finish() for one in sums]
 
     attention_sums, expert_sums = blocks
     rows = attention_sums.shape[0]
     layers = query_weight.shape[0]
-    attention_sums = jnp.swapaxes(attention_sums.reshape(rows, layers, -1), 0, 1)
-    bounds = np.cumsum(
-        [0, SMALL, query_weight.shape[2], key_matrix.shape[2], value_matrix.shape[2],
-         output_weight.shape[1]]
-    )
-    attention_sums = [attention_sums[..., a:b] for a, b in zip(bounds[:-1], bounds[1:])]
+    bounds = np.cumsum([0, SMALL, query_weight.shape[2], key_matrix.shape[2]])
+    more_bounds = np.cumsum([0, value_matrix.shape[2], output_weight.shape[1]])
+    one, two = (
+        jnp.swapaxes(columns.reshape(rows, layers, -1), 0, 1)
+        for columns in (attention_sums[:, : layers * split], attention_sums[:, layers * split :])
+    )
+    attention_sums = [one[..., a:b] for a, b in zip(bounds[:-1], bounds[1:])]
+    attention_sums += [two[..., a:b] for a, b in zip(more_bounds[:-1], more_bounds[1:])]
     expert_sums = expert_sums.reshape(rows, 2, layers, experts // 2, 3, hidden)
     expert_sums = [
         expert_sums[..., kind, :].transpose(2, 1, 3, 0, 4).reshape(layers, experts, rows, hidden)

time: 367 us -> 374 us (1.019)
  waiting for transfers between devices: 142 us -> 119 us
  starting transfers between devices: 53.9 us -> 74.4 us
  other arithmetic: 39.9 us -> 46.7 us
    ppermute x18 -> x24, waiting for transfers between devices: 73.8 us -> 45.6 us  [move(): lax.ppermute(send, RING_AXES, ring_pairs(orders, self.step))]
    ppermute x18 -> x24, starting transfers between devices: 19.9 us -> 38.8 us  [move(): lax.ppermute(send, RING_AXES, ring_pairs(orders, self.step))]
    add x18 -> x26, other arithmetic: 31.3 us -> 37.5 us  [halve(): self.kept = [first[:half] + second[:half] for first, second in self.parts]]
    ppermute x4, waiting for transfers between devices: 15.2 us -> 20.2 us  [__init__(): received = lax.ppermute(send, 'dp_3', SWAP)]
    ppermute x10 -> x8, starting transfers between devices: 9.36 us -> 8.2 us  [exchange(): return lax.ppermute(array, 'tensor', SWAP)]
    unnamed x77 -> x80, local copies, waits for them, and re-layouts: 11.4 us -> 11.9 us
    ppermute x10 -> x8, waiting for transfers between devices: 34.4 us -> 34.4 us  [exchange(): return lax.ppermute(array, 'tensor', SWAP)]
  transfers between devices with their start and end apart: 44 -> 48, of which waited for: 20 -> 23; matrix products, arithmetic and copies ran while one was open for 15% -> 18% of each run, Pallas kernels for 14% -> 14%
where the time goes in v1:
time: 374 us; the launch traced here: 367 us
  waiting for transfers between devices  119 us (32%)
  Pallas kernels  95.5 us (26%)
  starting transfers between devices  74.4 us (20%)
  other arithmetic  46.7 us (12%)
  local copies, waits for them, and re-layouts  30 us (8%)
    ppermute x24, waiting for transfers between devices, move(): lax.ppermute(send, RING_AXES, ring_pairs(orders, self.step))  45.6 us
    ppermute x24, starting transfers between devices, move(): lax.ppermute(send, RING_AXES, ring_pairs(orders, self.step))  38.8 us
    add x26, other arithmetic, halve(): self.kept = [first[:half] + second[:half] for first, second in self.parts]  37.5 us
    pallas_call x2, Pallas kernels, attention_backward(): pl.pallas_call(functools.partial(attention_backward_kernel, len(after), b...  36.6 us
    pallas_call x3, Pallas kernels, run_experts(): pl.pallas_call(kernel, grid=(STREAMS,), in_specs=in_specs, out_specs=[spe...  36.2 us
    ppermute x8, waiting for transfers between devices, exchange(): return lax.ppermute(array, 'tensor', SWAP)  34.4 us
    pallas_call x2, Pallas kernels, attention_forward(): pl.pallas_call(functools.partial(attention_forward_kernel, len(parts), bo...  22.7 us
    ppermute x4, waiting for transfers between devices, __init__(): received = lax.ppermute(send, 'dp_3', SWAP)  20.2 us
  transfers between devices with their start and end apart: 48, of which 23 were waited for; matrix products, arithmetic and copies ran while one was open for 18% of the time, Pallas kernels for 14%

profile of v1, /device:TPU:0, one launch (start us, length us, event | category | flops | bytes accessed | tf_op | source)
XLA Modules:
  0.0 366.6 jit_solution(4371739373157762927)
XLA Ops:
  2.5 1.7 collective-permute-start.2
  5.7 6.6 %attention_forward.2 = (f32[256,1024]{1,0:T(8,128)}, bf16[256,1024]{1,0:T(8,128)(2,1)}, bf16[256,512]{1,0:T(8,128)(2,1)}, bf16[4,256,128]{2,1,0:T(8,128)(2,1)}, ...) custom-call(bf16[256,1024]{1,0:T(8,128)(2,1)} %refs_0_.1, ...), custom_call_target="tpu_custom_call" | custom-call | flops 6442450944 | bytes 8388608 | tf_op jit(solution)/shard_map/attention_forward/pallas_call | solution.py:286
  13.0 2.8 collective-permute-start.3
  16.2 3.9 %collective-permute-done.3 = f32[48,1024]{1,0:T(8,128)S(1)} collective-permute-done((f32[48,1024]{1,0:T(8,128)}, f32[48,1024]{1,0:T(8,128)S(1)}, u32[]{:S(2)}, u32[]{:S(2)}) %collective-permute-start.3) | collective-permute-done | bytes 196640 | tf_op jit(solution)/shard_map/ppermute | solution.py:759
  21.0 4.1 %collective-permute-start.4 = (f32[96,1024]{1,0:T(8,128)S(1)}, f32[96,1024]{1,0:T(8,128)S(1)}, u32[]{:S(2)}, u32[]{:S(2)}) collective-permute-start(f32[96,1024]{1,0:T(8,128)S(1)} %pad_maximum_fusion.5), channel_id=1, source_target_pairs={{0,12},{2,34},{4,8},{6,38},{8,4},{10,42},{12,0},{14,46},{32,44},{3... | collective-permute-start | bytes 1179656 | tf_op jit(solution)/shard_map/ppermute | solution.py:759
  27.9 3.0 collective-permute-done.4
  31.9 7.6 %collective-permute-done.other.refs_2_ = f32[256,1024]{1,0:T(8,128)S(1)} collective-permute-done((f32[256,1024]{1,0:T(8,128)}, f32[256,1024]{1,0:T(8,128)S(1)}, u32[]{:S(2)}, u32[]{:S(2)}) %collective-permute-start) | collective-permute-done | bytes 1048608 | tf_op jit(solution)/shard_map/ppermute | solution.py:675
  40.7 1.5 collective-permute-start.6
  42.2 7.9 %experts_forward.1 = (f32[256,1024]{1,0:T(8,128)}, bf16[256,1024]{1,0:T(8,128)(2,1)}, f32[256,128]{1,0:T(8,128)}, f32[4,256,256]{2,1,0:T(8,128)}, f32[4,256,256]{2,1,0:T(8,128)}, /*index=5*/f32[256,1024]{1,0:T(8,128)}) custom-call(f32[256,1024]{1,0:T(8,128)} %get-tuple-element.67.x, f32[256,1024]{1,0:T(8,128)} %get-tuple-element.68.own.refs_1_, ...), custom_call_target="tpu_custom_call" | custom-call | flops 8589934592 | bytes 12582912 | tf_op jit(solution)/shard_map/experts_forward/pallas_call | solution.py:433
  53.0 1.8 collective-permute-start.8
  56.1 8.4 %collective-permute-done.7.refs_15_ = f32[384,512]{1,0:T(8,128)} collective-permute-done((f32[384,512]{1,0:T(8,128)S(1)}, f32[384,512]{1,0:T(8,128)}, u32[]{:S(2)}, u32[]{:S(2)}) %collective-permute-start.7) | collective-permute-done | bytes 786464 | tf_op jit(solution)/shard_map/ppermute | solution.py:767
  65.8 2.4 collective-permute-start.12
  69.4 11.5 %collective-permute-done.1.refs_2_ = f32[256,1024]{1,0:T(8,128)} collective-permute-done((f32[256,1024]{1,0:T(8,128)S(1)}, f32[256,1024]{1,0:T(8,128)}, u32[]{:S(2)}, u32[]{:S(2)}) %collective-permute-start.1) | collective-permute-done | bytes 1048608 | tf_op jit(solution)/shard_map/ppermute | solution.py:675
  80.9 16.1 %attention_forward.3 = (f32[256,1024]{1,0:T(8,128)}, bf16[256,1024]{1,0:T(8,128)(2,1)}, bf16[256,512]{1,0:T(8,128)(2,1)}, bf16[4,256,128]{2,1,0:T(8,128)(2,1)}, ...) custom-call(f32[256,1024]{1,0:T(8,128)} %get-tuple-element.69.refs_0, ...), custom_call_target="tpu_custom_call" | custom-call | flops 6442450944 | bytes 8388608 | tf_op jit(solution)/shard_map/attention_forward/pallas_call | solution.py:286
  97.0 14.8 %experts_both.1 = (f32[256,1024]{1,0:T(8,128)}, bf16[256,1024]{1,0:T(8,128)(2,1)}, f32[256,128]{1,0:T(8,128)}, f32[256,1024]{1,0:T(8,128)}, f32[256,1152]{1,0:T(...) custom-call(s32[5]{0:T(128)} %stack.47.places, f32[256,1024]{1,0:T(8,128)} %get-tuple-element.75.x, ...), custom_call_target="tpu_custom_call" | custom-call | flops 17179869184 | bytes 31457280 | tf_op jit(solution)/shard_map/experts_both/pallas_call | solution.py:433
  113.6 8.8 %collective-permute-done.13 = f32[512,3072]{1,0:T(8,128)} collective-permute-done((f32[512,3072]{1,0:T(8,128)}, f32[512,3072]{1,0:T(8,128)}, u32[]{:S(2)}, u32[]{:S(2)}) %collective-permute-start.13) | collective-permute-done | bytes 6291488 | tf_op jit(solution)/shard_map/ppermute | solution.py:696
  122.4 7.8 %slice_add_fusion.4 = (f32[256,1536]{1,0:T(8,128)S(1)}, f32[256,1536]{1,0:T(8,128)S(1)}, f32[256,1536]{1,0:T(8,128)}, f32[256,1536]{1,0:T(8,128)}) fusion(f32[512,3072]{1,0:T(8,128)} %collective-permute-done.13, f32[512,3072]{1,0:T(8,128)} %get-tuple-element.79), kind=kLoop, calls=%fused_computation.4 | loop fusion | flops 1572864 | bytes 18874368 | tf_op jit(solution)/shard_map/add | solution.py:706
  130.2 10.5 %collective-permute-done.14.refs_3_.other = f32[256,1152]{1,0:T(8,128)} collective-permute-done((f32[256,1152]{1,0:T(8,128)}, f32[256,1152]{1,0:T(8,128)}, u32[]{:S(2)}, u32[]{:S(2)}) %collective-permute-start.14) | collective-permute-done | bytes 1179680 | tf_op jit(solution)/shard_map/ppermute | solution.py:675
  141.4 12.9 %collective-permute-start.17 = (f32[256,1536]{1,0:T(8,128)}, f32[256,1536]{1,0:T(8,128)}, u32[]{:S(2)}, u32[]{:S(2)}) collective-permute-start(f32[256,1536]{1,0:T(8,128)} %get-tuple-element.96.rest_5_), channel_id=1, source_target_pairs={{0,4},{2,98},{4,0},{6,102},{8,12},{10,106},{12,8},{14,110},{32,36}... | collective-permute-start | bytes 4718600 | tf_op jit(solution)/shard_map/ppermute | solution.py:711
  154.9 21.5 %attention_backward.2 = (f32[256,1024]{1,0:T(8,128)}, f32[256,1024]{1,0:T(8,128)}, f32[512,1664]{1,0:T(8,128)}, f32[512,1664]{1,0:T(8,128)}, f32[256,1024]{1,0:T(8,128)}) custom-call(s32[5]{0:T(128)} %stack.53.places, bf16[256,1024]{1,0:T(8,128)(2,1)} %g.1, f32[256,1152]{1,0:T(8,128)} %get-tuple-element.82.own, ...), custom_call_target="tpu_custom_call" | custom-call | flops 17179869184 | bytes 18874368 | tf_op jit(solution)/shard_map/attention_backward/pallas_call | solution.py:655
  176.4 2.7 slice_add_fusion.18
  179.2 2.7 slice_add_fusion.13
  181.9 13.5 %experts_backward.1 = (f32[256,1024]{1,0:T(8,128)}, f32[8,1024]{1,0:T(8,128)}, f32[256,1152]{1,0:T(8,128)}, f32[512,3072]{1,0:T(8,128)}, f32[512,3072]{1,0:T(8,128)}) custom-call(s32[5]{0:T(128)} %stack.47.places, f32[256,1024]{1,0:T(8,128)} %get-tuple-element.97.g_in, f32[256,1024]{1,0:T(8,128)} %get-tuple-element.75.x, ...), custom_call_target="tpu_custom_call" | custom-call | flops 4294967296 | bytes 31457280 | tf_op jit(solution)/shard_map/experts_backward/pallas_call | solution.py:433
  195.4 2.1 collective-permute-start.20
  199.3 1.7 collective-permute-start.18
  201.0 11.4 %collective-permute-done.19 = f32[512,1664]{1,0:T(8,128)S(1)} collective-permute-done((f32[512,1664]{1,0:T(8,128)}, f32[512,1664]{1,0:T(8,128)S(1)}, u32[]{:S(2)}, u32[]{:S(2)}) %collective-permute-start.19) | collective-permute-done | bytes 3407904 | tf_op jit(solution)/shard_map/ppermute | solution.py:696
  212.4 1.5 slice_add_fusion.8
  213.9 1.7 collective-permute-start.24
  217.0 1.7 collective-permute-start.25
  218.7 3.1 slice_add_fusion
  221.8 1.4 collective-permute-start.26
  223.7 4.5 %collective-permute-done.18.other = f32[256,1152]{1,0:T(8,128)} collective-permute-done((f32[256,1152]{1,0:T(8,128)}, f32[256,1152]{1,0:T(8,128)}, u32[]{:S(2)}, u32[]{:S(2)}) %collective-permute-start.18) | collective-permute-done | bytes 1179680 | tf_op jit(solution)/shard_map/ppermute | solution.py:675
  228.1 15.1 %attention_backward.3 = (f32[256,1024]{1,0:T(8,128)}, f32[256,1024]{1,0:T(8,128)}, f32[512,1664]{1,0:T(8,128)}, f32[512,1664]{1,0:T(8,128)}) custom-call(s32[5]{0:T(128)} %stack.53.places, f32[256,1024]{1,0:T(8,128)} %get-tuple-element.104.g, f32[256,1152]{1,0:T(8,128)} %get-tuple-element.105.own, f32[256,1152]{1,0:T(8,128)} %collective-permute-done.18.other, ...), custom_call_target="tpu_custom_call" | custom-call | flops 17179869184 | bytes 18874368 | tf_op jit(solution)/shard_map/attention_backward/pallas_call | solution.py:655
  244.4 2.9 collective-permute-start.28
  247.2 2.9 add_convert_fusion
  250.2 2.0 slice_add_fusion.38
  252.2 1.5 collective-permute-start.36
  253.7 2.4 slice_add_fusion.19
  256.2 1.7 slice_add_fusion.14
  258.0 2.4 slice_add_fusion.29
  260.4 2.1 collective-permute-start.32
  262.5 1.6 collective-permute-start.23
  266.8 5.1 %collective-permute-done.41.refs_0_ = f32[128,1536]{1,0:T(8,128)} collective-permute-done((f32[128,1536]{1,0:T(8,128)S(1)}, f32[128,1536]{1,0:T(8,128)}, u32[]{:S(2)}, u32[]{:S(2)}) %collective-permute-start.41) | collective-permute-done | bytes 786464 | tf_op jit(solution)/shard_map/ppermute | solution.py:711
  274.6 3.3 collective-permute-start.45
  280.6 13.1 %collective-permute-done.45 = f32[64,3072]{1,0:T(8,128)S(1)} collective-permute-done((f32[64,3072]{1,0:T(8,128)S(1)}, f32[64,3072]{1,0:T(8,128)S(1)}, u32[]{:S(2)}, u32[]{:S(2)}) %collective-permute-start.45) | collective-permute-done | bytes 786464 | tf_op jit(solution)/shard_map/ppermute | solution.py:711
  293.7 1.4 collective-permute-start.43
  296.2 1.8 collective-permute-start.29
  298.0 2.1 slice_add_fusion.39
  300.0 6.9 %collective-permute-done.43 = f32[64,3072]{1,0:T(8,128)S(1)} collective-permute-done((f32[64,3072]{1,0:T(8,128)S(1)}, f32[64,3072]{1,0:T(8,128)S(1)}, u32[]{:S(2)}, u32[]{:S(2)}) %collective-permute-start.43) | collective-permute-done | bytes 786464 | tf_op jit(solution)/shard_map/ppermute | solution.py:711
  306.9 1.6 collective-permute-start.35
  309.5 1.8 collective-permute-start.46
  311.3 5.4 %collective-permute-done.29.refs_1_ = f32[256,896]{1,0:T(8,128)S(1)} collective-permute-done((f32[256,896]{1,0:T(8,128)S(1)}, f32[256,896]{1,0:T(8,128)S(1)}, u32[]{:S(2)}, u32[]{:S(2)}) %collective-permute-start.29) | collective-permute-done | bytes 917536 | tf_op jit(solution)/shard_map/ppermute | solution.py:711
  318.9 1.7 multiply_reduce_fusion.1
  322.7 2.1 collective-permute-start.31
  328.3 2.2 collective-permute-done.44
  331.6 3.3 collective-permute-start.47
  337.4 2.1 collective-permute-start.38
  339.5 1.5 collective-permute-done.47
  341.3 4.5 %collective-permute-done.33 = f32[64,1792]{1,0:T(8,128)S(1)} collective-permute-done((f32[64,1792]{1,0:T(8,128)S(1)}, f32[64,1792]{1,0:T(8,128)S(1)}, u32[]{:S(2)}, u32[]{:S(2)}) %collective-permute-start.33) | collective-permute-done | bytes 458784 | tf_op jit(solution)/shard_map/ppermute | solution.py:711
  345.9 2.0 collective-permute-done.38
  347.9 4.0 %collective-permute-done.34 = f32[32,1792]{1,0:T(8,128)S(1)} collective-permute-done((f32[32,1792]{1,0:T(8,128)S(1)}, f32[32,1792]{1,0:T(8,128)S(1)}, u32[]{:S(2)}, u32[]{:S(2)}) %collective-permute-start.34) | collective-permute-done | bytes 229408 | tf_op jit(solution)/shard_map/ppermute | solution.py:711
  352.0 3.3 collective-permute-start.39
  357.9 1.6 collective-permute-done.39
  362.3 1.6 collective-permute-start.40
  (210 shorter events, 54.6 us)
Async XLA Ops:
  2.5 9.8 %collective-permute-start.2 = (f32[48,1024]{1,0:T(8,128)S(1)}, f32[48,1024]{1,0:T(8,128)S(1)}, u32[]{:S(2)}, u32[]{:S(2)}) collective-permute-start(f32[48,1024]{1,0:T(8,128)S(1)} %maximum_convert_fusion), channel_id=1, source_target_pairs={{0,1},{1,0},{2,3},{3,2},{4,5},{5,4},{6,7},{7,6},{8,9},{9,8},{10,11... | collective-permute-start | bytes 589832 | tf_op jit(solution)/shard_map/ppermute | solution.py:675
  12.3 12.9 %copy-start.30 = (bf16[2,1024]{1,0:T(2,128)(2,1)S(1)}, bf16[2,1024]{1,0:T(2,128)(2,1)}, u32[]{:S(2)}) copy-start(bf16[2,1024]{1,0:T(2,128)(2,1)} %param.24) | copy-start | bytes 12292
  12.3 13.5 %copy-start.28 = (bf16[2,1024,4]{1,2,0:T(4,128)(2,1)S(1)}, bf16[2,1024,4]{1,2,0:T(4,128)(2,1)}, u32[]{:S(2)}) copy-start(bf16[2,1024,4]{1,2,0:T(4,128)(2,1)} %param.25) | copy-start | bytes 49156
  12.3 13.8 %copy-start.31 = (s32[2,256,2]{1,2,0:T(2,128)S(1)}, s32[2,256,2]{1,2,0:T(2,128)}, u32[]{:S(2)}) copy-start(s32[2,256,2]{1,2,0:T(2,128)} %param.18) | copy-start | bytes 12292
  13.0 17.9 %copy-start.19 = (f32[48,1024]{1,0:T(8,128)S(1)}, f32[48,1024]{1,0:T(8,128)}, u32[]{:S(2)}) copy-start(f32[48,1024]{1,0:T(8,128)} %behind.7) | copy-start | bytes 589828
  13.0 7.1 %collective-permute-start.3 = (f32[48,1024]{1,0:T(8,128)}, f32[48,1024]{1,0:T(8,128)S(1)}, u32[]{:S(2)}, u32[]{:S(2)}) collective-permute-start(f32[48,1024]{1,0:T(8,128)} %behind.7), channel_id=1, source_target_pairs={{0,96},{2,6},{4,100},{6,2},{8,104},{10,14},{12,108},{14,10},{32,64... | collective-permute-start | bytes 589832 | tf_op jit(solution)/shard_map/ppermute | solution.py:759
  15.7 23.7 %collective-permute-start = (f32[256,1024]{1,0:T(8,128)}, f32[256,1024]{1,0:T(8,128)S(1)}, u32[]{:S(2)}, u32[]{:S(2)}) collective-permute-start(f32[256,1024]{1,0:T(8,128)} %get-tuple-element.68.own.refs_1_), channel_id=1, source_target_pairs={{0,1},{1,0},{2,3},{3,2},{4,5},{5,4},{6,7},{7,6},{8,9},{9,8},{10,11... | collective-permute-start | bytes 3145736 | tf_op jit(solution)/shard_map/ppermute | solution.py:675
  21.0 9.9 %collective-permute-start.4 = (f32[96,1024]{1,0:T(8,128)S(1)}, f32[96,1024]{1,0:T(8,128)S(1)}, u32[]{:S(2)}, u32[]{:S(2)}) collective-permute-start(f32[96,1024]{1,0:T(8,128)S(1)} %pad_maximum_fusion.5), channel_id=1, source_target_pairs={{0,12},{2,34},{4,8},{6,38},{8,4},{10,42},{12,0},{14,46},{32,44},{3... | collective-permute-start | bytes 1179656 | tf_op jit(solution)/shard_map/ppermute | solution.py:759
  40.4 9.7 %collective-permute-start.5 = (f32[192,512]{1,0:T(8,128)}, f32[192,512]{1,0:T(8,128)S(1)}, u32[]{:S(2)}, u32[]{:S(2)}) collective-permute-start(f32[192,512]{1,0:T(8,128)} %get-tuple-element.71.refs_0_), channel_id=1, source_target_pairs={{0,4},{2,98},{4,0},{6,102},{8,12},{10,106},{12,8},{14,110},{32,36}... | collective-permute-start | bytes 1179656 | tf_op jit(solution)/shard_map/ppermute | solution.py:767
  40.7 9.4 %collective-permute-start.6 = (f32[192,512]{1,0:T(8,128)}, f32[192,512]{1,0:T(8,128)S(1)}, u32[]{:S(2)}, u32[]{:S(2)}) collective-permute-start(f32[192,512]{1,0:T(8,128)} %get-tuple-element.72.refs_1_), channel_id=1, source_target_pairs={{0,32},{2,14},{4,36},{6,10},{8,40},{10,6},{12,44},{14,2},{32,0},{3... | collective-permute-start | bytes 1179656 | tf_op jit(solution)/shard_map/ppermute | solution.py:767
  50.1 4.7 %copy-start.23 = (f32[256,1024]{1,0:T(8,128)S(1)}, f32[256,1024]{1,0:T(8,128)}, u32[]{:S(2)}) copy-start(f32[256,1024]{1,0:T(8,128)} %get-tuple-element.70.refs_2_.refs_1_) | copy-start | bytes 3145732
  52.3 28.6 %copy-start.27 = (f32[384,512]{1,0:T(8,128)}, f32[384,512]{1,0:T(8,128)S(1)}, u32[]{:S(2)}) copy-start(f32[384,512]{1,0:T(8,128)S(1)} %constant_dynamic-update-slice_fusion.refs_13_) | copy-start | bytes 2359300
  52.3 12.2 %collective-permute-start.7 = (f32[384,512]{1,0:T(8,128)S(1)}, f32[384,512]{1,0:T(8,128)}, u32[]{:S(2)}, u32[]{:S(2)}) collective-permute-start(f32[384,512]{1,0:T(8,128)S(1)} %constant_dynamic-update-slice_fusion.refs_13_), channel_id=1, source_target_pairs={{0,32},{2,14},{4,36},{6,10},{8,40},{10,6},{12,44},{14,2},{32,0},{3... | collective-permute-start | bytes 2359304 | tf_op jit(solution)/shard_map/ppermute | solution.py:767
  53.0 27.9 %copy-start.26 = (f32[384,512]{1,0:T(8,128)}, f32[384,512]{1,0:T(8,128)S(1)}, u32[]{:S(2)}) copy-start(f32[384,512]{1,0:T(8,128)S(1)} %constant_dynamic-update-slice_fusion.2.refs_14_) | copy-start | bytes 2359300
  53.0 12.8 %collective-permute-start.8 = (f32[384,512]{1,0:T(8,128)S(1)}, f32[384,512]{1,0:T(8,128)S(1)}, u32[]{:S(2)}, u32[]{:S(2)}) collective-permute-start(f32[384,512]{1,0:T(8,128)S(1)} %constant_dynamic-update-slice_fusion.2.refs_14_), channel_id=1, source_target_pairs={{0,4},{2,98},{4,0},{6,102},{8,12},{10,106},{12,8},{14,110},{32,36}... | collective-permute-start | bytes 2359304 | tf_op jit(solution)/shard_map/ppermute | solution.py:767
  54.8 26.1 %collective-permute-start.1 = (f32[256,1024]{1,0:T(8,128)S(1)}, f32[256,1024]{1,0:T(8,128)}, u32[]{:S(2)}, u32[]{:S(2)}) collective-permute-start(f32[256,1024]{1,0:T(8,128)S(1)} %copy-done.23), channel_id=1, source_target_pairs={{0,1},{1,0},{2,3},{3,2},{4,5},{5,4},{6,7},{7,6},{8,9},{9,8},{10,11... | collective-permute-start | bytes 3145736 | tf_op jit(solution)/shard_map/ppermute | solution.py:675
  55.3 25.6 %collective-permute-start.9 = (f32[384,512]{1,0:T(8,128)S(1)}, f32[384,512]{1,0:T(8,128)}, u32[]{:S(2)}, u32[]{:S(2)}) collective-permute-start(f32[384,512]{1,0:T(8,128)S(1)} %constant_dynamic-update-slice_fusion.refs_13_), channel_id=1, source_target_pairs={{0,2},{2,0},{1,3},{3,1},{4,6},{6,4},{5,7},{7,5},{8,10},{10,8},{9,1... | collective-permute-start | bytes 2359304 | tf_op jit(solution)/shard_map/ppermute | solution.py:775
  56.1 24.7 %collective-permute-start.10 = (f32[384,512]{1,0:T(8,128)S(1)}, f32[384,512]{1,0:T(8,128)}, u32[]{:S(2)}, u32[]{:S(2)}) collective-permute-start(f32[384,512]{1,0:T(8,128)S(1)} %constant_dynamic-update-slice_fusion.2.refs_14_), channel_id=1, source_target_pairs={{0,2},{2,0},{1,3},{3,1},{4,6},{6,4},{5,7},{7,5},{8,10},{10,8},{9,1... | collective-permute-start | bytes 2359304 | tf_op jit(solution)/shard_map/ppermute | solution.py:775
  64.5 16.4 %collective-permute-start.11 = (f32[384,512]{1,0:T(8,128)}, f32[384,512]{1,0:T(8,128)}, u32[]{:S(2)}, u32[]{:S(2)}) collective-permute-start(f32[384,512]{1,0:T(8,128)} %collective-permute-done.7.refs_15_), channel_id=1, source_target_pairs={{0,2},{2,0},{1,3},{3,1},{4,6},{6,4},{5,7},{7,5},{8,10},{10,8},{9,1... | collective-permute-start | bytes 2359304 | tf_op jit(solution)/shard_map/ppermute | solution.py:775
  65.8 15.1 %copy-start.33 = (f32[384,512]{1,0:T(8,128)}, f32[384,512]{1,0:T(8,128)S(1)}, u32[]{:S(2)}) copy-start(f32[384,512]{1,0:T(8,128)S(1)} %collective-permute-done.8.refs_16_) | copy-start | bytes 2359300
  65.8 15.1 %collective-permute-start.12 = (f32[384,512]{1,0:T(8,128)S(1)}, f32[384,512]{1,0:T(8,128)}, u32[]{:S(2)}, u32[]{:S(2)}) collective-permute-start(f32[384,512]{1,0:T(8,128)S(1)} %collective-permute-done.8.refs_16_), channel_id=1, source_target_pairs={{0,2},{2,0},{1,3},{3,1},{4,6},{6,4},{5,7},{7,5},{8,10},{10,8},{9,1... | collective-permute-start | bytes 2359304 | tf_op jit(solution)/shard_map/ppermute | solution.py:775
  111.8 10.6 %collective-permute-start.13 = (f32[512,3072]{1,0:T(8,128)}, f32[512,3072]{1,0:T(8,128)}, u32[]{:S(2)}, u32[]{:S(2)}) collective-permute-start(f32[512,3072]{1,0:T(8,128)} %get-tuple-element.80), channel_id=1, source_target_pairs={{0,2},{2,0},{1,3},{3,1},{4,6},{6,4},{5,7},{7,5},{8,10},{10,8},{9,1... | collective-permute-start | bytes 18874376 | tf_op jit(solution)/shard_map/ppermute | solution.py:696
  112.0 28.6 %collective-permute-start.14 = (f32[256,1152]{1,0:T(8,128)}, f32[256,1152]{1,0:T(8,128)}, u32[]{:S(2)}, u32[]{:S(2)}) collective-permute-start(f32[256,1152]{1,0:T(8,128)} %get-tuple-element.82.own), channel_id=1, source_target_pairs={{0,1},{1,0},{2,3},{3,2},{4,5},{5,4},{6,7},{7,6},{8,9},{9,8},{10,11... | collective-permute-start | bytes 3538952 | tf_op jit(solution)/shard_map/ppermute | solution.py:675
  140.7 41.2 %collective-permute-start.15 = (f32[256,1024]{1,0:T(8,128)}, f32[256,1024]{1,0:T(8,128)}, u32[]{:S(2)}, u32[]{:S(2)}) collective-permute-start(f32[256,1024]{1,0:T(8,128)} %get-tuple-element.83), channel_id=1, source_target_pairs={{0,1},{1,0},{2,3},{3,2},{4,5},{5,4},{6,7},{7,6},{8,9},{9,8},{10,11... | collective-permute-start | bytes 3145736 | tf_op jit(solution)/shard_map/ppermute | solution.py:675
  141.0 35.4 %collective-permute-start.16 = (f32[256,1536]{1,0:T(8,128)}, f32[256,1536]{1,0:T(8,128)}, u32[]{:S(2)}, u32[]{:S(2)}) collective-permute-start(f32[256,1536]{1,0:T(8,128)} %get-tuple-element.95.rest_4_), channel_id=1, source_target_pairs={{0,32},{2,14},{4,36},{6,10},{8,40},{10,6},{12,44},{14,2},{32,0},{3... | collective-permute-start | bytes 4718600 | tf_op jit(solution)/shard_map/ppermute | solution.py:711
  141.4 37.7 %collective-permute-start.17 = (f32[256,1536]{1,0:T(8,128)}, f32[256,1536]{1,0:T(8,128)}, u32[]{:S(2)}, u32[]{:S(2)}) collective-permute-start(f32[256,1536]{1,0:T(8,128)} %get-tuple-element.96.rest_5_), channel_id=1, source_target_pairs={{0,4},{2,98},{4,0},{6,102},{8,12},{10,106},{12,8},{14,110},{32,36}... | collective-permute-start | bytes 4718600 | tf_op jit(solution)/shard_map/ppermute | solution.py:711
  181.9 30.5 %copy-start.11 = (f32[512,1664]{1,0:T(8,128)S(1)}, f32[512,1664]{1,0:T(8,128)}, u32[]{:S(2)}) copy-start(f32[512,1664]{1,0:T(8,128)} %get-tuple-element.112) | copy-start | bytes 10223620
  195.4 21.6 %collective-permute-start.20 = (f32[512,3072]{1,0:T(8,128)}, f32[512,3072]{1,0:T(8,128)S(1)}, u32[]{:S(2)}, u32[]{:S(2)}) collective-permute-start(f32[512,3072]{1,0:T(8,128)} %get-tuple-element.115), channel_id=1, source_target_pairs={{0,2},{2,0},{1,3},{3,1},{4,6},{6,4},{5,7},{7,5},{8,10},{10,8},{9,1... | collective-permute-start | bytes 18874376 | tf_op jit(solution)/shard_map/ppermute | solution.py:696
  197.5 14.9 %collective-permute-start.19 = (f32[512,1664]{1,0:T(8,128)}, f32[512,1664]{1,0:T(8,128)S(1)}, u32[]{:S(2)}, u32[]{:S(2)}) collective-permute-start(f32[512,1664]{1,0:T(8,128)} %get-tuple-element.113), channel_id=1, source_target_pairs={{0,2},{2,0},{1,3},{3,1},{4,6},{6,4},{5,7},{7,5},{8,10},{10,8},{9,1... | collective-permute-start | bytes 10223624 | tf_op jit(solution)/shard_map/ppermute | solution.py:696
  197.6 24.2 %collective-permute-start.21 = (f32[128,1536]{1,0:T(8,128)}, f32[128,1536]{1,0:T(8,128)}, u32[]{:S(2)}, u32[]{:S(2)}) collective-permute-start(f32[128,1536]{1,0:T(8,128)} %get-tuple-element.193.rest_0_), channel_id=1, source_target_pairs={{0,4},{2,98},{4,0},{6,102},{8,12},{10,106},{12,8},{14,110},{32,36}... | collective-permute-start | bytes 2359304 | tf_op jit(solution)/shard_map/ppermute | solution.py:711
  198.8 24.4 %collective-permute-start.22 = (f32[128,1536]{1,0:T(8,128)}, f32[128,1536]{1,0:T(8,128)}, u32[]{:S(2)}, u32[]{:S(2)}) collective-permute-start(f32[128,1536]{1,0:T(8,128)} %get-tuple-element.199.rest_1_), channel_id=1, source_target_pairs={{0,32},{2,14},{4,36},{6,10},{8,40},{10,6},{12,44},{14,2},{32,0},{3... | collective-permute-start | bytes 2359304 | tf_op jit(solution)/shard_map/ppermute | solution.py:711
  199.3 28.8 %collective-permute-start.18 = (f32[256,1152]{1,0:T(8,128)}, f32[256,1152]{1,0:T(8,128)}, u32[]{:S(2)}, u32[]{:S(2)}) collective-permute-start(f32[256,1152]{1,0:T(8,128)} %get-tuple-element.105.own), channel_id=1, source_target_pairs={{0,1},{1,0},{2,3},{3,2},{4,5},{5,4},{6,7},{7,6},{8,9},{9,8},{10,11... | collective-permute-start | bytes 3538952 | tf_op jit(solution)/shard_map/ppermute | solution.py:675
  212.4 6.3 %copy-start.2 = (f32[512,3072]{1,0:T(8,128)S(1)}, f32[512,3072]{1,0:T(8,128)}, u32[]{:S(2)}) copy-start(f32[512,3072]{1,0:T(8,128)} %get-tuple-element.114) | copy-start | bytes 18874372
  213.9 29.3 %collective-permute-start.24 = (f32[256,896]{1,0:T(8,128)}, f32[256,896]{1,0:T(8,128)}, u32[]{:S(2)}, u32[]{:S(2)}) collective-permute-start(f32[256,896]{1,0:T(8,128)} %get-tuple-element.181.rest_0_), channel_id=1, source_target_pairs={{0,12},{2,34},{4,8},{6,38},{8,4},{10,42},{12,0},{14,46},{32,44},{3... | collective-permute-start | bytes 2752520 | tf_op jit(solution)/shard_map/ppermute | solution.py:711
  217.0 26.2 %collective-permute-start.25 = (f32[256,768]{1,0:T(8,128)}, f32[256,768]{1,0:T(8,128)}, u32[]{:S(2)}, u32[]{:S(2)}) collective-permute-start(f32[256,768]{1,0:T(8,128)} %get-tuple-element.185.rest_1_), channel_id=1, source_target_pairs={{0,96},{2,6},{4,100},{6,2},{8,104},{10,14},{12,108},{14,10},{32,64... | collective-permute-start | bytes 2359304 | tf_op jit(solution)/shard_map/ppermute | solution.py:711
  221.8 22.1 %collective-permute-start.26 = (f32[256,1536]{1,0:T(8,128)}, f32[256,1536]{1,0:T(8,128)}, u32[]{:S(2)}, u32[]{:S(2)}) collective-permute-start(f32[256,1536]{1,0:T(8,128)} %get-tuple-element.175.rest_2_), channel_id=1, source_target_pairs={{0,32},{2,14},{4,36},{6,10},{8,40},{10,6},{12,44},{14,2},{32,0},{3... | collective-permute-start | bytes 4718600 | tf_op jit(solution)/shard_map/ppermute | solution.py:711
  223.3 21.1 %collective-permute-start.27 = (f32[256,1536]{1,0:T(8,128)}, f32[256,1536]{1,0:T(8,128)}, u32[]{:S(2)}, u32[]{:S(2)}) collective-permute-start(f32[256,1536]{1,0:T(8,128)} %get-tuple-element.174.rest_3_), channel_id=1, source_target_pairs={{0,4},{2,98},{4,0},{6,102},{8,12},{10,106},{12,8},{14,110},{32,36}... | collective-permute-start | bytes 4718600 | tf_op jit(solution)/shard_map/ppermute | solution.py:711
  244.4 18.1 %collective-permute-start.28 = (f32[512,1664]{1,0:T(8,128)}, f32[512,1664]{1,0:T(8,128)S(1)}, u32[]{:S(2)}, u32[]{:S(2)}) collective-permute-start(f32[512,1664]{1,0:T(8,128)} %behind.11), channel_id=1, source_target_pairs={{0,2},{2,0},{1,3},{3,1},{4,6},{6,4},{5,7},{7,5},{8,10},{10,8},{9,1... | collective-permute-start | bytes 10223624 | tf_op jit(solution)/shard_map/ppermute | solution.py:696
  252.2 73.7 %collective-permute-start.36 = (f32[128,768]{1,0:T(8,128)}, f32[128,768]{1,0:T(8,128)}, u32[]{:S(2)}, u32[]{:S(2)}) collective-permute-start(f32[128,768]{1,0:T(8,128)} %get-tuple-element.215), channel_id=1, source_target_pairs={{0,12},{2,34},{4,8},{6,38},{8,4},{10,42},{12,0},{14,46},{32,44},{3... | collective-permute-start | bytes 1179656 | tf_op jit(solution)/shard_map/ppermute | solution.py:711
  256.2 15.7 %collective-permute-start.41 = (f32[128,1536]{1,0:T(8,128)S(1)}, f32[128,1536]{1,0:T(8,128)}, u32[]{:S(2)}, u32[]{:S(2)}) collective-permute-start(f32[128,1536]{1,0:T(8,128)S(1)} %get-tuple-element.191), channel_id=1, source_target_pairs={{0,4},{2,98},{4,0},{6,102},{8,12},{10,106},{12,8},{14,110},{32,36}... | collective-permute-start | bytes 2359304 | tf_op jit(solution)/shard_map/ppermute | solution.py:711
  256.2 7.9 %copy-start.10 = (f32[512,1664]{1,0:T(8,128)S(1)}, f32[512,1664]{1,0:T(8,128)}, u32[]{:S(2)}) copy-start(f32[512,1664]{1,0:T(8,128)} %get-tuple-element.118) | copy-start | bytes 10223620
  257.9 4.6 %copy-start.4 = (f32[256,1024]{1,0:T(8,128)S(1)}, f32[256,1024]{1,0:T(8,128)}, u32[]{:S(2)}) copy-start(f32[256,1024]{1,0:T(8,128)} %get-tuple-element.117) | copy-start | bytes 3145732
  257.9 14.0 %collective-permute-start.42 = (f32[128,1536]{1,0:T(8,128)S(1)}, f32[128,1536]{1,0:T(8,128)}, u32[]{:S(2)}, u32[]{:S(2)}) collective-permute-start(f32[128,1536]{1,0:T(8,128)S(1)} %get-tuple-element.197), channel_id=1, source_target_pairs={{0,32},{2,14},{4,36},{6,10},{8,40},{10,6},{12,44},{14,2},{32,0},{3... | collective-permute-start | bytes 2359304 | tf_op jit(solution)/shard_map/ppermute | solution.py:711
  260.4 75.7 %collective-permute-start.32 = (f32[128,896]{1,0:T(8,128)}, f32[128,896]{1,0:T(8,128)}, u32[]{:S(2)}, u32[]{:S(2)}) collective-permute-start(f32[128,896]{1,0:T(8,128)} %get-tuple-element.205), channel_id=1, source_target_pairs={{0,96},{2,6},{4,100},{6,2},{8,104},{10,14},{12,108},{14,10},{32,64... | collective-permute-start | bytes 1376264 | tf_op jit(solution)/shard_map/ppermute | solution.py:711
  262.5 47.1 %collective-permute-start.23 = (f32[256,1024]{1,0:T(8,128)S(1)}, f32[256,1024]{1,0:T(8,128)S(1)}, u32[]{:S(2)}, u32[]{:S(2)}) collective-permute-start(f32[256,1024]{1,0:T(8,128)S(1)} %copy-done.4), channel_id=1, source_target_pairs={{0,1},{1,0},{2,3},{3,2},{4,5},{5,4},{6,7},{7,6},{8,9},{9,8},{10,11... | collective-permute-start | bytes 3145736 | tf_op jit(solution)/shard_map/ppermute | solution.py:675
  271.9 24.3 %collective-permute-start.30 = (f32[256,768]{1,0:T(8,128)}, f32[256,768]{1,0:T(8,128)}, u32[]{:S(2)}, u32[]{:S(2)}) collective-permute-start(f32[256,768]{1,0:T(8,128)} %get-tuple-element.187.refs_3_), channel_id=1, source_target_pairs={{0,96},{2,6},{4,100},{6,2},{8,104},{10,14},{12,108},{14,10},{32,64... | collective-permute-start | bytes 2359304 | tf_op jit(solution)/shard_map/ppermute | solution.py:711
  274.6 19.2 %collective-permute-start.45 = (f32[64,3072]{1,0:T(8,128)S(1)}, f32[64,3072]{1,0:T(8,128)S(1)}, u32[]{:S(2)}, u32[]{:S(2)}) collective-permute-start(f32[64,3072]{1,0:T(8,128)S(1)} %get-tuple-element.195), channel_id=1, source_target_pairs={{0,96},{2,6},{4,100},{6,2},{8,104},{10,14},{12,108},{14,10},{32,64... | collective-permute-start | bytes 2359304 | tf_op jit(solution)/shard_map/ppermute | solution.py:711
  280.6 15.6 %copy-start.5 = (f32[256,896]{1,0:T(8,128)S(1)}, f32[256,896]{1,0:T(8,128)}, u32[]{:S(2)}) copy-start(f32[256,896]{1,0:T(8,128)} %get-tuple-element.183.refs_2_) | copy-start | bytes 2752516
  280.6 17.4 %copy-start.16 = (f32[256,768]{1,0:T(8,128)S(1)}, f32[256,768]{1,0:T(8,128)}, u32[]{:S(2)}) copy-start(f32[256,768]{1,0:T(8,128)} %get-tuple-element.186) | copy-start | bytes 2359300
  293.7 13.2 %collective-permute-start.43 = (f32[64,3072]{1,0:T(8,128)S(1)}, f32[64,3072]{1,0:T(8,128)S(1)}, u32[]{:S(2)}, u32[]{:S(2)}) collective-permute-start(f32[64,3072]{1,0:T(8,128)S(1)} %get-tuple-element.189), channel_id=1, source_target_pairs={{0,12},{2,34},{4,8},{6,38},{8,4},{10,42},{12,0},{14,46},{32,44},{3... | collective-permute-start | bytes 2359304 | tf_op jit(solution)/shard_map/ppermute | solution.py:711
  296.2 20.6 %collective-permute-start.29 = (f32[256,896]{1,0:T(8,128)S(1)}, f32[256,896]{1,0:T(8,128)S(1)}, u32[]{:S(2)}, u32[]{:S(2)}) collective-permute-start(f32[256,896]{1,0:T(8,128)S(1)} %copy-done.5), channel_id=1, source_target_pairs={{0,12},{2,34},{4,8},{6,38},{8,4},{10,42},{12,0},{14,46},{32,44},{3... | collective-permute-start | bytes 2752520 | tf_op jit(solution)/shard_map/ppermute | solution.py:711
  306.9 15.8 %collective-permute-start.35 = (f32[128,768]{1,0:T(8,128)}, f32[128,768]{1,0:T(8,128)}, u32[]{:S(2)}, u32[]{:S(2)}) collective-permute-start(f32[128,768]{1,0:T(8,128)} %get-tuple-element.213), channel_id=1, source_target_pairs={{0,12},{2,34},{4,8},{6,38},{8,4},{10,42},{12,0},{14,46},{32,44},{3... | collective-permute-start | bytes 1179656 | tf_op jit(solution)/shard_map/ppermute | solution.py:711
  309.5 8.7 %copy-start = (f32[256,1024]{1,0:T(8,128)}, f32[256,1024]{1,0:T(8,128)S(1)}, u32[]{:S(2)}) copy-start(f32[256,1024]{1,0:T(8,128)S(1)} %collective-permute-done.23.refs_0_) | copy-start | bytes 3145732
  309.5 17.6 %collective-permute-start.46 = (f32[32,3072]{1,0:T(8,128)}, f32[32,3072]{1,0:T(8,128)}, u32[]{:S(2)}, u32[]{:S(2)}) collective-permute-start(f32[32,3072]{1,0:T(8,128)} %get-tuple-element.209), channel_id=1, source_target_pairs={{0,12},{2,34},{4,8},{6,38},{8,4},{10,42},{12,0},{14,46},{32,44},{3... | collective-permute-start | bytes 1179656 | tf_op jit(solution)/shard_map/ppermute | solution.py:711
  317.7 12.8 %collective-permute-start.44 = (f32[32,3072]{1,0:T(8,128)}, f32[32,3072]{1,0:T(8,128)}, u32[]{:S(2)}, u32[]{:S(2)}) collective-permute-start(f32[32,3072]{1,0:T(8,128)} %get-tuple-element.207), channel_id=1, source_target_pairs={{0,96},{2,6},{4,100},{6,2},{8,104},{10,14},{12,108},{14,10},{32,64... | collective-permute-start | bytes 1179656 | tf_op jit(solution)/shard_map/ppermute | solution.py:711
  322.7 13.3 %collective-permute-start.31 = (f32[128,896]{1,0:T(8,128)S(1)}, f32[128,896]{1,0:T(8,128)S(1)}, u32[]{:S(2)}, u32[]{:S(2)}) collective-permute-start(f32[128,896]{1,0:T(8,128)S(1)} %get-tuple-element.203), channel_id=1, source_target_pairs={{0,96},{2,6},{4,100},{6,2},{8,104},{10,14},{12,108},{14,10},{32,64... | collective-permute-start | bytes 1376264 | tf_op jit(solution)/shard_map/ppermute | solution.py:711
  327.1 10.2 %collective-permute-start.37 = (f32[64,1536]{1,0:T(8,128)S(1)}, f32[64,1536]{1,0:T(8,128)S(1)}, u32[]{:S(2)}, u32[]{:S(2)}) collective-permute-start(f32[64,1536]{1,0:T(8,128)S(1)} %get-tuple-element.211), channel_id=1, source_target_pairs={{0,4},{2,98},{4,0},{6,102},{8,12},{10,106},{12,8},{14,110},{32,36}... | collective-permute-start | bytes 1179656 | tf_op jit(solution)/shard_map/ppermute | solution.py:711
  331.6 5.5 %copy-start.17 = (f32[128,896]{1,0:T(8,128)S(1)}, f32[128,896]{1,0:T(8,128)}, u32[]{:S(2)}) copy-start(f32[128,896]{1,0:T(8,128)} %get-tuple-element.204) | copy-start | bytes 1376260
  331.6 9.4 %collective-permute-start.47 = (f32[16,6144]{1,0:T(8,128)S(1)}, f32[16,6144]{1,0:T(8,128)S(1)}, u32[]{:S(2)}, u32[]{:S(2)}) collective-permute-start(f32[16,6144]{1,0:T(8,128)S(1)} %pad_maximum_fusion.6), channel_id=1, source_target_pairs={{0,16},{16,0},{1,17},{17,1},{2,18},{18,2},{3,19},{19,3},{4,20},{20... | collective-permute-start | bytes 1179656 | tf_op jit(solution)/shard_map/ppermute | solution.py:736
  337.2 8.6 %collective-permute-start.33 = (f32[64,1792]{1,0:T(8,128)S(1)}, f32[64,1792]{1,0:T(8,128)S(1)}, u32[]{:S(2)}, u32[]{:S(2)}) collective-permute-start(f32[64,1792]{1,0:T(8,128)S(1)} %get-tuple-element.201), channel_id=1, source_target_pairs={{0,32},{2,14},{4,36},{6,10},{8,40},{10,6},{12,44},{14,2},{32,0},{3... | collective-permute-start | bytes 1376264 | tf_op jit(solution)/shard_map/ppermute | solution.py:711
  337.4 10.5 %collective-permute-start.38 = (f32[32,1536]{1,0:T(8,128)S(1)}, f32[32,1536]{1,0:T(8,128)S(1)}, u32[]{:S(2)}, u32[]{:S(2)}) collective-permute-start(f32[32,1536]{1,0:T(8,128)S(1)} %get-tuple-element.225), channel_id=1, source_target_pairs={{0,32},{2,14},{4,36},{6,10},{8,40},{10,6},{12,44},{14,2},{32,0},{3... | collective-permute-start | bytes 589832 | tf_op jit(solution)/shard_map/ppermute | solution.py:711
  345.9 6.1 %collective-permute-start.34 = (f32[32,1792]{1,0:T(8,128)S(1)}, f32[32,1792]{1,0:T(8,128)S(1)}, u32[]{:S(2)}, u32[]{:S(2)}) collective-permute-start(f32[32,1792]{1,0:T(8,128)S(1)} %get-tuple-element.219), channel_id=1, source_target_pairs={{0,4},{2,98},{4,0},{6,102},{8,12},{10,106},{12,8},{14,110},{32,36}... | collective-permute-start | bytes 688136 | tf_op jit(solution)/shard_map/ppermute | solution.py:711
  352.0 7.4 %collective-permute-start.39 = (f32[16,3328]{1,0:T(8,128)S(1)}, f32[16,3328]{1,0:T(8,128)S(1)}, u32[]{:S(2)}, u32[]{:S(2)}) collective-permute-start(f32[16,3328]{1,0:T(8,128)S(1)} %pad_maximum_fusion.7), channel_id=1, source_target_pairs={{0,16},{16,0},{1,17},{17,1},{2,18},{18,2},{3,19},{19,3},{4,20},{20... | collective-permute-start | bytes 638984 | tf_op jit(solution)/shard_map/ppermute | solution.py:736
  362.3 3.6 collective-permute-start.40
  (22 other events, 45.9 us)

commit v2 on v1

--- a/solution.py
+++ b/solution.py
@@ -568,7 +568,7 @@
         rest = rest[4:]
     g_out, part_out, keep, send = rest[count : count + 4]
     rows_scratch = rest[-1]
-    first, second = (block_places(ATTENTION_ORDERS, places, later) for later in (False, True))
+    where_to = block_places(ATTENTION_ORDERS, places)
     length = middle.shape[0]
     lane = lane_of(length)
     shares = share[...]
@@ -612,13 +612,10 @@
     )
     a_full = a[...]
     column = 0
-    query_grad, key_grad, value_grad = grads
-    for total, where_to in (
-        (jnp.transpose(rows_scratch[...]), first),
-        (mm_tn(a_full, query_grad), first),
-        (mm_tn(a_full, key_grad), first),
-        (mm_tn(a_full, value_grad), second),
-        (mm_tn(output_grad, mix[...]), second),
+    for total in (
+        jnp.transpose(rows_scratch[...]),
+        *(mm_tn(a_full, grad) for grad in grads),
+        mm_tn(output_grad, mix[...]),
     ):
         store_blocks(keep, send, total, column, where_to)
         column += total.shape[1]
@@ -691,49 +688,118 @@
     return pairs
 
 
-class Scatter:
-    def __init__(self, keep, send, orders, column):
-        received = lax.ppermute(send, "dp_3", SWAP)
-        self.orders = (orders, crossed(orders))
-        self.parts = [
-            [array[:, :column] for array in (keep, received)],
-            [array[:, column:] for array in (keep, received)],
-        ]
-        self.step = 0
-
-    def halve(self):
-        half = self.parts[0][0].shape[0] // 2
-        self.kept = [first[:half] + second[:half] for first, second in self.parts]
-        return [first[half:] + second[half:] for first, second in self.parts]
-
-    def move(self, sends):
-        moved = [
-            lax.ppermute(send, RING_AXES, ring_pairs(orders, self.step))
-            for send, orders in zip(sends, self.orders)
-        ]
-        self.parts = [list(pair) for pair in zip(self.kept, moved)]
-        self.step += 1
-
-    def received(self):
-        return [second for _, second in self.parts]
-
-    def hold(self, *after):
-        for pair, second in zip(self.parts, behind(self.received(), *after)):
-            pair[1] = second
-
-    def advance(self, count=1):
-        for _ in range(count):
-            self.move(self.halve())
-
-    def join(self, other):
-        self.parts = [
-            [jnp.concatenate(pair, axis=1) for pair in zip(*both)]
-            for both in zip(self.parts, other.parts)
-        ]
-
-    def finish(self):
-        sends = jnp.concatenate(self.halve(), axis=-1)
-        return jnp.concatenate(self.kept, axis=-1) + lax.ppermute(sends, "dp_1", SWAP)
+def halve_kernel(groups, rows, *refs):
+    count = sum(len(terms) for streams in groups for terms, _ in streams)
+    ins, outs = iter(refs[:count]), iter(refs[count:])
+    for streams in groups:
+        kept, sent = next(outs), next(outs)
+        column = 0
+        for terms, width in streams:
+            total = next(ins)[...]
+            for _ in terms[1:]:
+                total = total + next(ins)[...]
+            kept[:, column : column + width] = total[: rows // 2]
+            sent[:, column : column + width] = total[rows // 2 :]
+            column += width
+
+
+def halve(rows, *groups):
+    plan, ins, in_specs, outs = [], [], [], []
+    for streams in groups:
+        plan.append([])
+        for terms in streams:
+            width = min((term[0] if isinstance(term, tuple) else term).shape[1] for term in terms)
+            for term in terms:
+                array, at = term if isinstance(term, tuple) else (term, 0)
+                ins.append(array)
+                in_specs.append(
+                    pl.BlockSpec((rows, width), lambda i, at=at: (0, at), pipeline_mode=ONCE)
+                )
+            plan[-1].append((terms, width))
+        outs += [(rows // 2, sum(width for _, width in plan[-1]))] * 2
+    found = pl.pallas_call(
+        functools.partial(halve_kernel, plan, rows),
+        grid=(1,),
+        in_specs=in_specs,
+        out_specs=[whole(shape) for shape in outs],
+        out_shape=[jax.ShapeDtypeStruct(shape, F32) for shape in outs],
+        compiler_params=params(60),
+        cost_estimate=cost(1 << 20, 8 * MIB),
+        name="halve",
+    )(*ins)
+    return [list(found[at : at + 2]) for at in range(0, len(found), 2)]
+
+
+def move(send, orders, step):
+    return lax.ppermute(send, RING_AXES, ring_pairs(orders, step))
+
+
+def both_streams(sends, step):
+    return [
+        move(send, orders, step) for send, orders in zip(sends, (EXPERT_ORDERS, crossed(EXPERT_ORDERS)))
+    ]
+
+
+def begin_experts(keep, received):
+    half, width = keep.shape[0] // 2, keep.shape[1] // 2
+    return [
+        keep[half:, at : at + width] + received[half:, at : at + width] for at in (0, width)
+    ]
+
+
+def expert_streams(keep, received, moved):
+    return [[[(keep, at), (received, at), moved[at]]] for at in range(2)]
+
+
+def turned(block):
+    rows, columns = block.shape
+    filled = jnp.concatenate([block, jnp.zeros((LANES - rows, columns), F32)], axis=0)
+    return jnp.transpose(filled)[:, :rows]
+
+
+def unpack_kernel(
+    layers, experts, kept, moved, small, query, key, value, projection, gate, up, down
+):
+    hidden = gate.shape[-1]
+    total = kept[...] + moved[...]
+    column = 0
+    for stream in range(2):
+        for layer in range(layers):
+            for at in range(experts // 2):
+                expert = stream * (experts // 2) + at
+                gate[layer, expert] = total[:, column : column + hidden]
+                up[layer, expert] = total[:, column + hidden : column + 2 * hidden]
+                down[layer, expert] = turned(total[:, column + 2 * hidden : column + 3 * hidden])
+                column += 3 * hidden
+    for layer in range(layers):
+        for out in (small, query, key, value):
+            width = out.shape[-1]
+            out[layer] = total[:, column : column + width]
+            column += width
+        width = projection.shape[1]
+        projection[layer] = turned(total[:, column : column + width])
+        column += width
+
+
+def unpack_sums(kept, moved, layers, experts, hidden, widths, depth):
+    rows = kept.shape[0]
+    outs = [
+        (layers, rows, SMALL),
+        *((layers, rows, width) for width in widths),
+        (layers, depth, rows),
+        (layers, experts, rows, hidden),
+        (layers, experts, rows, hidden),
+        (layers, experts, hidden, rows),
+    ]
+    return pl.pallas_call(
+        functools.partial(unpack_kernel, layers, experts),
+        grid=(1,),
+        in_specs=[whole(kept.shape)] * 2,
+        out_specs=[whole(shape) for shape in outs],
+        out_shape=[jax.ShapeDtypeStruct(shape, F32) for shape in outs],
+        compiler_params=params(60),
+        name="unpack_sums",
+    )(kept, moved)
 
 
 class Gather:
@@ -849,12 +915,11 @@
         1, expert_places, x2, part, part_other, gain_experts, router, mask, *expert_weights,
         cotangent,
     )
-    half = keep.shape[1] // 2
-    split = SMALL + query_weight.shape[2] + key_matrix.shape[2]
-    sum_e2 = Scatter(keep, send, EXPERT_ORDERS, half)
+    half = features // 4
+    keep_e2, received_e2 = keep, lax.ppermute(send, "dp_3", SWAP)
     other = exchange(back)
-    *sends, last = behind([*sum_e2.halve(), last], other)
-    sum_e2.move(sends)
+    *sends, last = behind([*begin_experts(keep_e2, received_e2), last], other)
+    moved = both_streams(sends, 0)
     last_other = exchange(last)
     no_gain = jnp.zeros((8, features), F32)
     g2, part, keep, send, part_other = attention_backward(
@@ -862,72 +927,85 @@
         (x2, *saved2), tables, segment, no_gain, sends,
         (q_other, kk_other, vv_other, weights_other),
     )
-    sum_a2 = Scatter(keep, send, ATTENTION_ORDERS, split)
-    sends = sum_e2.halve()
+    keep_a2, received_a2 = keep, lax.ppermute(send, "dp_3", SWAP)
+    held_e2 = halve(half, *expert_streams(keep_e2, received_e2, moved))
+    sends = [send for _, send in held_e2]
     g1, late_gain, back, keep, send = expert_backward(
         0, expert_places, g2, x2, gain_attention, part, part_other, xi1, share1, gate1,
         linear1, *expert_weights, [*sends, last_other],
     )
-    sum_e2.move(sends)
-    sum_e1 = Scatter(keep, send, EXPERT_ORDERS, half)
+    moved_e2 = both_streams(sends, 1)
+    keep_e1, received_e1 = keep, lax.ppermute(send, "dp_3", SWAP)
     other = exchange(back)
-    sends_a, sends_e = sum_a2.halve(), sum_e1.halve()
-    sum_a2.move(sends_a)
-    sum_e1.move(sends_e)
+    send_a2 = keep_a2[half:] + received_a2[half:]
+    moved_a2 = move(send_a2, ATTENTION_ORDERS, 0)
+    sends = begin_experts(keep_e1, received_e1)
+    moved_e1 = both_streams(sends, 0)
     g0, part, keep, send = attention_backward(
         0, attention_places, g1, back, other, (middle1, xi1, share1), back_weights,
-        (x1, *saved1), tables, segment, late_gain, sends_a + sends_e + sum_e2.received(),
-    )
-    (send,) = behind([send], *sum_a2.received(), *sum_e1.received())
-    sum_a1 = Scatter(keep, send, ATTENTION_ORDERS, split)
-    sends = sum_a1.halve()
-    sum_a1.move(sends)
-    (other,) = behind([exchange(part)], *sum_a1.received())
-    sum_a1.advance()
-    sum_a2.advance()
-    sum_e1.advance()
-    sum_e1.hold(*sends)
-    sum_e1.join(sum_e2)
-    sum_e1.advance(2)
-    sum_a1.join(sum_a2)
-    sum_a1.advance(2)
-    sums = (sum_a1, sum_e1)
+        (x1, *saved1), tables, segment, late_gain, [send_a2, *sends, *moved_e2],
+    )
+    (send,) = behind([send], moved_a2, *moved_e1)
+    keep_a1, received_a1 = keep, lax.ppermute(send, "dp_3", SWAP)
+    *held_e1, held_a2 = halve(
+        half, *expert_streams(keep_e1, received_e1, moved_e1), [[keep_a2, received_a2, moved_a2]]
+    )
+    sends = [send for _, send in held_e1]
+    moved_e1 = both_streams(sends, 1)
+    moved_a2 = move(held_a2[1], ATTENTION_ORDERS, 1)
+    (received_a1,) = behind([received_a1], *sends)
+    ((kept_a1, send),) = halve(2 * half, [[keep_a1, received_a1]])
+    moved_a1 = move(send, ATTENTION_ORDERS, 0)
+    moved_e1 = behind(moved_e1, send)
+    held_e = halve(
+        half // 2,
+        *(
+            [[one[0], first], [two[0], second]]
+            for one, first, two, second in zip(held_e1, moved_e1, held_e2, moved_e2)
+        ),
+    )
+    sends = [send for _, send in held_e]
+    moved_e = both_streams(sends, 2)
+    other = exchange(part)
+    (moved_a1,) = behind([moved_a1], *sends, other)
+    (held_a1,) = halve(half, [[kept_a1, moved_a1]])
+    moved_a1 = move(held_a1[1], ATTENTION_ORDERS, 1)
+    held_e = halve(half // 4, *([[held[0], moved]] for held, moved in zip(held_e, moved_e)))
+    sends = [send for _, send in held_e]
+    moved_e = both_streams(sends, 3)
+    (moved_a1,) = behind([moved_a1], *sends)
+    (held_a,) = halve(half // 2, [[held_a1[0], moved_a1], [held_a2[0], moved_a2]])
+    moved_a = move(held_a[1], ATTENTION_ORDERS, 2)
+    (other,) = behind([other], moved_a)
+    (held_a,) = halve(half // 4, [[held_a[0], moved_a]])
+    moved_a = move(held_a[1], ATTENTION_ORDERS, 3)
+    ((kept, send),) = halve(
+        half // 8,
+        [*([held[0], moved] for held, moved in zip(held_e, moved_e)), [held_a[0], moved_a]],
+    )
+    widths = (query_weight.shape[2], key_matrix.shape[2], value_matrix.shape[2])
+    sums = unpack_sums(
+        kept, lax.ppermute(send, "dp_1", SWAP), query_weight.shape[0], experts, hidden, widths,
+        output_weight.shape[1],
+    )
     gain = norm_attention[0].astype(F32)
     change, _ = norm_back(x1, row_factor(x1), gain, part + other)
     gradient = g0 + change
     output = (middle2 + (last + last_other)).astype(BF16)
-    blocks = [one.finish() for one in sums]
-
-    attention_sums, expert_sums = blocks
-    rows = attention_sums.shape[0]
-    layers = query_weight.shape[0]
-    bounds = np.cumsum([0, SMALL, query_weight.shape[2], key_matrix.shape[2]])
-    more_bounds = np.cumsum([0, value_matrix.shape[2], output_weight.shape[1]])
-    one, two = (
-        jnp.swapaxes(columns.reshape(rows, layers, -1), 0, 1)
-        for columns in (attention_sums[:, : layers * split], attention_sums[:, layers * split :])
-    )
-    attention_sums = [one[..., a:b] for a, b in zip(bounds[:-1], bounds[1:])]
-    attention_sums += [two[..., a:b] for a, b in zip(more_bounds[:-1], more_bounds[1:])]
-    expert_sums = expert_sums.reshape(rows, 2, layers, experts // 2, 3, hidden)
-    expert_sums = [
-        expert_sums[..., kind, :].transpose(2, 1, 3, 0, 4).reshape(layers, experts, rows, hidden)
-        for kind in range(3)
-    ]
-    small = attention_sums[0]
+
+    small, *attention_sums, gate_sum, up_sum, down_sum = sums
     attention_gain = small[:, :, 5]
     attention_gain = attention_gain + exchange(attention_gain)
     return (
         output,
         gradient,
         attention_gain,
-        *attention_sums[1:4],
-        jnp.swapaxes(attention_sums[4], 1, 2),
+        *attention_sums,
         small[:, :, 4],
         small[:, :, :experts],
-        expert_sums[0],
-        expert_sums[1],
-        jnp.swapaxes(expert_sums[2], 2, 3),
+        gate_sum,
+        up_sum,
+        down_sum,
     )
 
 

time: 374 us -> 413 us (1.10)
  Pallas kernels: 95.5 us -> 136 us
  waiting for transfers between devices: 119 us -> 152 us
  other arithmetic: 46.7 us -> 21.2 us
  starting transfers between devices: 74.4 us -> 62.5 us
    pallas_call x0 -> x10, Pallas kernels: none -> 40.5 us  [the longest x9 37.6 us: halve(): pl.pallas_call(functools.partial(halve_kernel, plan, rows), grid=(1,), in...]
    ppermute x30 -> x23, waiting for transfers between devices: 68.9 us -> 100 us  [the longest x18 70.6 us: move(): return lax.ppermute(send, RING_AXES, ring_pairs(orders, step))]
    add x28 -> x3, other arithmetic: 37.5 us -> 13 us  [the longest x2 11.4 us: begin_experts(): keep[half:, at:at + width] + received[half:, at:at + width]]
    ppermute x30 -> x23, starting transfers between devices: 50.6 us -> 38.8 us  [the longest x18 31.9 us: move(): return lax.ppermute(send, RING_AXES, ring_pairs(orders, step))]
    unnamed x80 -> x76, local copies, waits for them, and re-layouts: 11.9 us -> 22.7 us
    concatenate x4 -> x0, local copies, waits for them, and re-layouts: 4.5 us -> none  [join(): jnp.concatenate(pair, axis=1)]
  transfers between devices with their start and end apart: 48 -> 41, of which waited for: 23 -> 19; matrix products, arithmetic and copies ran while one was open for 18% -> 8% of each run, Pallas kernels for 14% -> 18%
where the time goes in v2:
time: 413 us; the launch traced here: 406 us
  waiting for transfers between devices  152 us (37%)
  Pallas kernels  136 us (33%)
  starting transfers between devices  62.5 us (15%)
  local copies, waits for them, and re-layouts  32.4 us (8%)
  other arithmetic  21.2 us (5%)
    ppermute x18, waiting for transfers between devices, move(): return lax.ppermute(send, RING_AXES, ring_pairs(orders, step))  70.6 us
    pallas_call x9, Pallas kernels, halve(): pl.pallas_call(functools.partial(halve_kernel, plan, rows), grid=(1,), in...  37.6 us
    pallas_call x2, Pallas kernels, attention_backward(): pl.pallas_call(functools.partial(attention_backward_kernel, len(after), b...  36.6 us
    ppermute x8, waiting for transfers between devices, exchange(): return lax.ppermute(array, 'tensor', SWAP)  36.4 us
    pallas_call x3, Pallas kernels, run_experts(): pl.pallas_call(kernel, grid=(STREAMS,), in_specs=in_specs, out_specs=[spe...  36.2 us
    ppermute x18, starting transfers between devices, move(): return lax.ppermute(send, RING_AXES, ring_pairs(orders, step))  31.9 us
    unnamed x76, local copies, waits for them, and re-layouts  22.7 us
    pallas_call x2, Pallas kernels, attention_forward(): pl.pallas_call(functools.partial(attention_forward_kernel, len(parts), bo...  22.7 us
  transfers between devices with their start and end apart: 41, of which 19 were waited for; matrix products, arithmetic and copies ran while one was open for 8% of the time, Pallas kernels for 18%

profile of v2, /device:TPU:0, one launch (start us, length us, event | category | flops | bytes accessed | tf_op | source)
XLA Modules:
  0.0 405.5 jit_solution(10029292644908620010)
XLA Ops:
  2.5 1.7 collective-permute-start.2
  5.7 6.6 %attention_forward.2 = (f32[256,1024]{1,0:T(8,128)}, bf16[256,1024]{1,0:T(8,128)(2,1)}, bf16[256,512]{1,0:T(8,128)(2,1)}, bf16[4,256,128]{2,1,0:T(8,128)(2,1)}, ...) custom-call(bf16[256,1024]{1,0:T(8,128)(2,1)} %refs_0_.1, ...), custom_call_target="tpu_custom_call" | custom-call | flops 6442450944 | bytes 8388608 | tf_op jit(solution)/shard_map/attention_forward/pallas_call | solution.py:286
  13.0 2.8 collective-permute-start.3
  16.2 3.9 collective-permute-done.3
  21.1 4.1 %collective-permute-start.4 = (f32[96,1024]{1,0:T(8,128)S(1)}, f32[96,1024]{1,0:T(8,128)S(1)}, u32[]{:S(2)}, u32[]{:S(2)}) collective-permute-start(f32[96,1024]{1,0:T(8,128)S(1)} %pad_maximum_fusion.1), channel_id=1, source_target_pairs={{0,12},{2,34},{4,8},{6,38},{8,4},{10,42},{12,0},{14,46},{32,44},{3... | collective-permute-start | bytes 1179656 | tf_op jit(solution)/shard_map/ppermute | solution.py:825
  27.9 3.0 collective-permute-done.4
  32.0 7.5 %collective-permute-done.other.refs_2_ = f32[256,1024]{1,0:T(8,128)S(1)} collective-permute-done((f32[256,1024]{1,0:T(8,128)}, f32[256,1024]{1,0:T(8,128)S(1)}, u32[]{:S(2)}, u32[]{:S(2)}) %collective-permute-start) | collective-permute-done | bytes 1048608 | tf_op jit(solution)/shard_map/ppermute | solution.py:672
  42.3 7.9 %experts_forward.1 = (f32[256,1024]{1,0:T(8,128)}, bf16[256,1024]{1,0:T(8,128)(2,1)}, f32[256,128]{1,0:T(8,128)}, f32[4,256,256]{2,1,0:T(8,128)}, f32[4,256,256]{2,1,0:T(8,128)}, /*index=5*/f32[256,1024]{1,0:T(8,128)}) custom-call(f32[256,1024]{1,0:T(8,128)} %get-tuple-element.103.x, f32[256,1024]{1,0:T(8,128)} %get-tuple-element.104.own.refs_1_, ...), custom_call_target="tpu_custom_call" | custom-call | flops 8589934592 | bytes 12582912 | tf_op jit(solution)/shard_map/experts_forward/pallas_call | solution.py:433
  53.1 1.8 collective-permute-start.8
  56.2 8.4 %collective-permute-done.7.refs_15_ = f32[384,512]{1,0:T(8,128)} collective-permute-done((f32[384,512]{1,0:T(8,128)S(1)}, f32[384,512]{1,0:T(8,128)}, u32[]{:S(2)}, u32[]{:S(2)}) %collective-permute-start.7) | collective-permute-done | bytes 786464 | tf_op jit(solution)/shard_map/ppermute | solution.py:833
  65.9 2.3 collective-permute-start.12
  69.4 11.5 %collective-permute-done.1.refs_2_ = f32[256,1024]{1,0:T(8,128)} collective-permute-done((f32[256,1024]{1,0:T(8,128)S(1)}, f32[256,1024]{1,0:T(8,128)}, u32[]{:S(2)}, u32[]{:S(2)}) %collective-permute-start.1) | collective-permute-done | bytes 1048608 | tf_op jit(solution)/shard_map/ppermute | solution.py:672
  81.0 16.1 %attention_forward.3 = (f32[256,1024]{1,0:T(8,128)}, bf16[256,1024]{1,0:T(8,128)(2,1)}, bf16[256,512]{1,0:T(8,128)(2,1)}, bf16[4,256,128]{2,1,0:T(8,128)(2,1)}, ...) custom-call(f32[256,1024]{1,0:T(8,128)} %get-tuple-element.105.refs_, ...), custom_call_target="tpu_custom_call" | custom-call | flops 6442450944 | bytes 8388608 | tf_op jit(solution)/shard_map/attention_forward/pallas_call | solution.py:286
  97.1 14.7 %experts_both.1 = (f32[256,1024]{1,0:T(8,128)}, bf16[256,1024]{1,0:T(8,128)(2,1)}, f32[256,128]{1,0:T(8,128)}, f32[256,1024]{1,0:T(8,128)}, f32[256,1152]{1,0:T(...) custom-call(s32[5]{0:T(128)} %stack.47.places, f32[256,1024]{1,0:T(8,128)} %get-tuple-element.111.x, ...), custom_call_target="tpu_custom_call" | custom-call | flops 17179869184 | bytes 31457280 | tf_op jit(solution)/shard_map/experts_both/pallas_call | solution.py:433
  113.6 8.8 %collective-permute-done.13.refs_1_.refs_4_ = f32[512,3072]{1,0:T(8,128)} collective-permute-done((f32[512,3072]{1,0:T(8,128)}, f32[512,3072]{1,0:T(8,128)}, u32[]{:S(2)}, u32[]{:S(2)}) %collective-permute-start.13) | collective-permute-done | bytes 6291488 | tf_op jit(solution)/shard_map/ppermute | solution.py:919
  122.4 5.1 %slice_add_fusion.3 = (f32[256,1536]{1,0:T(8,128)}, f32[256,1536]{1,0:T(8,128)}) fusion(f32[512,3072]{1,0:T(8,128)} %collective-permute-done.13.refs_1_.refs_4_, f32[512,3072]{1,0:T(8,128)} %get-tuple-element.115.refs_0_.refs_3_), kind=kLoop, calls=%fused_computation.3 | loop fusion | flops 786432 | bytes 9437184 | tf_op jit(solution)/shard_map/add | solution.py:746
  127.5 13.0 %collective-permute-done.14.refs_3_.other = f32[256,1152]{1,0:T(8,128)S(1)} collective-permute-done((f32[256,1152]{1,0:T(8,128)}, f32[256,1152]{1,0:T(8,128)S(1)}, u32[]{:S(2)}, u32[]{:S(2)}) %collective-permute-start.14) | collective-permute-done | bytes 1179680 | tf_op jit(solution)/shard_map/ppermute | solution.py:672
  142.4 11.9 %collective-permute-start.17 = (f32[256,1536]{1,0:T(8,128)}, f32[256,1536]{1,0:T(8,128)}, u32[]{:S(2)}, u32[]{:S(2)}) collective-permute-start(f32[256,1536]{1,0:T(8,128)} %get-tuple-element.132.rest_5_), channel_id=1, source_target_pairs={{0,4},{2,98},{4,0},{6,102},{8,12},{10,106},{12,8},{14,110},{32,36}... | collective-permute-start | bytes 4718600 | tf_op jit(solution)/shard_map/ppermute | solution.py:734
  154.9 21.5 %attention_backward.2 = (f32[256,1024]{1,0:T(8,128)}, f32[256,1024]{1,0:T(8,128)}, f32[512,1664]{1,0:T(8,128)}, f32[512,1664]{1,0:T(8,128)}, f32[256,1024]{1,0:T(8,128)}) custom-call(s32[5]{0:T(128)} %stack.53.places, bf16[256,1024]{1,0:T(8,128)(2,1)} %g.1, f32[256,1152]{1,0:T(8,128)} %get-tuple-element.118.own, f32[256,1152]{1,0:T(8,128)} %copy-done.20, ...), custom_call_target="tpu_custom_call" | custom-call | flops 17179869184 | bytes 18874368 | tf_op jit(solution)/shard_map/attention_backward/pallas_call | solution.py:652
  177.6 5.8 %halve.9 = (f32[128,1536]{1,0:T(8,128)}, f32[128,1536]{1,0:T(8,128)}, f32[128,1536]{1,0:T(8,128)}, f32[128,1536]{1,0:T(8,128)}) custom-call(f32[512,3072]{1,0:T(8,128)} %get-tuple-element.115.refs_0_.refs_3_, f32[512,3072]{1,0:T(8,128)} %collective-permute-done.13.refs_1_.refs_4_, f32[256,1536]{1,0:T(8,128)} %copy-done.19, ...), custom_call_target="tpu_custom_call" | custom-call | flops 1048576 | bytes 8388608 | tf_op jit(solution)/shard_map/halve/pallas_call | solution.py:720
  184.3 13.5 %experts_backward.1 = (f32[256,1024]{1,0:T(8,128)}, f32[8,1024]{1,0:T(8,128)}, f32[256,1152]{1,0:T(8,128)}, f32[512,3072]{1,0:T(8,128)}, f32[512,3072]{1,0:T(8,128)}) custom-call(s32[5]{0:T(128)} %stack.47.places, f32[256,1024]{1,0:T(8,128)} %get-tuple-element.133.g_in, f32[256,1024]{1,0:T(8,128)} %get-tuple-element.111.x, ...), custom_call_target="tpu_custom_call" | custom-call | flops 4294967296 | bytes 31457280 | tf_op jit(solution)/shard_map/experts_backward/pallas_call | solution.py:433
  197.8 2.2 collective-permute-start.20
  201.7 1.6 collective-permute-start.18
  203.3 11.6 %collective-permute-done.19.refs_7_ = f32[512,1664]{1,0:T(8,128)S(1)} collective-permute-done((f32[512,1664]{1,0:T(8,128)}, f32[512,1664]{1,0:T(8,128)S(1)}, u32[]{:S(2)}, u32[]{:S(2)}) %collective-permute-start.19) | collective-permute-done | bytes 3407904 | tf_op jit(solution)/shard_map/ppermute | solution.py:930
  214.8 1.6 slice_add_fusion.rest_0_
  217.1 1.9 collective-permute-start.24
  219.0 6.4 %slice_add_fusion.1 = (f32[256,1536]{1,0:T(8,128)}, f32[256,1536]{1,0:T(8,128)}) fusion(f32[512,3072]{1,0:T(8,128)S(1)} %collective-permute-done.20.refs_1_.refs_4_, f32[512,3072]{1,0:T(8,128)} %get-tuple-element.152.refs_0_.refs_3_), kind=kLoop, calls=%fused_computation.1 | loop fusion | flops 786432 | bytes 9437184 | tf_op jit(solution)/shard_map/add | solution.py:746
  226.3 4.3 %collective-permute-done.18.other = f32[256,1152]{1,0:T(8,128)} collective-permute-done((f32[256,1152]{1,0:T(8,128)}, f32[256,1152]{1,0:T(8,128)}, u32[]{:S(2)}, u32[]{:S(2)}) %collective-permute-start.18) | collective-permute-done | bytes 1179680 | tf_op jit(solution)/shard_map/ppermute | solution.py:672
  230.6 15.1 %attention_backward.3 = (f32[256,1024]{1,0:T(8,128)}, f32[256,1024]{1,0:T(8,128)}, f32[512,1664]{1,0:T(8,128)}, f32[512,1664]{1,0:T(8,128)}) custom-call(s32[5]{0:T(128)} %stack.53.places, f32[256,1024]{1,0:T(8,128)} %get-tuple-element.142.g, f32[256,1152]{1,0:T(8,128)} %get-tuple-element.143.own, f32[256,1152]{1,0:T(8,128)} %collective-permute-done.18.other, ...), custom_call_target="tpu_custom_call" | custom-call | flops 17179869184 | bytes 18874368 | tf_op jit(solution)/shard_map/attention_backward/pallas_call | solution.py:652
  245.7 7.1 %collective-permute-done.24.refs_1_.refs_8_ = f32[256,1664]{1,0:T(8,128)S(1)} collective-permute-done((f32[256,1664]{1,0:T(8,128)}, f32[256,1664]{1,0:T(8,128)S(1)}, u32[]{:S(2)}, u32[]{:S(2)}) %collective-permute-start.24) | collective-permute-done | bytes 1703968 | tf_op jit(solution)/shard_map/ppermute | solution.py:734
  252.8 2.7 collective-permute-done.25.refs_2_
  256.6 1.6 collective-permute-start.27
  258.2 7.6 %halve.10 = (f32[128,1536]{1,0:T(8,128)}, f32[128,1536]{1,0:T(8,128)}, f32[128,1536]{1,0:T(8,128)}, f32[128,1536]{1,0:T(8,128)}, f32[128,1664]{1,0:T(8,128)}, /*index=5*/f32[128,1664]{1,0:T(8,128)}) custom-call(f32[512,3072]{1,0:T(8,128)} %get-tuple-element.152.refs_0_.refs_3_, f32[512,3072]{1,0:T(8,128)} %copy-done, f32[256,1536]{1,0:T(8,128)} %copy-done.8, ...), custom_call_target="tpu_custom_call" | custom-call | flops 1048576 | bytes 8388608 | tf_op jit(solution)/shard_map/halve/pallas_call | solution.py:720
  265.8 1.7 copy-done.3
  267.5 4.9 %halve.11 = (f32[256,1664]{1,0:T(8,128)}, f32[256,1664]{1,0:T(8,128)}) custom-call(f32[512,1664]{1,0:T(8,128)} %get-tuple-element.156.refs_0_, f32[512,1664]{1,0:T(8,128)} %behind.15.refs_1_), custom_call_target="tpu_custom_call" | custom-call | flops 1048576 | bytes 8388608 | tf_op jit(solution)/shard_map/halve/pallas_call | solution.py:720
  272.4 1.9 collective-permute-start.28
  274.3 1.6 collective-permute-start.23
  276.6 11.6 %collective-permute-done.29.refs_0_ = f32[128,1536]{1,0:T(8,128)S(1)} collective-permute-done((f32[128,1536]{1,0:T(8,128)}, f32[128,1536]{1,0:T(8,128)S(1)}, u32[]{:S(2)}, u32[]{:S(2)}) %collective-permute-start.29) | collective-permute-done | bytes 786464 | tf_op jit(solution)/shard_map/ppermute | solution.py:734
  288.1 8.6 %collective-permute-done.30.refs_1_ = f32[128,1536]{1,0:T(8,128)} collective-permute-done((f32[128,1536]{1,0:T(8,128)}, f32[128,1536]{1,0:T(8,128)}, u32[]{:S(2)}, u32[]{:S(2)}) %collective-permute-start.30) | collective-permute-done | bytes 786464 | tf_op jit(solution)/shard_map/ppermute | solution.py:734
  296.7 4.5 %halve.12 = (f32[64,3072]{1,0:T(8,128)}, f32[64,3072]{1,0:T(8,128)}, f32[64,3072]{1,0:T(8,128)}, f32[64,3072]{1,0:T(8,128)}) custom-call(f32[128,1536]{1,0:T(8,128)} %get-tuple-element.162.refs_0_, f32[128,1536]{1,0:T(8,128)} %get-tuple-element.163.refs_1_, f32[128,1536]{1,0:T(8,128)} %get-tuple-element.164.refs_2_, ...), custom_call_target="tpu_custom_call" | custom-call | flops 1048576 | bytes 8388608 | tf_op jit(solution)/shard_map/halve/pallas_call | solution.py:720
  301.3 2.8 collective-permute-done.28.refs_0_
  305.3 3.3 halve.13
  309.1 2.7 collective-permute-start.34
  311.8 1.9 collective-permute-start.32
  313.6 1.5 collective-permute-start.33
  315.2 10.0 %collective-permute-done.32.refs_1_ = f32[64,3072]{1,0:T(8,128)S(1)} collective-permute-done((f32[64,3072]{1,0:T(8,128)}, f32[64,3072]{1,0:T(8,128)S(1)}, u32[]{:S(2)}, u32[]{:S(2)}) %collective-permute-start.32) | collective-permute-done | bytes 786464 | tf_op jit(solution)/shard_map/ppermute | solution.py:734
  325.2 15.0 %collective-permute-done.33.refs_3_ = f32[64,3072]{1,0:T(8,128)S(1)} collective-permute-done((f32[64,3072]{1,0:T(8,128)}, f32[64,3072]{1,0:T(8,128)S(1)}, u32[]{:S(2)}, u32[]{:S(2)}) %collective-permute-start.33) | collective-permute-done | bytes 786464 | tf_op jit(solution)/shard_map/ppermute | solution.py:734
  341.1 3.0 halve.14
  345.9 3.4 halve.15
  350.8 3.0 collective-permute-start.37
  353.9 10.0 %collective-permute-done.35.refs_1_ = f32[64,3328]{1,0:T(8,128)S(1)} collective-permute-done((f32[64,3328]{1,0:T(8,128)}, f32[64,3328]{1,0:T(8,128)S(1)}, u32[]{:S(2)}, u32[]{:S(2)}) %collective-permute-start.35) | collective-permute-done | bytes 852000 | tf_op jit(solution)/shard_map/ppermute | solution.py:734
  364.8 2.4 halve.16
  367.2 1.7 collective-permute-start.38
  371.4 1.5 multiply_reduce_fusion.1
  373.0 2.7 collective-permute-done.38.refs_5_
  375.6 2.8 halve.17
  378.4 2.9 collective-permute-start.39
  381.3 2.5 subtract_add_fusion
  383.8 9.3 %collective-permute-done.39.moved = f32[16,9472]{1,0:T(8,128)} collective-permute-done((f32[16,9472]{1,0:T(8,128)}, f32[16,9472]{1,0:T(8,128)}, u32[]{:S(2)}, u32[]{:S(2)}) %collective-permute-start.39) | collective-permute-done | bytes 606240 | tf_op jit(solution)/shard_map/ppermute | solution.py:988
  393.1 2.9 unpack_sums.1
  396.1 1.5 slice_reduce_fusion
  397.6 1.5 collective-permute-start.40
  399.1 1.8 copy.76
  402.3 2.2 copy.78
  (160 shorter events, 41.4 us)
Async XLA Ops:
  0.7 1.8 slice-start.3
  0.7 3.5 copy-start.30
  0.7 4.1 %copy-start.33 = (s32[1,256]{1,0:T(1,128)S(1)}, s32[1,256]{1,0:T(1,128)}, u32[]{:S(2)}) copy-start(s32[1,256]{1,0:T(1,128)} %seg_row.3) | copy-start | bytes 3076
  2.5 9.8 %collective-permute-start.2 = (f32[48,1024]{1,0:T(8,128)S(1)}, f32[48,1024]{1,0:T(8,128)S(1)}, u32[]{:S(2)}, u32[]{:S(2)}) collective-permute-start(f32[48,1024]{1,0:T(8,128)S(1)} %maximum_convert_fusion), channel_id=1, source_target_pairs={{0,1},{1,0},{2,3},{3,2},{4,5},{5,4},{6,7},{7,6},{8,9},{9,8},{10,11... | collective-permute-start | bytes 589832 | tf_op jit(solution)/shard_map/ppermute | solution.py:672
  12.3 12.9 %copy-start.31 = (bf16[2,1024]{1,0:T(2,128)(2,1)S(1)}, bf16[2,1024]{1,0:T(2,128)(2,1)}, u32[]{:S(2)}) copy-start(bf16[2,1024]{1,0:T(2,128)(2,1)} %param.24) | copy-start | bytes 12292
  12.3 13.5 %copy-start.29 = (bf16[2,1024,4]{1,2,0:T(4,128)(2,1)S(1)}, bf16[2,1024,4]{1,2,0:T(4,128)(2,1)}, u32[]{:S(2)}) copy-start(bf16[2,1024,4]{1,2,0:T(4,128)(2,1)} %param.25) | copy-start | bytes 49156
  12.3 13.8 %copy-start.32 = (s32[2,256,2]{1,2,0:T(2,128)S(1)}, s32[2,256,2]{1,2,0:T(2,128)}, u32[]{:S(2)}) copy-start(s32[2,256,2]{1,2,0:T(2,128)} %param.18) | copy-start | bytes 12292
  13.0 17.9 %copy-start.18 = (f32[48,1024]{1,0:T(8,128)S(1)}, f32[48,1024]{1,0:T(8,128)}, u32[]{:S(2)}) copy-start(f32[48,1024]{1,0:T(8,128)} %behind.10) | copy-start | bytes 589828
  13.0 7.1 %collective-permute-start.3 = (f32[48,1024]{1,0:T(8,128)}, f32[48,1024]{1,0:T(8,128)S(1)}, u32[]{:S(2)}, u32[]{:S(2)}) collective-permute-start(f32[48,1024]{1,0:T(8,128)} %behind.10), channel_id=1, source_target_pairs={{0,96},{2,6},{4,100},{6,2},{8,104},{10,14},{12,108},{14,10},{32,64... | collective-permute-start | bytes 589832 | tf_op jit(solution)/shard_map/ppermute | solution.py:825
  15.8 23.7 %collective-permute-start = (f32[256,1024]{1,0:T(8,128)}, f32[256,1024]{1,0:T(8,128)S(1)}, u32[]{:S(2)}, u32[]{:S(2)}) collective-permute-start(f32[256,1024]{1,0:T(8,128)} %get-tuple-element.104.own.refs_1_), channel_id=1, source_target_pairs={{0,1},{1,0},{2,3},{3,2},{4,5},{5,4},{6,7},{7,6},{8,9},{9,8},{10,11... | collective-permute-start | bytes 3145736 | tf_op jit(solution)/shard_map/ppermute | solution.py:672
  21.1 9.9 %collective-permute-start.4 = (f32[96,1024]{1,0:T(8,128)S(1)}, f32[96,1024]{1,0:T(8,128)S(1)}, u32[]{:S(2)}, u32[]{:S(2)}) collective-permute-start(f32[96,1024]{1,0:T(8,128)S(1)} %pad_maximum_fusion.1), channel_id=1, source_target_pairs={{0,12},{2,34},{4,8},{6,38},{8,4},{10,42},{12,0},{14,46},{32,44},{3... | collective-permute-start | bytes 1179656 | tf_op jit(solution)/shard_map/ppermute | solution.py:825
  40.5 9.7 %collective-permute-start.5 = (f32[192,512]{1,0:T(8,128)}, f32[192,512]{1,0:T(8,128)S(1)}, u32[]{:S(2)}, u32[]{:S(2)}) collective-permute-start(f32[192,512]{1,0:T(8,128)} %get-tuple-element.107.refs_0_), channel_id=1, source_target_pairs={{0,4},{2,98},{4,0},{6,102},{8,12},{10,106},{12,8},{14,110},{32,36}... | collective-permute-start | bytes 1179656 | tf_op jit(solution)/shard_map/ppermute | solution.py:833
  40.8 9.5 %collective-permute-start.6 = (f32[192,512]{1,0:T(8,128)}, f32[192,512]{1,0:T(8,128)S(1)}, u32[]{:S(2)}, u32[]{:S(2)}) collective-permute-start(f32[192,512]{1,0:T(8,128)} %get-tuple-element.108.refs_1_), channel_id=1, source_target_pairs={{0,32},{2,14},{4,36},{6,10},{8,40},{10,6},{12,44},{14,2},{32,0},{3... | collective-permute-start | bytes 1179656 | tf_op jit(solution)/shard_map/ppermute | solution.py:833
  50.2 4.7 %copy-start.22 = (f32[256,1024]{1,0:T(8,128)S(1)}, f32[256,1024]{1,0:T(8,128)}, u32[]{:S(2)}) copy-start(f32[256,1024]{1,0:T(8,128)} %get-tuple-element.106.refs_2_.refs_1_) | copy-start | bytes 3145732
  52.4 28.6 %copy-start.28 = (f32[384,512]{1,0:T(8,128)}, f32[384,512]{1,0:T(8,128)S(1)}, u32[]{:S(2)}) copy-start(f32[384,512]{1,0:T(8,128)S(1)} %constant_dynamic-update-slice_fusion.refs_13_) | copy-start | bytes 2359300
  52.4 12.2 %collective-permute-start.7 = (f32[384,512]{1,0:T(8,128)S(1)}, f32[384,512]{1,0:T(8,128)}, u32[]{:S(2)}, u32[]{:S(2)}) collective-permute-start(f32[384,512]{1,0:T(8,128)S(1)} %constant_dynamic-update-slice_fusion.refs_13_), channel_id=1, source_target_pairs={{0,32},{2,14},{4,36},{6,10},{8,40},{10,6},{12,44},{14,2},{32,0},{3... | collective-permute-start | bytes 2359304 | tf_op jit(solution)/shard_map/ppermute | solution.py:833
  53.1 27.9 %copy-start.27 = (f32[384,512]{1,0:T(8,128)}, f32[384,512]{1,0:T(8,128)S(1)}, u32[]{:S(2)}) copy-start(f32[384,512]{1,0:T(8,128)S(1)} %constant_dynamic-update-slice_fusion.2.refs_14_) | copy-start | bytes 2359300
  53.1 12.8 %collective-permute-start.8 = (f32[384,512]{1,0:T(8,128)S(1)}, f32[384,512]{1,0:T(8,128)S(1)}, u32[]{:S(2)}, u32[]{:S(2)}) collective-permute-start(f32[384,512]{1,0:T(8,128)S(1)} %constant_dynamic-update-slice_fusion.2.refs_14_), channel_id=1, source_target_pairs={{0,4},{2,98},{4,0},{6,102},{8,12},{10,106},{12,8},{14,110},{32,36}... | collective-permute-start | bytes 2359304 | tf_op jit(solution)/shard_map/ppermute | solution.py:833
  54.9 26.0 %collective-permute-start.1 = (f32[256,1024]{1,0:T(8,128)S(1)}, f32[256,1024]{1,0:T(8,128)}, u32[]{:S(2)}, u32[]{:S(2)}) collective-permute-start(f32[256,1024]{1,0:T(8,128)S(1)} %copy-done.22), channel_id=1, source_target_pairs={{0,1},{1,0},{2,3},{3,2},{4,5},{5,4},{6,7},{7,6},{8,9},{9,8},{10,11... | collective-permute-start | bytes 3145736 | tf_op jit(solution)/shard_map/ppermute | solution.py:672
  55.4 25.6 %collective-permute-start.9 = (f32[384,512]{1,0:T(8,128)S(1)}, f32[384,512]{1,0:T(8,128)}, u32[]{:S(2)}, u32[]{:S(2)}) collective-permute-start(f32[384,512]{1,0:T(8,128)S(1)} %constant_dynamic-update-slice_fusion.refs_13_), channel_id=1, source_target_pairs={{0,2},{2,0},{1,3},{3,1},{4,6},{6,4},{5,7},{7,5},{8,10},{10,8},{9,1... | collective-permute-start | bytes 2359304 | tf_op jit(solution)/shard_map/ppermute | solution.py:841
  56.2 24.7 %collective-permute-start.10 = (f32[384,512]{1,0:T(8,128)S(1)}, f32[384,512]{1,0:T(8,128)}, u32[]{:S(2)}, u32[]{:S(2)}) collective-permute-start(f32[384,512]{1,0:T(8,128)S(1)} %constant_dynamic-update-slice_fusion.2.refs_14_), channel_id=1, source_target_pairs={{0,2},{2,0},{1,3},{3,1},{4,6},{6,4},{5,7},{7,5},{8,10},{10,8},{9,1... | collective-permute-start | bytes 2359304 | tf_op jit(solution)/shard_map/ppermute | solution.py:841
  64.6 16.4 %collective-permute-start.11 = (f32[384,512]{1,0:T(8,128)}, f32[384,512]{1,0:T(8,128)}, u32[]{:S(2)}, u32[]{:S(2)}) collective-permute-start(f32[384,512]{1,0:T(8,128)} %collective-permute-done.7.refs_15_), channel_id=1, source_target_pairs={{0,2},{2,0},{1,3},{3,1},{4,6},{6,4},{5,7},{7,5},{8,10},{10,8},{9,1... | collective-permute-start | bytes 2359304 | tf_op jit(solution)/shard_map/ppermute | solution.py:841
  65.9 15.1 %copy-start.34 = (f32[384,512]{1,0:T(8,128)}, f32[384,512]{1,0:T(8,128)S(1)}, u32[]{:S(2)}) copy-start(f32[384,512]{1,0:T(8,128)S(1)} %collective-permute-done.8.refs_16_) | copy-start | bytes 2359300
  65.9 15.1 %collective-permute-start.12 = (f32[384,512]{1,0:T(8,128)S(1)}, f32[384,512]{1,0:T(8,128)}, u32[]{:S(2)}, u32[]{:S(2)}) collective-permute-start(f32[384,512]{1,0:T(8,128)S(1)} %collective-permute-done.8.refs_16_), channel_id=1, source_target_pairs={{0,2},{2,0},{1,3},{3,1},{4,6},{6,4},{5,7},{7,5},{8,10},{10,8},{9,1... | collective-permute-start | bytes 2359304 | tf_op jit(solution)/shard_map/ppermute | solution.py:841
  111.8 10.6 %collective-permute-start.13 = (f32[512,3072]{1,0:T(8,128)}, f32[512,3072]{1,0:T(8,128)}, u32[]{:S(2)}, u32[]{:S(2)}) collective-permute-start(f32[512,3072]{1,0:T(8,128)} %get-tuple-element.116), channel_id=1, source_target_pairs={{0,2},{2,0},{1,3},{3,1},{4,6},{6,4},{5,7},{7,5},{8,10},{10,8},{9,1... | collective-permute-start | bytes 18874376 | tf_op jit(solution)/shard_map/ppermute | solution.py:919
  112.0 28.5 %collective-permute-start.14 = (f32[256,1152]{1,0:T(8,128)}, f32[256,1152]{1,0:T(8,128)S(1)}, u32[]{:S(2)}, u32[]{:S(2)}) collective-permute-start(f32[256,1152]{1,0:T(8,128)} %get-tuple-element.118.own), channel_id=1, source_target_pairs={{0,1},{1,0},{2,3},{3,2},{4,5},{5,4},{6,7},{7,6},{8,9},{9,8},{10,11... | collective-permute-start | bytes 3538952 | tf_op jit(solution)/shard_map/ppermute | solution.py:672
  141.5 41.8 %collective-permute-start.15 = (f32[256,1024]{1,0:T(8,128)}, f32[256,1024]{1,0:T(8,128)S(1)}, u32[]{:S(2)}, u32[]{:S(2)}) collective-permute-start(f32[256,1024]{1,0:T(8,128)} %get-tuple-element.119), channel_id=1, source_target_pairs={{0,1},{1,0},{2,3},{3,2},{4,5},{5,4},{6,7},{7,6},{8,9},{9,8},{10,11... | collective-permute-start | bytes 3145736 | tf_op jit(solution)/shard_map/ppermute | solution.py:672
  141.9 34.4 %collective-permute-start.16 = (f32[256,1536]{1,0:T(8,128)}, f32[256,1536]{1,0:T(8,128)S(1)}, u32[]{:S(2)}, u32[]{:S(2)}) collective-permute-start(f32[256,1536]{1,0:T(8,128)} %get-tuple-element.131.rest_4_), channel_id=1, source_target_pairs={{0,32},{2,14},{4,36},{6,10},{8,40},{10,6},{12,44},{14,2},{32,0},{3... | collective-permute-start | bytes 4718600 | tf_op jit(solution)/shard_map/ppermute | solution.py:734
  142.4 34.0 %collective-permute-start.17 = (f32[256,1536]{1,0:T(8,128)}, f32[256,1536]{1,0:T(8,128)}, u32[]{:S(2)}, u32[]{:S(2)}) collective-permute-start(f32[256,1536]{1,0:T(8,128)} %get-tuple-element.132.rest_5_), channel_id=1, source_target_pairs={{0,4},{2,98},{4,0},{6,102},{8,12},{10,106},{12,8},{14,110},{32,36}... | collective-permute-start | bytes 4718600 | tf_op jit(solution)/shard_map/ppermute | solution.py:734
  184.3 30.5 %copy-start.4 = (f32[512,1664]{1,0:T(8,128)S(1)}, f32[512,1664]{1,0:T(8,128)}, u32[]{:S(2)}) copy-start(f32[512,1664]{1,0:T(8,128)} %get-tuple-element.150.refs_6_) | copy-start | bytes 10223620
  197.8 21.2 %collective-permute-start.20 = (f32[512,3072]{1,0:T(8,128)}, f32[512,3072]{1,0:T(8,128)S(1)}, u32[]{:S(2)}, u32[]{:S(2)}) collective-permute-start(f32[512,3072]{1,0:T(8,128)} %get-tuple-element.153), channel_id=1, source_target_pairs={{0,2},{2,0},{1,3},{3,1},{4,6},{6,4},{5,7},{7,5},{8,10},{10,8},{9,1... | collective-permute-start | bytes 18874376 | tf_op jit(solution)/shard_map/ppermute | solution.py:938
  200.0 14.9 %collective-permute-start.19 = (f32[512,1664]{1,0:T(8,128)}, f32[512,1664]{1,0:T(8,128)S(1)}, u32[]{:S(2)}, u32[]{:S(2)}) collective-permute-start(f32[512,1664]{1,0:T(8,128)} %get-tuple-element.151), channel_id=1, source_target_pairs={{0,2},{2,0},{1,3},{3,1},{4,6},{6,4},{5,7},{7,5},{8,10},{10,8},{9,1... | collective-permute-start | bytes 10223624 | tf_op jit(solution)/shard_map/ppermute | solution.py:930
  200.1 26.0 %collective-permute-start.21 = (f32[128,1536]{1,0:T(8,128)}, f32[128,1536]{1,0:T(8,128)}, u32[]{:S(2)}, u32[]{:S(2)}) collective-permute-start(f32[128,1536]{1,0:T(8,128)} %get-tuple-element.140.rest_0_), channel_id=1, source_target_pairs={{0,4},{2,98},{4,0},{6,102},{8,12},{10,106},{12,8},{14,110},{32,36}... | collective-permute-start | bytes 2359304 | tf_op jit(solution)/shard_map/ppermute | solution.py:734
  201.2 25.0 %collective-permute-start.22 = (f32[128,1536]{1,0:T(8,128)}, f32[128,1536]{1,0:T(8,128)}, u32[]{:S(2)}, u32[]{:S(2)}) collective-permute-start(f32[128,1536]{1,0:T(8,128)} %get-tuple-element.141.rest_1_), channel_id=1, source_target_pairs={{0,32},{2,14},{4,36},{6,10},{8,40},{10,6},{12,44},{14,2},{32,0},{3... | collective-permute-start | bytes 2359304 | tf_op jit(solution)/shard_map/ppermute | solution.py:734
  201.7 28.9 %collective-permute-start.18 = (f32[256,1152]{1,0:T(8,128)}, f32[256,1152]{1,0:T(8,128)}, u32[]{:S(2)}, u32[]{:S(2)}) collective-permute-start(f32[256,1152]{1,0:T(8,128)} %get-tuple-element.143.own), channel_id=1, source_target_pairs={{0,1},{1,0},{2,3},{3,2},{4,5},{5,4},{6,7},{7,6},{8,9},{9,8},{10,11... | collective-permute-start | bytes 3538952 | tf_op jit(solution)/shard_map/ppermute | solution.py:672
  214.8 2.3 copy-start.5
  217.1 35.6 %collective-permute-start.24 = (f32[256,1664]{1,0:T(8,128)}, f32[256,1664]{1,0:T(8,128)S(1)}, u32[]{:S(2)}, u32[]{:S(2)}) collective-permute-start(f32[256,1664]{1,0:T(8,128)} %slice_add_fusion.rest_0_), channel_id=1, source_target_pairs={{0,12},{2,34},{4,8},{6,38},{8,4},{10,42},{12,0},{14,46},{32,44},{3... | collective-permute-start | bytes 5111816 | tf_op jit(solution)/shard_map/ppermute | solution.py:734
  219.0 6.4 %copy-start = (f32[512,3072]{1,0:T(8,128)}, f32[512,3072]{1,0:T(8,128)S(1)}, u32[]{:S(2)}) copy-start(f32[512,3072]{1,0:T(8,128)S(1)} %collective-permute-done.20.refs_1_.refs_4_) | copy-start | bytes 18874372
  225.4 30.0 %collective-permute-start.25 = (f32[256,1536]{1,0:T(8,128)}, f32[256,1536]{1,0:T(8,128)S(1)}, u32[]{:S(2)}, u32[]{:S(2)}) collective-permute-start(f32[256,1536]{1,0:T(8,128)} %get-tuple-element.235.rest_1_), channel_id=1, source_target_pairs={{0,32},{2,14},{4,36},{6,10},{8,40},{10,6},{12,44},{14,2},{32,0},{3... | collective-permute-start | bytes 4718600 | tf_op jit(solution)/shard_map/ppermute | solution.py:734
  226.1 29.4 %collective-permute-start.26 = (f32[256,1536]{1,0:T(8,128)}, f32[256,1536]{1,0:T(8,128)}, u32[]{:S(2)}, u32[]{:S(2)}) collective-permute-start(f32[256,1536]{1,0:T(8,128)} %get-tuple-element.234.rest_2_), channel_id=1, source_target_pairs={{0,4},{2,98},{4,0},{6,102},{8,12},{10,106},{12,8},{14,110},{32,36}... | collective-permute-start | bytes 4718600 | tf_op jit(solution)/shard_map/ppermute | solution.py:734
  252.8 2.7 copy-start.7
  256.6 9.2 %collective-permute-start.27 = (f32[512,1664]{1,0:T(8,128)}, f32[512,1664]{1,0:T(8,128)S(1)}, u32[]{:S(2)}, u32[]{:S(2)}) collective-permute-start(f32[512,1664]{1,0:T(8,128)} %behind.14), channel_id=1, source_target_pairs={{0,2},{2,0},{1,3},{3,1},{4,6},{6,4},{5,7},{7,5},{8,10},{10,8},{9,1... | collective-permute-start | bytes 10223624 | tf_op jit(solution)/shard_map/ppermute | solution.py:949
  265.8 1.7 copy-start.3
  272.4 31.7 %collective-permute-start.28 = (f32[256,1664]{1,0:T(8,128)}, f32[256,1664]{1,0:T(8,128)S(1)}, u32[]{:S(2)}, u32[]{:S(2)}) collective-permute-start(f32[256,1664]{1,0:T(8,128)} %get-tuple-element.161.refs_2_), channel_id=1, source_target_pairs={{0,12},{2,34},{4,8},{6,38},{8,4},{10,42},{12,0},{14,46},{32,44},{3... | collective-permute-start | bytes 5111816 | tf_op jit(solution)/shard_map/ppermute | solution.py:734
  274.3 27.0 %collective-permute-start.23 = (f32[256,1024]{1,0:T(8,128)}, f32[256,1024]{1,0:T(8,128)S(1)}, u32[]{:S(2)}, u32[]{:S(2)}) collective-permute-start(f32[256,1024]{1,0:T(8,128)} %get-tuple-element.155), channel_id=1, source_target_pairs={{0,1},{1,0},{2,3},{3,2},{4,5},{5,4},{6,7},{7,6},{8,9},{9,8},{10,11... | collective-permute-start | bytes 3145736 | tf_op jit(solution)/shard_map/ppermute | solution.py:672
  275.9 12.2 %collective-permute-start.29 = (f32[128,1536]{1,0:T(8,128)}, f32[128,1536]{1,0:T(8,128)S(1)}, u32[]{:S(2)}, u32[]{:S(2)}) collective-permute-start(f32[128,1536]{1,0:T(8,128)} %get-tuple-element.158.refs_1_), channel_id=1, source_target_pairs={{0,4},{2,98},{4,0},{6,102},{8,12},{10,106},{12,8},{14,110},{32,36}... | collective-permute-start | bytes 2359304 | tf_op jit(solution)/shard_map/ppermute | solution.py:734
  275.9 20.8 %collective-permute-start.30 = (f32[128,1536]{1,0:T(8,128)}, f32[128,1536]{1,0:T(8,128)}, u32[]{:S(2)}, u32[]{:S(2)}) collective-permute-start(f32[128,1536]{1,0:T(8,128)} %get-tuple-element.159.refs_2_), channel_id=1, source_target_pairs={{0,32},{2,14},{4,36},{6,10},{8,40},{10,6},{12,44},{14,2},{32,0},{3... | collective-permute-start | bytes 2359304 | tf_op jit(solution)/shard_map/ppermute | solution.py:734
  288.1 8.6 %copy-start.16 = (f32[128,1536]{1,0:T(8,128)}, f32[128,1536]{1,0:T(8,128)S(1)}, u32[]{:S(2)}) copy-start(f32[128,1536]{1,0:T(8,128)S(1)} %collective-permute-done.29.refs_0_) | copy-start | bytes 2359300
  301.3 2.8 copy-start.1
  308.5 35.6 %collective-permute-start.31 = (f32[128,1664]{1,0:T(8,128)}, f32[128,1664]{1,0:T(8,128)S(1)}, u32[]{:S(2)}, u32[]{:S(2)}) collective-permute-start(f32[128,1664]{1,0:T(8,128)} %get-tuple-element.171), channel_id=1, source_target_pairs={{0,96},{2,6},{4,100},{6,2},{8,104},{10,14},{12,108},{14,10},{32,64... | collective-permute-start | bytes 2555912 | tf_op jit(solution)/shard_map/ppermute | solution.py:734
  309.1 35.9 %collective-permute-start.34 = (f32[128,1664]{1,0:T(8,128)}, f32[128,1664]{1,0:T(8,128)S(1)}, u32[]{:S(2)}, u32[]{:S(2)}) collective-permute-start(f32[128,1664]{1,0:T(8,128)} %get-tuple-element.177), channel_id=1, source_target_pairs={{0,96},{2,6},{4,100},{6,2},{8,104},{10,14},{12,108},{14,10},{32,64... | collective-permute-start | bytes 2555912 | tf_op jit(solution)/shard_map/ppermute | solution.py:734
  311.8 13.4 %collective-permute-start.32 = (f32[64,3072]{1,0:T(8,128)}, f32[64,3072]{1,0:T(8,128)S(1)}, u32[]{:S(2)}, u32[]{:S(2)}) collective-permute-start(f32[64,3072]{1,0:T(8,128)} %get-tuple-element.168.refs_1_), channel_id=1, source_target_pairs={{0,12},{2,34},{4,8},{6,38},{8,4},{10,42},{12,0},{14,46},{32,44},{3... | collective-permute-start | bytes 2359304 | tf_op jit(solution)/shard_map/ppermute | solution.py:734
  313.6 26.6 %collective-permute-start.33 = (f32[64,3072]{1,0:T(8,128)}, f32[64,3072]{1,0:T(8,128)S(1)}, u32[]{:S(2)}, u32[]{:S(2)}) collective-permute-start(f32[64,3072]{1,0:T(8,128)} %get-tuple-element.169.refs_2_), channel_id=1, source_target_pairs={{0,96},{2,6},{4,100},{6,2},{8,104},{10,14},{12,108},{14,10},{32,64... | collective-permute-start | bytes 2359304 | tf_op jit(solution)/shard_map/ppermute | solution.py:734
  325.2 15.0 %copy-start.25 = (f32[64,3072]{1,0:T(8,128)}, f32[64,3072]{1,0:T(8,128)S(1)}, u32[]{:S(2)}) copy-start(f32[64,3072]{1,0:T(8,128)S(1)} %collective-permute-done.32.refs_1_) | copy-start | bytes 2359300
  345.9 22.9 %copy-start.11 = (f32[256,1024]{1,0:T(8,128)S(1)}, f32[256,1024]{1,0:T(8,128)}, u32[]{:S(2)}) copy-start(f32[256,1024]{1,0:T(8,128)} %get-tuple-element.119) | copy-start | bytes 3145732
  345.9 22.9 %copy-start.21 = (f32[256,1024]{1,0:T(8,128)S(1)}, f32[256,1024]{1,0:T(8,128)}, u32[]{:S(2)}) copy-start(f32[256,1024]{1,0:T(8,128)} %get-tuple-element.114.middle) | copy-start | bytes 3145732
  349.4 19.5 %copy-start.10 = (f32[256,1024]{1,0:T(8,128)S(1)}, f32[256,1024]{1,0:T(8,128)}, u32[]{:S(2)}) copy-start(f32[256,1024]{1,0:T(8,128)} %copy-done.9) | copy-start | bytes 3145732
  349.4 14.5 %collective-permute-start.35 = (f32[64,3328]{1,0:T(8,128)}, f32[64,3328]{1,0:T(8,128)S(1)}, u32[]{:S(2)}, u32[]{:S(2)}) collective-permute-start(f32[64,3328]{1,0:T(8,128)} %get-tuple-element.178), channel_id=1, source_target_pairs={{0,32},{2,14},{4,36},{6,10},{8,40},{10,6},{12,44},{14,2},{32,0},{3... | collective-permute-start | bytes 2555912 | tf_op jit(solution)/shard_map/ppermute | solution.py:734
  349.4 23.6 %collective-permute-start.36 = (f32[32,3072]{1,0:T(8,128)}, f32[32,3072]{1,0:T(8,128)}, u32[]{:S(2)}, u32[]{:S(2)}) collective-permute-start(f32[32,3072]{1,0:T(8,128)} %get-tuple-element.174.refs_1_), channel_id=1, source_target_pairs={{0,96},{2,6},{4,100},{6,2},{8,104},{10,14},{12,108},{14,10},{32,64... | collective-permute-start | bytes 1179656 | tf_op jit(solution)/shard_map/ppermute | solution.py:734
  350.8 22.1 %collective-permute-start.37 = (f32[32,3072]{1,0:T(8,128)}, f32[32,3072]{1,0:T(8,128)}, u32[]{:S(2)}, u32[]{:S(2)}) collective-permute-start(f32[32,3072]{1,0:T(8,128)} %get-tuple-element.175.refs_2_), channel_id=1, source_target_pairs={{0,12},{2,34},{4,8},{6,38},{8,4},{10,42},{12,0},{14,46},{32,44},{3... | collective-permute-start | bytes 1179656 | tf_op jit(solution)/shard_map/ppermute | solution.py:734
  367.2 8.4 %collective-permute-start.38 = (f32[32,3328]{1,0:T(8,128)}, f32[32,3328]{1,0:T(8,128)}, u32[]{:S(2)}, u32[]{:S(2)}) collective-permute-start(f32[32,3328]{1,0:T(8,128)} %get-tuple-element.183), channel_id=1, source_target_pairs={{0,4},{2,98},{4,0},{6,102},{8,12},{10,106},{12,8},{14,110},{32,36}... | collective-permute-start | bytes 1277960 | tf_op jit(solution)/shard_map/ppermute | solution.py:734
  372.9 8.4 %copy-start.2 = (f32[256,1024]{1,0:T(8,128)S(1)}, f32[256,1024]{1,0:T(8,128)}, u32[]{:S(2)}) copy-start(f32[256,1024]{1,0:T(8,128)} %behind.19) | copy-start | bytes 3145732
  378.4 14.7 %collective-permute-start.39 = (f32[16,9472]{1,0:T(8,128)}, f32[16,9472]{1,0:T(8,128)}, u32[]{:S(2)}, u32[]{:S(2)}) collective-permute-start(f32[16,9472]{1,0:T(8,128)} %get-tuple-element.185), channel_id=1, source_target_pairs={{0,16},{16,0},{1,17},{17,1},{2,18},{18,2},{3,19},{19,3},{4,20},{20... | collective-permute-start | bytes 1818632 | tf_op jit(solution)/shard_map/ppermute | solution.py:988
  397.6 6.9 %collective-permute-start.40 = (f32[2,16]{1,0:T(2,128)S(1)}, f32[2,16]{1,0:T(2,128)S(1)}, u32[]{:S(2)}, u32[]{:S(2)}) collective-permute-start(f32[2,16]{1,0:T(2,128)S(1)} %get-tuple-element.233), channel_id=1, source_target_pairs={{0,1},{1,0},{2,3},{3,2},{4,5},{5,4},{6,7},{7,6},{8,9},{9,8},{10,11... | collective-permute-start | bytes 392 | tf_op jit(solution)/shard_map/ppermute | solution.py:672
  (16 other events, 18.0 us)
